TPU v7x, 256 devices: a whole 4x4x8 slice. The times are simulated.
256 devices in a mesh: dp: 16 (over y, z_hi), mp: 16 (over z_lo, x, core).
Axes of the slice: x: 4, y: 4, z: 8 (z_hi: 4, z_lo: 2; z = z_hi * 2 + z_lo), core: 2. Of those that a mesh axis runs over, the one named last changes fastest.
Arguments:
- dec_input: bfloat16 [16, 256, 4096], P('dp', None, 'mp'), may hold values from -6 to 6
- enc_output: bfloat16 [16, 256, 4096], P('dp', 'mp'), may hold values from -32 to 32
- query_weight: bfloat16 [4096, 4096], P('dp', 'mp'), may hold values from -3 to 3
- key_weight: bfloat16 [4096, 4096], P('dp', 'mp'), may hold values from -1 to 1
- value_weight: bfloat16 [4096, 4096], P('dp', 'mp'), may hold values from -0.09375 to 0.09375
- output_weight: bfloat16 [4096, 4096], P('mp', 'dp'), may hold values from -0.09375 to 0.09375
- cotangent: bfloat16 [16, 256, 4096], P('dp', None, 'mp'), may hold values from -6 to 6
- enc_lengths: int32 [16], P('dp'), may hold values from 64 to 256
- dec_lengths: int32 [16], P('dp'), may hold values from 64 to 256
Outputs:
- layer_out: bfloat16 [16, 256, 4096], P('dp', None, 'mp')
- input_grad: bfloat16 [16, 256, 4096], P('dp', None, 'mp')
- enc_grad: bfloat16 [16, 256, 4096], P('dp', 'mp')
- query_grad: bfloat16 [4096, 4096], P('dp', 'mp')
- key_grad: bfloat16 [4096, 4096], P('dp', 'mp')
- value_grad: bfloat16 [4096, 4096], P('dp', 'mp')
- output_grad: bfloat16 [4096, 4096], P('mp', 'dp')
All inputs are finite; a program needn't handle non-finite values.
Results may differ from a plain program's by a relative error of at most 0.019.
The roundings to bfloat16 on the way count: a program that leaves them out, or rounds other values in their place, can miss the bound.
Values may be sent and summed in bfloat16 or wider, within the bound.
No kernel may reach another device: no remote copies, remote signals or barrier semaphores. Data moves between devices by JAX's collectives and lax.ppermute only.
A program may use at most 64 MiB of HBM per device.

v0:
```python
import jax
import jax.numpy as jnp
from jax import lax
from jax.sharding import PartitionSpec as P

DH = 256


def local(
    dec_input,
    enc_output,
    query_weight,
    key_weight,
    value_weight,
    output_weight,
    cotangent,
    enc_lengths,
    dec_lengths,
):
    scale = DH ** (-0.5)
    hidden = lax.all_gather(dec_input, "mp", axis=2, tiled=True)[0]
    query_full, key_full, value_full = (
        lax.all_gather(query_weight, "dp", axis=0, tiled=True),
        lax.all_gather(key_weight, "dp", axis=0, tiled=True),
        lax.all_gather(value_weight, "dp", axis=0, tiled=True),
    )
    output_full = lax.all_gather(output_weight, "dp", axis=1, tiled=True)
    encoded = lax.all_gather(enc_output, "mp", axis=1, tiled=True)[0]
    tokens = hidden.shape[0]
    keys_len = encoded.shape[0]
    width = query_weight.shape[1]
    heads_here = width // DH
    hidden32 = hidden.astype(jnp.float32)
    inv_rms = lax.rsqrt(jnp.mean(hidden32 * hidden32, axis=-1, keepdims=True) + 1e-06)
    normed = (hidden32 * inv_rms).astype(jnp.bfloat16)
    query = jnp.dot(normed, query_full, preferred_element_type=jnp.float32).astype(jnp.bfloat16)
    keyed = jnp.dot(encoded, key_full, preferred_element_type=jnp.float32).astype(jnp.bfloat16)
    valued = jnp.dot(encoded, value_full, preferred_element_type=jnp.float32).astype(jnp.bfloat16)
    query_heads = query.reshape(tokens, heads_here, DH)
    key_heads = keyed.reshape(keys_len, heads_here, DH)
    value_heads = valued.reshape(keys_len, heads_here, DH)
    scores = (
        jnp.einsum("thd,lhd->htl", query_heads, key_heads, preferred_element_type=jnp.float32)
        * scale
    )
    valid = jnp.arange(keys_len, dtype=jnp.int32) < enc_lengths[0]
    scores = jnp.where(valid[None, None, :], scores, -1e30)
    shifted = jnp.exp(scores - jnp.max(scores, axis=-1, keepdims=True))
    probs = shifted / jnp.sum(shifted, axis=-1, keepdims=True)
    probs_low = probs.astype(jnp.bfloat16)
    attended = (
        jnp.einsum("htl,lhd->thd", probs_low, value_heads, preferred_element_type=jnp.float32)
        .reshape(tokens, width)
        .astype(jnp.bfloat16)
    )
    partial_out = jnp.dot(attended, output_full, preferred_element_type=jnp.float32)
    out_share = lax.psum_scatter(
        partial_out.astype(jnp.bfloat16), "mp", scatter_dimension=1, tiled=True
    ).astype(jnp.float32)
    own_input = dec_input[0].astype(jnp.float32)
    layer_out = (own_input + out_share).astype(jnp.bfloat16)[None]
    upstream = lax.all_gather(cotangent, "mp", axis=2, tiled=True)[0]
    keep = (jnp.arange(tokens, dtype=jnp.int32) < dec_lengths[0])[:, None]
    masked = jnp.where(keep, upstream, jnp.zeros_like(upstream))
    own_masked = jnp.where(keep, cotangent[0], jnp.zeros_like(cotangent[0]))
    attended_grad = jnp.dot(masked, output_full.T, preferred_element_type=jnp.float32).astype(
        jnp.bfloat16
    )
    grad_heads = attended_grad.reshape(tokens, heads_here, DH)
    probs_grad = jnp.einsum(
        "thd,lhd->htl", grad_heads, value_heads, preferred_element_type=jnp.float32
    )
    scores_grad = (
        probs * (probs_grad - jnp.sum(probs * probs_grad, axis=-1, keepdims=True)) * scale
    ).astype(jnp.bfloat16)
    q_grad = (
        jnp.einsum("htl,lhd->thd", scores_grad, key_heads, preferred_element_type=jnp.float32)
        .reshape(tokens, width)
        .astype(jnp.bfloat16)
    )
    k_grad = (
        jnp.einsum("htl,thd->lhd", scores_grad, query_heads, preferred_element_type=jnp.float32)
        .reshape(keys_len, width)
        .astype(jnp.bfloat16)
    )
    v_grad = (
        jnp.einsum("htl,thd->lhd", probs_low, grad_heads, preferred_element_type=jnp.float32)
        .reshape(keys_len, width)
        .astype(jnp.bfloat16)
    )
    normed_part = jnp.dot(q_grad, query_full.T, preferred_element_type=jnp.float32)
    feature_width = dec_input.shape[2]
    normed_grad = lax.psum(normed_part.astype(jnp.bfloat16), "mp").astype(jnp.float32)
    stat = jnp.mean(normed_grad * hidden32, axis=-1, keepdims=True)
    full_grad = inv_rms * normed_grad - hidden32 * inv_rms**3 * stat
    start = lax.axis_index("mp") * feature_width
    input_share = lax.dynamic_slice_in_dim(full_grad, start, feature_width, 1)
    input_grad = (own_masked.astype(jnp.float32) + input_share).astype(jnp.bfloat16)[None]
    enc_share = lax.psum_scatter(
        (
            jnp.dot(k_grad, key_full.T, preferred_element_type=jnp.float32)
            + jnp.dot(v_grad, value_full.T, preferred_element_type=jnp.float32)
        ).astype(jnp.bfloat16),
        "mp",
        scatter_dimension=0,
        tiled=True,
    )
    enc_grad = enc_share[None]
    weight_share = lax.psum_scatter(
        jnp.concatenate(
            [
                jnp.dot(normed.T, q_grad, preferred_element_type=jnp.float32),
                jnp.dot(encoded.T, k_grad, preferred_element_type=jnp.float32),
                jnp.dot(encoded.T, v_grad, preferred_element_type=jnp.float32),
                jnp.dot(masked.T, attended, preferred_element_type=jnp.float32),
            ],
            axis=1,
        ).astype(jnp.bfloat16),
        "dp",
        scatter_dimension=0,
        tiled=True,
    ).astype(jnp.float32)
    query_grad = weight_share[:, :width].astype(jnp.bfloat16)
    key_grad = weight_share[:, width : 2 * width].astype(jnp.bfloat16)
    value_grad = weight_share[:, 2 * width : 3 * width].astype(jnp.bfloat16)
    output_grad = weight_share[:, 3 * width :].T.astype(jnp.bfloat16)
    return (layer_out, input_grad, enc_grad, query_grad, key_grad, value_grad, output_grad)


def solution(mesh):
    in_specs = (
        P("dp", None, "mp"),
        P("dp", "mp", None),
        P("dp", "mp"),
        P("dp", "mp"),
        P("dp", "mp"),
        P("mp", "dp"),
        P("dp", None, "mp"),
        P("dp"),
        P("dp"),
    )
    out_specs = (
        P("dp", None, "mp"),
        P("dp", None, "mp"),
        P("dp", "mp", None),
        P("dp", "mp"),
        P("dp", "mp"),
        P("dp", "mp"),
        P("mp", "dp"),
    )
    return jax.shard_map(local, mesh=mesh, in_specs=in_specs, out_specs=out_specs, check_vma=False)
```

profile of v0, /device:TPU:1, one launch (start us, length us, event | category | flops | bytes accessed | tf_op | source)
XLA Modules:
  0.0 772.5 jit_solution(4257522152478109794)
XLA Ops:
  13.2 40.7 %all-gather.12.cloned.1.call-done = bf16[1,256,4096]{2,1,0:T(8,128)(2,1)} async-done(((bf16[1,256,256]{2,1,0:T(8,128)(2,1)}), bf16[1,256,4096]{2,1,0:T(8,128)(2,1)}) %all-gather.12.cloned.1.call-update) | async-done | bytes 2097168 | tf_op jit(solution)/shard_map/all_gather | solution.py:21
  53.9 2.1 multiply_reduce_fusion.1
  56.0 36.3 %all-gather.8.cloned.1.call-done = bf16[1,256,4096]{2,1,0:T(8,128)(2,1)} async-done(((bf16[1,16,4096]{2,1,0:T(8,128)(2,1)}), bf16[1,256,4096]{2,1,0:T(8,128)(2,1)}) %all-gather.8.cloned.1.call-update) | async-done | bytes 2097168 | tf_op jit(solution)/shard_map/all_gather | solution.py:28
  92.3 61.0 %all-gather.16.cloned.1.call-done = bf16[4096,256]{1,0:T(8,128)(2,1)} async-done(((bf16[256,256]{1,0:T(8,128)(2,1)}), bf16[4096,256]{1,0:T(8,128)(2,1)}) %all-gather.16.cloned.1.call-update) | async-done | bytes 2097168 | tf_op jit(solution)/shard_map/all_gather | solution.py:24
  153.3 2.9 fusion.25
  156.2 56.8 %all-gather.14.cloned.1.call-done = bf16[4096,256]{1,0:T(8,128)(2,1)} async-done(((bf16[256,256]{1,0:T(8,128)(2,1)}), bf16[4096,256]{1,0:T(8,128)(2,1)}) %all-gather.14.cloned.1.call-update) | async-done | bytes 2097168 | tf_op jit(solution)/shard_map/all_gather | solution.py:23
  213.0 2.3 fusion.28
  215.7 57.0 %all-gather.10.cloned.1.call-done = bf16[4096,256]{1,0:T(8,128)(2,1)} async-done(((bf16[256,256]{1,0:T(8,128)(2,1)}), bf16[4096,256]{1,0:T(8,128)(2,1)}) %all-gather.10.cloned.1.call-update) | async-done | bytes 2097168 | tf_op jit(solution)/shard_map/all_gather | solution.py:25
  272.7 2.9 fusion.22
  275.6 60.3 %all-gather.18.cloned.1.call-done = bf16[256,4096]{1,0:T(8,128)(2,1)} async-done(((bf16[256,256]{1,0:T(8,128)(2,1)}), bf16[256,4096]{1,0:T(8,128)(2,1)}) %all-gather.18.cloned.1.call-update) | async-done | bytes 2097168 | tf_op jit(solution)/shard_map/all_gather | solution.py:27
  335.9 39.8 %all-gather.20.cloned.1.call-done = bf16[1,256,4096]{2,1,0:T(8,128)(2,1)} async-done(((bf16[1,256,256]{2,1,0:T(8,128)(2,1)}), bf16[1,256,4096]{2,1,0:T(8,128)(2,1)}) %all-gather.20.cloned.1.call-update) | async-done | bytes 2097168 | tf_op jit(solution)/shard_map/all_gather | solution.py:62
  375.7 3.0 fusion.21
  380.3 2.1 convolution_convert_fusion.4
  382.7 3.7 convolution_convert_fusion.5
  386.9 2.5 fusion.1
  392.6 4.0 pad_maximum_fusion
  396.9 2.5 fusion.51
  399.4 2.1 fusion
  401.5 2.5 convert_bitcast_fusion
  404.0 105.3 %all-reduce.2.cloned.1.call-done = bf16[256,4096]{1,0:T(8,128)(2,1)} async-done(((bf16[256,4096]{1,0:T(8,128)(2,1)}), bf16[256,4096]{1,0:T(8,128)(2,1)}) %all-reduce.2.cloned.1.call-update) | async-done | bytes 2097168 | tf_op jit(solution)/shard_map/psum | solution.py:93
  509.3 2.2 convert_element_type.160
  514.2 61.5 %reduce-scatter.4.cloned.1.call-done = bf16[256,256]{1,0:T(8,128)(2,1)} async-done(((bf16[256,4096]{1,0:T(8,128)(2,1)}), bf16[256,256]{1,0:T(8,128)(2,1)}) %reduce-scatter.4.cloned.1.call-update) | async-done | bytes 131088 | tf_op jit(solution)/shard_map/reduce_scatter | solution.py:57
  577.3 123.3 %reduce-scatter.8.cloned.1.call-done = bf16[256,1024]{0,1:T(8,128)(2,1)} async-done(((bf16[4096,1024]{0,1:T(8,128)(2,1)}), bf16[256,1024]{0,1:T(8,128)(2,1)}) %reduce-scatter.8.cloned.1.call-update) | async-done | bytes 524304 | tf_op jit(solution)/shard_map/reduce_scatter | solution.py:109
  704.6 61.3 %reduce-scatter.6.cloned.1.call-done = bf16[16,4096]{1,0:T(8,128)(2,1)} async-done(((bf16[256,4096]{1,0:T(8,128)(2,1)}), bf16[16,4096]{1,0:T(8,128)(2,1)}) %reduce-scatter.6.cloned.1.call-update) | async-done | bytes 131088 | tf_op jit(solution)/shard_map/reduce_scatter | solution.py:99
  (60 shorter events, 19.2 us)
Async XLA Ops:
  7.2 46.7 %all-gather.12.cloned.1.call-start = ((), (), s32[]{:S(2)}) async-start(), calls=%async_computation.5 | async-start | bytes 2228224 | tf_op jit(solution)/shard_map/all_gather | solution.py:21
  7.9 84.4 %all-gather.8.cloned.1.call-start = ((), (), s32[]{:S(2)}) async-start(), calls=%async_computation.3 | async-start | bytes 2228224 | tf_op jit(solution)/shard_map/all_gather | solution.py:28
  8.6 144.6 %all-gather.16.cloned.1.call-start = ((), (), s32[]{:S(2)}) async-start(), calls=%async_computation.7 | async-start | bytes 2228224 | tf_op jit(solution)/shard_map/all_gather | solution.py:24
  9.4 203.6 %all-gather.14.cloned.1.call-start = ((), (), s32[]{:S(2)}) async-start(), calls=%async_computation.6 | async-start | bytes 2228224 | tf_op jit(solution)/shard_map/all_gather | solution.py:23
  10.0 262.7 %all-gather.10.cloned.1.call-start = ((), (), s32[]{:S(2)}) async-start(), calls=%async_computation.4 | async-start | bytes 2228224 | tf_op jit(solution)/shard_map/all_gather | solution.py:25
  10.5 325.4 %all-gather.18.cloned.1.call-start = ((), (), s32[]{:S(2)}) async-start(), calls=%async_computation.8 | async-start | bytes 2228224 | tf_op jit(solution)/shard_map/all_gather | solution.py:27
  11.1 364.6 %all-gather.20.cloned.1.call-start = ((), (), s32[]{:S(2)}) async-start(), calls=%async_computation.10 | async-start | bytes 2228224 | tf_op jit(solution)/shard_map/all_gather | solution.py:62
  11.9 497.4 %all-reduce.2.cloned.1.call-start = ((), (), s32[]{:S(2)}) async-start(), calls=%async_computation.11 | async-start | bytes 4194304 | tf_op jit(solution)/shard_map/psum | solution.py:93
  56.0 157.0 %copy-start = (bf16[1,256,4096]{2,1,0:T(8,128)(2,1)S(1)}, bf16[1,256,4096]{2,1,0:T(8,128)(2,1)}, u32[]{:S(2)}) copy-start(bf16[1,256,4096]{2,1,0:T(8,128)(2,1)} %all-gather.12.cloned.1.call-done) | copy-start | bytes 6291460
  378.7 1.6 copy-start.3
  382.4 193.3 %reduce-scatter.4.cloned.1.call-start = ((), (), s32[]{:S(2)}) async-start(), calls=%async_computation.9 | async-start | bytes 2228224 | tf_op jit(solution)/shard_map/reduce_scatter | solution.py:57
  386.4 314.2 %reduce-scatter.8.cloned.1.call-start = ((), (), s32[]{:S(2)}) async-start(), calls=%async_computation.13 | async-start | bytes 8912896 | tf_op jit(solution)/shard_map/reduce_scatter | solution.py:109
  386.9 2.5 copy-start.2
  389.4 1.6 copy-start.7
  396.6 369.3 %reduce-scatter.6.cloned.1.call-start = ((), (), s32[]{:S(2)}) async-start(), calls=%async_computation.12 | async-start | bytes 2228224 | tf_op jit(solution)/shard_map/reduce_scatter | solution.py:99
  396.9 2.5 copy-start.4
  509.3 2.2 copy-start.1
  511.5 0.9 copy-start.6
  511.5 64.2 %copy-start.5 = (bf16[1,256,256]{2,1,0:T(8,128)(2,1)S(1)}, bf16[1,256,256]{2,1,0:T(8,128)(2,1)}, u32[]{:S(2)}) copy-start(bf16[1,256,256]{2,1,0:T(8,128)(2,1)} %param.9) | copy-start | bytes 393220
Sparse Core Ops, SparseCore 0:
  9.8 44.0 all-gather.11
  55.7 36.4 all-gather.7
  94.7 58.5 all-gather.15
  155.6 57.3 all-gather.13
  215.3 57.3 all-gather.9
  275.0 60.9 all-gather.17
  337.7 37.9 all-gather.19
  382.5 126.6 all-reduce.1
  511.8 63.8 reduce-scatter.3
  579.3 121.2 reduce-scatter.7
  703.7 62.2 reduce-scatter.5
where the time goes:
time: 775 us; the launch traced here: 772 us
  waiting for transfers between devices  708 us (91%)
  matrix products  27.7 us (4%)
  between operations  15.4 us (2%)
  other arithmetic  15 us (2%)
    reduce_scatter x1, waiting for transfers between devices, local(): lax.psum_scatter(jnp.concatenate([jnp.dot(normed.T, q_grad, preferred_ele...  123 us
    psum x1, waiting for transfers between devices, local(): lax.psum(normed_part.astype(jnp.bfloat16), 'mp').astype(jnp.float32)  105 us
    reduce_scatter x1, waiting for transfers between devices, local(): lax.psum_scatter(partial_out.astype(jnp.bfloat16), 'mp', scatter_dimensio...  61.5 us
    reduce_scatter x1, waiting for transfers between devices, local(): lax.psum_scatter((jnp.dot(k_grad, key_full.T, preferred_element_type=jnp....  61.3 us
    all_gather x1, waiting for transfers between devices, local(): lax.all_gather(key_weight, 'dp', axis=0, tiled=True)  61 us
    all_gather x1, waiting for transfers between devices, local(): output_full = lax.all_gather(output_weight, 'dp', axis=1, tiled=True)  60.3 us
    all_gather x1, waiting for transfers between devices, local(): lax.all_gather(value_weight, 'dp', axis=0, tiled=True)  57 us
    all_gather x1, waiting for transfers between devices, local(): lax.all_gather(query_weight, 'dp', axis=0, tiled=True)  56.8 us
  transfers between devices with their start and end apart: 11, of which 11 were waited for; matrix products, arithmetic and copies ran while one was open for 5% of the time, Pallas kernels for 0%

commit v1 on v0

v1 whole, which is shorter than its diff:
```python
import functools

import jax
import jax.numpy as jnp
from jax import lax
from jax.experimental import pallas as pl
from jax.experimental.pallas import tpu as pltpu
from jax.sharding import PartitionSpec as P

BF = jnp.bfloat16
F32 = jnp.float32
NB = 16
VMEM = 40 * 1024 * 1024

ZXC = [(a, b, c) for a in range(2) for b in range(4) for c in range(2)]


def mp_index(a, b, c):
    return (a % 2) * 8 + (b % 4) * 2 + (c % 2)


def mp_shift(da, db, dc):
    return [(mp_index(a, b, c), mp_index(a + da, b + db, c + dc)) for a, b, c in ZXC]


def nn(a, b):
    return lax.dot_general(a, b, (((1,), (0,)), ((), ())), preferred_element_type=F32)


def nt(a, b):
    return lax.dot_general(a, b, (((1,), (1,)), ((), ())), preferred_element_type=F32)


def tn(a, b):
    return lax.dot_general(a, b, (((0,), (0,)), ((), ())), preferred_element_type=F32)


def attention(scale, enc_len, query, keyed, valued, attended_grad):
    scores = nt(query, keyed) * scale
    column = lax.broadcasted_iota(jnp.int32, scores.shape, 1)
    scores = jnp.where(column < enc_len, scores, -1e30)
    shifted = jnp.exp(scores - jnp.max(scores, axis=-1, keepdims=True))
    probs = shifted / jnp.sum(shifted, axis=-1, keepdims=True)
    probs_low = probs.astype(BF)
    attended = nn(probs_low, valued).astype(BF)
    probs_grad = nt(attended_grad, valued)
    inner = jnp.sum(probs * probs_grad, axis=-1, keepdims=True)
    scores_grad = (probs * (probs_grad - inner) * scale).astype(BF)
    q_grad = nn(scores_grad, keyed).astype(BF)
    k_grad = tn(scores_grad, query).astype(BF)
    v_grad = tn(probs_low, attended_grad).astype(BF)
    stat = jnp.sum(q_grad.astype(F32) * query.astype(F32), axis=-1, keepdims=True)
    return q_grad, k_grad, v_grad, attended, stat


def forward_kernel(
    scale, length_ref, normed_ref, masked_ref, enc_ref, weight_ref,
    qg_ref, kg_ref, vg_ref, at_ref, stat_ref, q_acc, kv_acc, g_acc,
):
    step = pl.program_id(0)
    width = q_acc.shape[1]

    @pl.when(step == 0)
    def _():
        q_acc[...] = jnp.zeros_like(q_acc)
        kv_acc[...] = jnp.zeros_like(kv_acc)
        g_acc[...] = jnp.zeros_like(g_acc)

    q_acc[...] += nn(normed_ref[0], weight_ref[:, :width])
    kv_acc[...] += nn(enc_ref[0], weight_ref[:, width : 3 * width])
    g_acc[...] += nn(masked_ref[0], weight_ref[:, 3 * width :])

    @pl.when(step == pl.num_programs(0) - 1)
    def _():
        query = q_acc[...].astype(BF)
        keyed = kv_acc[:, :width].astype(BF)
        valued = kv_acc[:, width:].astype(BF)
        out = attention(scale, length_ref[0], query, keyed, valued, g_acc[...].astype(BF))
        qg_ref[...], kg_ref[...], vg_ref[...], at_ref[...] = out[:4]
        stat_ref[...] = jnp.broadcast_to(out[4], stat_ref.shape)


def weight_grad_kernel(normed_ref, masked_ref, enc_ref, qg_ref, kg_ref, vg_ref, at_ref, out_ref):
    width = qg_ref.shape[1]
    out_ref[:, :width] = tn(normed_ref[0], qg_ref[...]).astype(BF)
    out_ref[:, width : 2 * width] = tn(enc_ref[0], kg_ref[...]).astype(BF)
    out_ref[:, 2 * width : 3 * width] = tn(enc_ref[0], vg_ref[...]).astype(BF)
    out_ref[:, 3 * width :] = tn(masked_ref[0], at_ref[...]).astype(BF)


def partial_kernel(weight_ref, qg_ref, kg_ref, vg_ref, at_ref, out_ref):
    step = pl.program_id(0)
    width = qg_ref.shape[1]
    a, b, c = step // 8, (step // 2) % 4, step % 2
    out_ref[c, b, a, 0] = nt(qg_ref[...], weight_ref[:, :width]).astype(BF)
    out_ref[c, b, a, 1] = nt(at_ref[...], weight_ref[:, 3 * width :]).astype(BF)
    enc = nt(kg_ref[...], weight_ref[:, width : 2 * width])
    enc += nt(vg_ref[...], weight_ref[:, 2 * width : 3 * width])
    enc = enc.astype(BF)
    rows = enc.shape[0] // NB
    start = pl.multiple_of(step * rows, rows)
    for n, (a, b, c) in enumerate(ZXC):
        out_ref[c, b, a, 2, pl.ds(start, rows), :] = enc[n * rows : (n + 1) * rows]


def call(kernel, grid, ins, outs, scratch, args, flops):
    return pl.pallas_call(
        kernel,
        grid=(grid,),
        in_specs=ins,
        out_specs=[s for s, _ in outs],
        out_shape=[o for _, o in outs],
        scratch_shapes=scratch,
        compiler_params=pltpu.CompilerParams(
            dimension_semantics=("arbitrary",), vmem_limit_bytes=VMEM
        ),
        cost_estimate=pl.CostEstimate(flops=flops, bytes_accessed=16 << 20, transcendentals=0),
    )(*args)


def gather_mp(acts, a, b, c):
    other = lax.ppermute(acts, "mp", mp_shift(1, 0, 0))
    pair = jnp.where(a == 0, jnp.stack([acts, other]), jnp.stack([other, acts]))
    line = jnp.zeros((4,) + pair.shape, pair.dtype)
    parts = [pair] + [lax.ppermute(pair, "mp", mp_shift(0, d, 0)) for d in (1, 2, 3)]
    for d, part in enumerate(parts):
        line = lax.dynamic_update_index_in_dim(line, part, (b - d) % 4, 0)
    sibling = lax.ppermute(line, "mp", mp_shift(0, 0, 1))
    return jnp.where(c == 0, jnp.stack([line, sibling]), jnp.stack([sibling, line]))


def take(array, index):
    return lax.dynamic_index_in_dim(array, index, 0, keepdims=False)


def scatter_mp(parts, a, b, c):
    got = lax.ppermute(take(parts, 1 - c), "mp", mp_shift(0, 0, 1))
    line = (take(parts, c).astype(F32) + got.astype(F32)).astype(BF)
    total = take(line, b).astype(F32)
    for d in (1, 2, 3):
        got = lax.ppermute(take(line, (b + d) % 4), "mp", mp_shift(0, d, 0))
        total = total + got.astype(F32)
    pair = total.astype(BF)
    got = lax.ppermute(take(pair, 1 - a), "mp", mp_shift(1, 0, 0))
    return take(pair, a).astype(F32) + got.astype(F32)


def sum_mp(value):
    for shift in ((0, 0, 1), (0, 2, 0), (1, 0, 0)):
        value = value + lax.ppermute(value, "mp", mp_shift(*shift))
    flip = [(mp_index(a, b, c), mp_index(a, b ^ 1, c)) for a, b, c in ZXC]
    return value + lax.ppermute(value, "mp", flip)


def local(
    dec_input,
    enc_output,
    query_weight,
    key_weight,
    value_weight,
    output_weight,
    cotangent,
    enc_lengths,
    dec_lengths,
):
    place = lax.axis_index("mp")
    a, b, c = place // 8, (place // 2) % 4, place % 2
    tokens, feat = dec_input.shape[1:]
    width = query_weight.shape[1]
    erows = enc_output.shape[1]
    keys = erows * NB
    scale = width ** (-0.5)

    weights = lax.all_gather(
        jnp.concatenate([query_weight, key_weight, value_weight, output_weight.T], axis=1),
        "dp", axis=0, tiled=True,
    )

    own_enc = enc_output[0].reshape(erows, NB, feat).transpose(1, 0, 2).reshape(NB * erows, feat)
    acts = gather_mp(jnp.stack([dec_input[0], cotangent[0], own_enc]), a, b, c)
    acts = acts.transpose(2, 1, 0, 3, 4, 5).reshape(NB, 3, tokens, feat)
    hidden32 = acts[:, 0].astype(F32)
    square = jnp.sum(hidden32 * hidden32, axis=(0, 2))[:, None] / (NB * feat)
    inv_rms = lax.rsqrt(square + 1e-06)
    normed = (hidden32 * inv_rms).astype(BF)
    keep = (jnp.arange(tokens, dtype=jnp.int32) < dec_lengths[0])[:, None]
    masked = jnp.where(keep, acts[:, 1], jnp.zeros((), BF))
    encoded = (
        acts[:, 2].reshape(NB, NB, erows, feat).transpose(1, 0, 2, 3).reshape(NB, keys, feat)
    )

    block = pl.BlockSpec((1, tokens, feat), lambda i: (i, 0, 0))
    eblock = pl.BlockSpec((1, keys, feat), lambda i: (i, 0, 0))
    wblock = pl.BlockSpec((feat, 4 * width), lambda i: (i, 0))
    tspec = pl.BlockSpec((tokens, width), lambda i: (0, 0))
    kspec = pl.BlockSpec((keys, width), lambda i: (0, 0))
    tshape = jax.ShapeDtypeStruct((tokens, width), BF)
    kshape = jax.ShapeDtypeStruct((keys, width), BF)
    unit = 2 * tokens * feat * width * NB
    q_grad, k_grad, v_grad, attended, stat = call(
        functools.partial(forward_kernel, scale),
        NB,
        [pl.BlockSpec(memory_space=pltpu.SMEM), block, block, eblock, wblock],
        [
            (tspec, tshape), (kspec, kshape), (kspec, kshape), (tspec, tshape),
            (pl.BlockSpec((tokens, 128), lambda i: (0, 0)),
             jax.ShapeDtypeStruct((tokens, 128), F32)),
        ],
        [
            pltpu.VMEM((tokens, width), F32),
            pltpu.VMEM((keys, 2 * width), F32),
            pltpu.VMEM((tokens, width), F32),
        ],
        (enc_lengths, normed, masked, encoded, weights),
        4 * unit,
    )
    (grads,) = call(
        weight_grad_kernel,
        NB,
        [block, block, eblock, tspec, kspec, kspec, tspec],
        [(wblock, jax.ShapeDtypeStruct((NB * feat, 4 * width), BF))],
        [],
        (normed, masked, encoded, q_grad, k_grad, v_grad, attended),
        4 * unit,
    )
    share = lax.psum_scatter(grads, "dp", scatter_dimension=0, tiled=True)
    (parts,) = call(
        partial_kernel,
        NB,
        [wblock, tspec, kspec, kspec, tspec],
        [(
            pl.BlockSpec((2, 4, 2, 3, tokens, feat), lambda i: (0,) * 6),
            jax.ShapeDtypeStruct((2, 4, 2, 3, tokens, feat), BF),
        )],
        [],
        (weights, q_grad, k_grad, v_grad, attended),
        4 * unit,
    )
    stat = sum_mp(stat[:, :1]) / (NB * feat)
    total = scatter_mp(parts, a, b, c)

    own = dec_input[0].astype(F32)
    own_masked = jnp.where(keep, cotangent[0], jnp.zeros((), BF)).astype(F32)
    layer_out = (own + total[1]).astype(BF)[None]
    input_grad = (own_masked + inv_rms * total[0] - own * (inv_rms * inv_rms * stat)).astype(BF)[None]
    enc_grad = (
        total[2].astype(BF).reshape(NB, erows, feat).transpose(1, 0, 2).reshape(1, erows, NB * feat)
    )
    query_grad = share[:, :width]
    key_grad = share[:, width : 2 * width]
    value_grad = share[:, 2 * width : 3 * width]
    output_grad = share[:, 3 * width :].T
    return (layer_out, input_grad, enc_grad, query_grad, key_grad, value_grad, output_grad)


def solution(mesh):
    in_specs = (
        P("dp", None, "mp"),
        P("dp", "mp", None),
        P("dp", "mp"),
        P("dp", "mp"),
        P("dp", "mp"),
        P("mp", "dp"),
        P("dp", None, "mp"),
        P("dp"),
        P("dp"),
    )
    out_specs = (
        P("dp", None, "mp"),
        P("dp", None, "mp"),
        P("dp", "mp", None),
        P("dp", "mp"),
        P("dp", "mp"),
        P("dp", "mp"),
        P("mp", "dp"),
    )
    return jax.shard_map(local, mesh=mesh, in_specs=in_specs, out_specs=out_specs, check_vma=False)
```

time: 775 us -> 291 us (0.38)
  waiting for transfers between devices: 708 us -> 170 us
  Pallas kernels: 0 us -> 33.9 us
  starting transfers between devices: 0.61 us -> 32.3 us
  matrix products: 27.7 us -> 0 us
  local copies, waits for them, and re-layouts: 6.2 us -> 19.2 us
    all_gather x7 -> x1, waiting for transfers between devices: 352 us -> 37 us  [local(): lax.all_gather(jnp.concatenate([query_weight, key_weight, value_weight, o...]
    reduce_scatter x3 -> x1, waiting for transfers between devices: 246 us -> 23.1 us  [local(): share = lax.psum_scatter(grads, 'dp', scatter_dimension=0, tiled=True)]
    ppermute x0 -> x14, waiting for transfers between devices: none -> 110 us  [the longest x3 37 us: scatter_mp(): got = lax.ppermute(take(line, (b + d) % 4), 'mp', mp_shift(0, d, 0))]
    psum x1 -> x0, waiting for transfers between devices: 105 us -> none  [local(): lax.psum(normed_part.astype(jnp.bfloat16), 'mp').astype(jnp.float32)]
    pallas_call x0 -> x3, Pallas kernels: none -> 33.9 us  [call(): pl.pallas_call(kernel, grid=(grid,), in_specs=ins, out_specs=[s for s, _...]
    ppermute x0 -> x14, starting transfers between devices: none -> 32.3 us  [the longest x1 15.3 us: scatter_mp(): got = lax.ppermute(take(pair, 1 - a), 'mp', mp_shift(1, 0, 0))]
    dot_general x18 -> x0, matrix products: 27.7 us -> none  [the longest x1 3.67 us: local(): jnp.dot(attended, output_full, preferred_element_type=jnp.float32)]
  transfers between devices with their start and end apart: 11 -> 16, of which waited for: 11 -> 14; matrix products, arithmetic and copies ran while one was open for 5% -> 9% of each run, Pallas kernels for 0% -> 4%
where the time goes in v1:
time: 291 us; the launch traced here: 290 us
  waiting for transfers between devices  170 us (58%)
  Pallas kernels  33.9 us (12%)
  starting transfers between devices  32.3 us (11%)
  other arithmetic  19.3 us (7%)
  local copies, waits for them, and re-layouts  19.2 us (7%)
  between operations  15.6 us (5%)
    all_gather x1, waiting for transfers between devices, local(): lax.all_gather(jnp.concatenate([query_weight, key_weight, value_weight, o...  37 us
    ppermute x3, waiting for transfers between devices, scatter_mp(): got = lax.ppermute(take(line, (b + d) % 4), 'mp', mp_shift(0, d, 0))  37 us
    pallas_call x3, Pallas kernels, call(): pl.pallas_call(kernel, grid=(grid,), in_specs=ins, out_specs=[s for s, _...  33.9 us
    ppermute x3, waiting for transfers between devices, gather_mp(): lax.ppermute(pair, 'mp', mp_shift(0, d, 0))  29.9 us
    reduce_scatter x1, waiting for transfers between devices, local(): share = lax.psum_scatter(grads, 'dp', scatter_dimension=0, tiled=True)  23.1 us
    ppermute x3, waiting for transfers between devices, sum_mp(): value = value + lax.ppermute(value, 'mp', mp_shift(*shift))  22 us
    ppermute x1, starting transfers between devices, scatter_mp(): got = lax.ppermute(take(pair, 1 - a), 'mp', mp_shift(1, 0, 0))  15.3 us
    unnamed x19, local copies, waits for them, and re-layouts  9.03 us
  transfers between devices with their start and end apart: 16, of which 14 were waited for; matrix products, arithmetic and copies ran while one was open for 9% of the time, Pallas kernels for 4%

profile of v1, /device:TPU:1, one launch (start us, length us, event | category | flops | bytes accessed | tf_op | source)
XLA Modules:
  0.0 290.4 jit_solution(9269204558048325018)
XLA Ops:
  12.2 2.6 collective-permute-start
  14.8 7.8 %collective-permute-done = bf16[3,256,256]{2,1,0:T(8,128)(2,1)S(1)} collective-permute-done((bf16[3,256,256]{2,1,0:T(8,128)(2,1)S(1)}, bf16[3,256,256]{2,1,0:T(8,128)(2,1)S(1)}, u32[]{:S(2)}, u32[]{:S(2)}) %collective-permute-start) | collective-permute-done | bytes 393248 | tf_op jit(solution)/shard_map/ppermute | solution.py:122
  23.6 2.1 collective-permute-start.1
  25.7 2.5 collective-permute-start.2
  30.5 12.8 %collective-permute-done.1 = bf16[2,3,256,256]{3,2,1,0:T(8,128)(2,1)} collective-permute-done((bf16[2,3,256,256]{3,2,1,0:T(8,128)(2,1)}, bf16[2,3,256,256]{3,2,1,0:T(8,128)(2,1)}, u32[]{:S(2)}, u32[]{:S(2)}) %collective-permute-start.1) | collective-permute-done | bytes 786464 | tf_op jit(solution)/shard_map/ppermute | solution.py:125
  44.5 17.0 %collective-permute-done.2 = bf16[2,3,256,256]{3,2,1,0:T(8,128)(2,1)} collective-permute-done((bf16[2,3,256,256]{3,2,1,0:T(8,128)(2,1)}, bf16[2,3,256,256]{3,2,1,0:T(8,128)(2,1)}, u32[]{:S(2)}, u32[]{:S(2)}) %collective-permute-start.2) | collective-permute-done | bytes 786464 | tf_op jit(solution)/shard_map/ppermute | solution.py:125
  64.0 2.4 collective-permute-start.4
  67.7 4.1 %collective-permute-done.4 = bf16[4,2,3,256,256]{4,3,0,1,2:T(8,128)(2,1)} collective-permute-done((bf16[4,2,3,256,256]{4,3,0,1,2:T(8,128)(2,1)S(1)}, bf16[4,2,3,256,256]{4,3,0,1,2:T(8,128)(2,1)}, u32[]{:S(2)}, u32[]{:S(2)}) %collective-permute-start.4) | collective-permute-done | bytes 3145760 | tf_op jit(solution)/shard_map/ppermute | solution.py:128
  71.8 4.3 %maximum_select_fusion = bf16[2,4,2,3,256,256]{5,4,0,1,2,3:T(8,128)(2,1)S(1)} fusion(bf16[1,4,2,3,256,256]{5,4,0,1,2,3:T(8,128)(2,1)} %bitcast.11, bf16[1,4,2,3,256,256]{5,4,0,1,2,3:T(8,128)(2,1)S(1)} %bitcast.77, pred[]{:T(512)S(6)} %eq.16), kind=kLoop, calls=%fused_computation | loop fusion | flops 9437184 | bytes 12582913 | tf_op jit(solution)/shard_map/jit(_where)/select_n | solution.py:129
  80.7 37.0 %all-gather.2.cloned.1.call-done.weight_ref = bf16[4096,1024]{1,0:T(8,128)(2,1)} async-done(((bf16[256,1024]{1,0:T(8,128)(2,1)}), bf16[4096,1024]{1,0:T(8,128)(2,1)}) %all-gather.2.cloned.1.call-update) | async-done | bytes 8388624 | tf_op jit(solution)/shard_map/all_gather | solution.py:174
  120.9 12.4 %shard_map.144 = (bf16[256,256]{1,0:T(8,128)(2,1)S(1)}, bf16[256,256]{1,0:T(8,128)(2,1)S(1)}, bf16[256,256]{1,0:T(8,128)(2,1)S(1)}, bf16[256,256]{1,0:T(8,128)(2,1)S(1)}, f32[256,128]{1,0:T(8,128)S(1)}) custom-call(s32[1]{0:T(128)S(6)} %copy.44.length_ref, bf16[16,256,256]{2,1,0:T(8,128)(2,1)S(1)} %fusion.2.normed_ref, bf16[16,256,256]{2,1,0:T(8,128)(2,1)S(1)} %copy-done.2, ...), custom_call_target="tpu_custom_call" | custom-call | flops 2147483648 | bytes 16777216 | tf_op jit(solution)/shard_map/pallas_call | solution.py:107
  133.3 9.6 %shard_map.146 = bf16[4096,1024]{1,0:T(8,128)(2,1)} custom-call(bf16[16,256,256]{2,1,0:T(8,128)(2,1)S(1)} %fusion.2.normed_ref, bf16[16,256,256]{2,1,0:T(8,128)(2,1)S(1)} %copy-done.2, bf16[16,256,256]{2,1,0:T(8,128)(2,1)S(1)} %bitcast.71, bf16[256,256]{1,0:T(8,128)(2,1)S(1)} %get-tuple-element.12.qg_ref, bf16[256,256]{1,0:T(8,128)(2,1)S(1)} %get-tuple-element.13.kg_ref, ...), custom_call_target="tpu_custom_call" | custom-call | flops 2147483648 | bytes 16777216 | tf_op jit(solution)/shard_map/pallas_call | solution.py:107
  143.0 11.8 %shard_map.145 = bf16[2,4,2,3,256,256]{5,4,3,2,1,0:T(8,128)(2,1)S(1)} custom-call(bf16[4096,1024]{1,0:T(8,128)(2,1)} %all-gather.2.cloned.1.call-done.weight_ref, bf16[256,256]{1,0:T(8,128)(2,1)S(1)} %get-tuple-element.12.qg_ref, bf16[256,256]{1,0:T(8,128)(2,1)S(1)} %get-tuple-element.13.kg_ref, bf16[256,256]{1,0:T(8,128)(2,1)S(1)} %get-tuple-element.14.vg_ref, ...), custom_call_target="tpu_custom_call" | custom-call | flops 2147483648 | bytes 16777216 | tf_op jit(solution)/shard_map/pallas_call | solution.py:107
  155.0 2.5 copy-done
  158.2 5.4 %collective-permute-done.5 = bf16[4,2,3,256,256]{4,3,2,1,0:T(8,128)(2,1)} collective-permute-done((bf16[4,2,3,256,256]{4,3,2,1,0:T(8,128)(2,1)S(1)}, bf16[4,2,3,256,256]{4,3,2,1,0:T(8,128)(2,1)}, u32[]{:S(2)}, u32[]{:S(2)}) %collective-permute-start.5) | collective-permute-done | bytes 3145760 | tf_op jit(solution)/shard_map/ppermute | solution.py:137
  163.6 3.9 %fusion = bf16[4,2,3,256,256]{4,3,2,1,0:T(8,128)(2,1)S(1)} fusion(bf16[4,2,3,256,256]{4,3,2,1,0:T(8,128)(2,1)} %collective-permute-done.5, bf16[2,4,2,3,256,256]{5,4,3,2,1,0:T(8,128)(2,1)} %copy-done, s32[]{:T(128)S(6)} %select_n.141), kind=kLoop, calls=%fused_computation.2 | loop fusion | flops 6291456 | bytes 9437188 | tf_op jit(solution)/shard_map/convert_element_type | solution.py:138
  172.3 16.1 %collective-permute-done.8 = bf16[2,3,256,256]{3,2,1,0:T(8,128)(2,1)} collective-permute-done((bf16[2,3,256,256]{3,2,1,0:T(8,128)(2,1)}, bf16[2,3,256,256]{3,2,1,0:T(8,128)(2,1)}, u32[]{:S(2)}, u32[]{:S(2)}) %collective-permute-start.8) | collective-permute-done | bytes 786464 | tf_op jit(solution)/shard_map/ppermute | solution.py:141
  188.4 3.0 %collective-permute-done.7 = bf16[2,3,256,256]{3,2,1,0:T(8,128)(2,1)} collective-permute-done((bf16[2,3,256,256]{3,2,1,0:T(8,128)(2,1)}, bf16[2,3,256,256]{3,2,1,0:T(8,128)(2,1)}, u32[]{:S(2)}, u32[]{:S(2)}) %collective-permute-start.7) | collective-permute-done | bytes 786464 | tf_op jit(solution)/shard_map/ppermute | solution.py:141
  191.4 17.8 %collective-permute-done.6 = bf16[2,3,256,256]{3,2,1,0:T(8,128)(2,1)} collective-permute-done((bf16[2,3,256,256]{3,2,1,0:T(8,128)(2,1)}, bf16[2,3,256,256]{3,2,1,0:T(8,128)(2,1)}, u32[]{:S(2)}, u32[]{:S(2)}) %collective-permute-start.6) | collective-permute-done | bytes 786464 | tf_op jit(solution)/shard_map/ppermute | solution.py:141
  211.4 15.3 %collective-permute-start.9 = (bf16[3,256,256]{2,1,0:T(8,128)(2,1)S(1)}, bf16[3,256,256]{2,1,0:T(8,128)(2,1)S(1)}, u32[]{:S(2)}, u32[]{:S(2)}) collective-permute-start(bf16[3,256,256]{2,1,0:T(8,128)(2,1)S(1)} %dynamic-slice_bitcast_fusion.4), channel_id=1, source_target_pairs={{0,8},{1,9},{2,10},{3,11},{4,12},{5,13},{6,14},{7,15},{8,0},{9,1},... | collective-permute-start | bytes 1179656 | tf_op jit(solution)/shard_map/ppermute | solution.py:144
  229.2 5.9 %collective-permute-done.11 = f32[256,1]{1,0:T(8,128)S(1)} collective-permute-done((f32[256,1]{1,0:T(8,128)S(1)}, f32[256,1]{1,0:T(8,128)S(1)}, u32[]{:S(2)}, u32[]{:S(2)}) %collective-permute-start.11) | collective-permute-done | bytes 1056 | tf_op jit(solution)/shard_map/ppermute | solution.py:150
  235.2 15.2 %collective-permute-done.12 = f32[256,1]{1,0:T(8,128)S(1)} collective-permute-done((f32[256,1]{1,0:T(8,128)S(1)}, f32[256,1]{1,0:T(8,128)S(1)}, u32[]{:S(2)}, u32[]{:S(2)}) %collective-permute-start.12) | collective-permute-done | bytes 1056 | tf_op jit(solution)/shard_map/ppermute | solution.py:150
  251.3 3.7 %collective-permute-done.13 = f32[256,1]{1,0:T(8,128)S(1)} collective-permute-done((f32[256,1]{1,0:T(8,128)S(1)}, f32[256,1]{1,0:T(8,128)S(1)}, u32[]{:S(2)}, u32[]{:S(2)}) %collective-permute-start.13) | collective-permute-done | bytes 1056 | tf_op jit(solution)/shard_map/ppermute | solution.py:152
  257.9 23.1 %reduce-scatter.2.cloned.1.call-done = bf16[256,1024]{1,0:T(8,128)(2,1)} async-done(((bf16[4096,1024]{1,0:T(8,128)(2,1)}), bf16[256,1024]{1,0:T(8,128)(2,1)}) %reduce-scatter.2.cloned.1.call-update) | async-done | bytes 524304 | tf_op jit(solution)/shard_map/reduce_scatter | solution.py:226
  (65 shorter events, 36.4 us)
Async XLA Ops:
  7.2 110.5 %all-gather.2.cloned.1.call-start = ((), (), s32[]{:S(2)}) async-start(), calls=%async_computation.1 | async-start | bytes 8912896 | tf_op jit(solution)/shard_map/all_gather | solution.py:174
  10.1 270.8 %reduce-scatter.2.cloned.1.call-start = ((), (), s32[]{:S(2)}) async-start(), calls=%async_computation.2 | async-start | bytes 8912896 | tf_op jit(solution)/shard_map/reduce_scatter | solution.py:226
  12.2 10.3 %collective-permute-start = (bf16[3,256,256]{2,1,0:T(8,128)(2,1)S(1)}, bf16[3,256,256]{2,1,0:T(8,128)(2,1)S(1)}, u32[]{:S(2)}, u32[]{:S(2)}) collective-permute-start(bf16[3,256,256]{2,1,0:T(8,128)(2,1)S(1)} %get-tuple-element.42), channel_id=1, source_target_pairs={{0,8},{1,9},{2,10},{3,11},{4,12},{5,13},{6,14},{7,15},{8,0},{9,1},... | collective-permute-start | bytes 1179656 | tf_op jit(solution)/shard_map/ppermute | solution.py:122
  22.6 6.8 %copy-start.4 = (bf16[3,256,256]{2,1,0:T(8,128)(2,1)}, bf16[3,256,256]{2,1,0:T(8,128)(2,1)S(1)}, u32[]{:S(2)}) copy-start(bf16[3,256,256]{2,1,0:T(8,128)(2,1)S(1)} %collective-permute-done) | copy-start | bytes 1179652
  23.6 19.8 %collective-permute-start.1 = (bf16[2,3,256,256]{3,2,1,0:T(8,128)(2,1)}, bf16[2,3,256,256]{3,2,1,0:T(8,128)(2,1)}, u32[]{:S(2)}, u32[]{:S(2)}) collective-permute-start(bf16[2,3,256,256]{3,2,1,0:T(8,128)(2,1)} %maximum_select_fusion.2), channel_id=1, source_target_pairs={{0,2},{1,3},{2,4},{3,5},{4,6},{5,7},{6,0},{7,1},{8,10},{9,11},{10,... | collective-permute-start | bytes 2359304 | tf_op jit(solution)/shard_map/ppermute | solution.py:125
  25.7 35.8 %collective-permute-start.2 = (bf16[2,3,256,256]{3,2,1,0:T(8,128)(2,1)}, bf16[2,3,256,256]{3,2,1,0:T(8,128)(2,1)}, u32[]{:S(2)}, u32[]{:S(2)}) collective-permute-start(bf16[2,3,256,256]{3,2,1,0:T(8,128)(2,1)} %maximum_select_fusion.2), channel_id=1, source_target_pairs={{0,4},{1,5},{2,6},{3,7},{4,0},{5,1},{6,2},{7,3},{8,12},{9,13},{10,... | collective-permute-start | bytes 2359304 | tf_op jit(solution)/shard_map/ppermute | solution.py:125
  28.2 34.6 %collective-permute-start.3 = (bf16[2,3,256,256]{3,2,1,0:T(8,128)(2,1)}, bf16[2,3,256,256]{3,2,1,0:T(8,128)(2,1)}, u32[]{:S(2)}, u32[]{:S(2)}) collective-permute-start(bf16[2,3,256,256]{3,2,1,0:T(8,128)(2,1)} %maximum_select_fusion.2), channel_id=1, source_target_pairs={{0,6},{1,7},{2,0},{3,1},{4,2},{5,3},{6,4},{7,5},{8,14},{9,15},{10,... | collective-permute-start | bytes 2359304 | tf_op jit(solution)/shard_map/ppermute | solution.py:125
  29.3 1.0 copy-start.5
  64.0 7.8 %collective-permute-start.4 = (bf16[4,2,3,256,256]{4,3,0,1,2:T(8,128)(2,1)S(1)}, bf16[4,2,3,256,256]{4,3,0,1,2:T(8,128)(2,1)}, u32[]{:S(2)}, u32[]{:S(2)}) collective-permute-start(bf16[4,2,3,256,256]{4,3,0,1,2:T(8,128)(2,1)S(1)} %copy_dynamic-update-slice_fusion), channel_id=1, source_target_pairs={{0,1},{1,0},{2,3},{3,2},{4,5},{5,4},{6,7},{7,6},{8,9},{9,8},{10,11... | collective-permute-start | bytes 9437192 | tf_op jit(solution)/shard_map/ppermute | solution.py:128
  117.7 1.6 copy-start.1
  119.3 1.6 copy-start.2
  154.8 2.7 copy-start
  157.5 6.1 %collective-permute-start.5 = (bf16[4,2,3,256,256]{4,3,2,1,0:T(8,128)(2,1)S(1)}, bf16[4,2,3,256,256]{4,3,2,1,0:T(8,128)(2,1)}, u32[]{:S(2)}, u32[]{:S(2)}) collective-permute-start(bf16[4,2,3,256,256]{4,3,2,1,0:T(8,128)(2,1)S(1)} %dynamic-slice_bitcast_fusion), channel_id=1, source_target_pairs={{0,1},{1,0},{2,3},{3,2},{4,5},{5,4},{6,7},{7,6},{8,9},{9,8},{10,11... | collective-permute-start | bytes 9437192 | tf_op jit(solution)/shard_map/ppermute | solution.py:137
  169.1 19.3 %collective-permute-start.8 = (bf16[2,3,256,256]{3,2,1,0:T(8,128)(2,1)}, bf16[2,3,256,256]{3,2,1,0:T(8,128)(2,1)}, u32[]{:S(2)}, u32[]{:S(2)}) collective-permute-start(bf16[2,3,256,256]{3,2,1,0:T(8,128)(2,1)} %get-tuple-element.32), channel_id=1, source_target_pairs={{0,6},{1,7},{2,0},{3,1},{4,2},{5,3},{6,4},{7,5},{8,14},{9,15},{10,... | collective-permute-start | bytes 2359304 | tf_op jit(solution)/shard_map/ppermute | solution.py:141
  171.1 20.3 %collective-permute-start.7 = (bf16[2,3,256,256]{3,2,1,0:T(8,128)(2,1)}, bf16[2,3,256,256]{3,2,1,0:T(8,128)(2,1)}, u32[]{:S(2)}, u32[]{:S(2)}) collective-permute-start(bf16[2,3,256,256]{3,2,1,0:T(8,128)(2,1)} %get-tuple-element.33), channel_id=1, source_target_pairs={{0,4},{1,5},{2,6},{3,7},{4,0},{5,1},{6,2},{7,3},{8,12},{9,13},{10,... | collective-permute-start | bytes 2359304 | tf_op jit(solution)/shard_map/ppermute | solution.py:141
  171.7 37.6 %collective-permute-start.6 = (bf16[2,3,256,256]{3,2,1,0:T(8,128)(2,1)}, bf16[2,3,256,256]{3,2,1,0:T(8,128)(2,1)}, u32[]{:S(2)}, u32[]{:S(2)}) collective-permute-start(bf16[2,3,256,256]{3,2,1,0:T(8,128)(2,1)} %get-tuple-element.31), channel_id=1, source_target_pairs={{0,2},{1,3},{2,4},{3,5},{4,6},{5,7},{6,0},{7,1},{8,10},{9,11},{10,... | collective-permute-start | bytes 2359304 | tf_op jit(solution)/shard_map/ppermute | solution.py:141
  211.3 17.3 %copy-start.3 = (bf16[2,3,256,256]{3,2,1,0:T(8,128)(2,1)}, bf16[2,3,256,256]{3,2,1,0:T(8,128)(2,1)S(1)}, u32[]{:S(2)}) copy-start(bf16[2,3,256,256]{3,2,1,0:T(8,128)(2,1)S(1)} %fusion.6) | copy-start | bytes 2359300
  211.3 45.7 %copy-start.6 = (bf16[1,256,256]{2,1,0:T(8,128)(2,1)S(1)}, bf16[1,256,256]{2,1,0:T(8,128)(2,1)}, u32[]{:S(2)}) copy-start(bf16[1,256,256]{2,1,0:T(8,128)(2,1)} %param.9) | copy-start | bytes 393220
  211.3 45.7 %copy-start.7 = (bf16[1,256,256]{2,1,0:T(8,128)(2,1)S(1)}, bf16[1,256,256]{2,1,0:T(8,128)(2,1)}, u32[]{:S(2)}) copy-start(bf16[1,256,256]{2,1,0:T(8,128)(2,1)} %param.15) | copy-start | bytes 393220
  211.4 43.8 %collective-permute-start.9 = (bf16[3,256,256]{2,1,0:T(8,128)(2,1)S(1)}, bf16[3,256,256]{2,1,0:T(8,128)(2,1)S(1)}, u32[]{:S(2)}, u32[]{:S(2)}) collective-permute-start(bf16[3,256,256]{2,1,0:T(8,128)(2,1)S(1)} %dynamic-slice_bitcast_fusion.4), channel_id=1, source_target_pairs={{0,8},{1,9},{2,10},{3,11},{4,12},{5,13},{6,14},{7,15},{8,0},{9,1},... | collective-permute-start | bytes 1179656 | tf_op jit(solution)/shard_map/ppermute | solution.py:144
  226.7 1.9 collective-permute-start.10
  228.7 6.4 %collective-permute-start.11 = (f32[256,1]{1,0:T(8,128)S(1)}, f32[256,1]{1,0:T(8,128)S(1)}, u32[]{:S(2)}, u32[]{:S(2)}) collective-permute-start(f32[256,1]{1,0:T(8,128)S(1)} %slice_add_fusion), channel_id=1, source_target_pairs={{0,4},{1,5},{2,6},{3,7},{4,0},{5,1},{6,2},{7,3},{8,12},{9,13},{10,... | collective-permute-start | bytes 3080 | tf_op jit(solution)/shard_map/ppermute | solution.py:150
  235.1 15.3 %collective-permute-start.12 = (f32[256,1]{1,0:T(8,128)S(1)}, f32[256,1]{1,0:T(8,128)S(1)}, u32[]{:S(2)}, u32[]{:S(2)}) collective-permute-start(f32[256,1]{1,0:T(8,128)S(1)} %add.177), channel_id=1, source_target_pairs={{0,8},{1,9},{2,10},{3,11},{4,12},{5,13},{6,14},{7,15},{8,0},{9,1},... | collective-permute-start | bytes 3080 | tf_op jit(solution)/shard_map/ppermute | solution.py:150
  250.4 4.6 %collective-permute-start.13 = (f32[256,1]{1,0:T(8,128)S(1)}, f32[256,1]{1,0:T(8,128)S(1)}, u32[]{:S(2)}, u32[]{:S(2)}) collective-permute-start(f32[256,1]{1,0:T(8,128)S(1)} %add.178), channel_id=1, source_target_pairs={{0,2},{1,3},{2,0},{3,1},{4,6},{5,7},{6,4},{7,5},{8,10},{9,11},{10,... | collective-permute-start | bytes 3080 | tf_op jit(solution)/shard_map/ppermute | solution.py:152
Sparse Core Ops, SparseCore 0:
  10.4 107.1 all-gather.1
  143.1 137.7 reduce-scatter.1

commit v2 on v0

v2 whole, which is shorter than its diff:
```python
import functools

import jax
import jax.numpy as jnp
from jax import lax
from jax.experimental import pallas as pl
from jax.experimental.pallas import tpu as pltpu
from jax.sharding import PartitionSpec as P

BF = jnp.bfloat16
F32 = jnp.float32
NB = 16
MIB = 1024 * 1024
COST = 16
EXTRA = 16

YZ = [(y, z) for y in range(4) for z in range(4)]
ZXC = [(a, b, c) for a in range(2) for b in range(4) for c in range(2)]


def dp_index(y, z):
    return (y % 4) * 4 + (z % 4)


def mp_index(a, b, c):
    return (a % 2) * 8 + (b % 4) * 2 + (c % 2)


def send_y(value, d):
    return lax.ppermute(value, "dp", [(dp_index(y, z), dp_index(y + d, z)) for y, z in YZ])


def send_z(value, d):
    return lax.ppermute(value, "dp", [(dp_index(y, z), dp_index(y, z + d)) for y, z in YZ])


def send_mp(value, da, db, dc):
    pairs = [(mp_index(a, b, c), mp_index(a + da, b + db, c + dc)) for a, b, c in ZXC]
    return lax.ppermute(value, "mp", pairs)


def send_x(value, bits):
    pairs = [(mp_index(a, b, c), mp_index(a, b ^ bits, c)) for a, b, c in ZXC]
    return lax.ppermute(value, "mp", pairs)


def nn(a, b):
    return lax.dot_general(a, b, (((1,), (0,)), ((), ())), preferred_element_type=F32)


def nt(a, b):
    return lax.dot_general(a, b, (((1,), (1,)), ((), ())), preferred_element_type=F32)


def tn(a, b):
    return lax.dot_general(a, b, (((0,), (0,)), ((), ())), preferred_element_type=F32)


def shape_of(shape, dtype=BF):
    return jax.ShapeDtypeStruct(shape, dtype)


def call(kernel, args, outs, scalars=(), scratch=(), flops=0, moved=0, vmem=8):
    spec = pl.BlockSpec(memory_space=pltpu.VMEM)
    return pl.pallas_call(
        kernel,
        in_specs=[pl.BlockSpec(memory_space=pltpu.SMEM)] * len(scalars) + [spec] * len(args),
        out_specs=[spec] * len(outs),
        out_shape=outs,
        scratch_shapes=scratch,
        compiler_params=pltpu.CompilerParams(vmem_limit_bytes=vmem * MIB),
        cost_estimate=pl.CostEstimate(flops=COST * flops, bytes_accessed=moved, transcendentals=0),
    )(*scalars, *args)


def call_out(kernel, args, outs, scalars=()):
    spec = pl.BlockSpec(memory_space=pltpu.VMEM)
    n = len(outs)

    def body(*refs):
        ins, results, sems = refs[: -2 * n - 1], refs[-2 * n - 1 : -n - 1], refs[-1]
        held = refs[-n - 1 : -1]
        kernel(*ins, *held)
        copies = [
            pltpu.make_async_copy(a, b, sems.at[k]) for k, (a, b) in enumerate(zip(held, results))
        ]
        for copy in copies:
            copy.start()
        for copy in copies:
            copy.wait()

    return pl.pallas_call(
        body,
        in_specs=[pl.BlockSpec(memory_space=pltpu.SMEM)] * len(scalars) + [spec] * len(args),
        out_specs=[pl.BlockSpec(memory_space=pltpu.HBM)] * n,
        out_shape=outs,
        scratch_shapes=[pltpu.VMEM(o.shape, o.dtype) for o in outs] + [pltpu.SemaphoreType.DMA((n,))],
        compiler_params=pltpu.CompilerParams(vmem_limit_bytes=8 * MIB),
    )(*scalars, *args)


def mp_place():
    place = lax.axis_index("mp")
    return lax.div(place, 8), lax.rem(lax.div(place, 2), 4), lax.rem(place, 2)


def dp_block(dy, dz):
    part = lax.axis_index("dp")
    return lax.rem(lax.div(part, 4) + dy, 4) * 4 + lax.rem(lax.rem(part, 4) + dz, 4)


def blocks_at(dz):
    return [dp_block(dy, dz) for dy in range(4)]


def after(values, *others):
    out = lax.optimization_barrier((others, tuple(values)))
    return out[1]


def pack_stat(row, shape):
    high = row.astype(BF).astype(F32)
    line = lax.broadcasted_iota(jnp.int32, shape, 0)
    rows = jnp.where(line == 0, high, jnp.where(line == 1, row - high, 0.0))
    return rows.astype(BF)


def stat_of(rows):
    return jnp.sum(rows.astype(F32), axis=0, keepdims=True)


def assemble_kernel(q_ref, k_ref, v_ref, o_ref, dec_ref, cot_ref, enc_ref, block_ref, acts_ref, o_buf, enc_buf, sems):
    width, feat = q_ref.shape[1], cot_ref.shape[2]
    tokens, erows = cot_ref.shape[1], enc_ref.shape[1]
    pairs = [(ref, block_ref.at[:, n * width : (n + 1) * width]) for n, ref in enumerate((q_ref, k_ref, v_ref))]
    pairs += [(o_ref, o_buf), (enc_ref.at[0], enc_buf)]
    pairs += [(dec_ref.at[0], acts_ref.at[:tokens]), (cot_ref.at[0], acts_ref.at[tokens : 2 * tokens])]
    copies = [pltpu.make_async_copy(a, b, sems.at[n]) for n, (a, b) in enumerate(pairs)]
    for copy in copies:
        copy.start()
    copies[3].wait()
    block_ref[:, 3 * width :] = o_buf[...].T
    copies[4].wait()
    for n in range(NB):
        line = 2 * tokens + n * erows
        acts_ref[line : line + erows] = enc_buf[:, n * feat : (n + 1) * feat]
    for n in (0, 1, 2, 5, 6):
        copies[n].wait()


def pair_kernel(first, second, out_ref):
    out_ref[0] = first[...]
    out_ref[1] = second[...]


def pick_kernel(first, second, out_first, out_second):
    out_first[...] = first[0]
    out_second[...] = second[1]


def halves_kernel(first, second, out_first, out_second):
    half = out_first.shape[0]
    out_first[...] = first[:half]
    out_second[...] = second[half:]


def prepare_kernel(len_ref, *refs):
    pieces, (normed_ref, masked_ref, enc_ref, inv_ref) = refs[:4], refs[4:]
    tokens, feat = normed_ref.shape[1:]
    erows = enc_ref.shape[1] // NB
    a, b, c = mp_place()
    square = jnp.zeros((tokens, 1), F32)
    for piece in pieces:

        def add_squares(k, total, piece=piece):
            hidden = piece[lax.div(k, 2), lax.rem(k, 2), :tokens].astype(F32)
            return total + jnp.sum(hidden * hidden, axis=1, keepdims=True)

        square = lax.fori_loop(0, 4, add_squares, square)
    inv_rms = lax.rsqrt(square / (NB * feat) + 1e-06)
    inv_ref[...] = jnp.broadcast_to(inv_rms, inv_ref.shape)
    keep = lax.broadcasted_iota(jnp.int32, (tokens, feat), 0) < len_ref[0]
    for n, piece in enumerate(pieces):

        def write(k, carry, n=n, piece=piece):
            x, z = lax.div(k, 2), lax.rem(k, 2)
            spot = lax.bitwise_xor(b, x + 2 * (n % 2))
            place = lax.rem(a + z, 2) * 8 + spot * 2 + lax.rem(c + n // 2, 2)
            normed_ref[place] = (piece[x, z, :tokens].astype(F32) * inv_ref[:, :1]).astype(BF)
            rows = piece[x, z, tokens : 2 * tokens]
            masked_ref[place] = jnp.where(keep, rows.astype(F32), 0.0).astype(BF)
            start = pl.multiple_of(place * erows, erows)
            for m in range(NB):
                line = 2 * tokens + m * erows
                enc_ref[m, pl.ds(start, erows), :] = piece[x, z, line : line + erows]
            return carry

        lax.fori_loop(0, 4, write, 0)


def attention(scale, enc_len, query, keyed, valued, attended_grad):
    scores = nt(query, keyed) * scale
    column = lax.broadcasted_iota(jnp.int32, scores.shape, 1)
    scores = jnp.where(column < enc_len, scores, -1e30)
    shifted = jnp.exp(scores - jnp.max(scores, axis=-1, keepdims=True))
    probs = shifted / jnp.sum(shifted, axis=-1, keepdims=True)
    probs_low = probs.astype(BF)
    attended = nn(probs_low, valued).astype(BF)
    probs_grad = nt(attended_grad, valued)
    inner = jnp.sum(probs * probs_grad, axis=-1, keepdims=True)
    scores_grad = (probs * (probs_grad - inner) * scale).astype(BF)
    q_grad = nn(scores_grad, keyed).astype(BF)
    k_grad = tn(scores_grad, query).astype(BF)
    v_grad = tn(probs_low, attended_grad).astype(BF)
    stat = jnp.sum(q_grad.astype(F32) * query.astype(F32), axis=-1, keepdims=True)
    return q_grad, k_grad, v_grad, attended, stat


def project(places, pieces, normed_ref, masked_ref, enc_ref, stack_ref, init):
    width = stack_ref.shape[2] // 4
    for n, piece in enumerate(pieces):
        stack_ref[n] = piece()
    out = init
    for n in range(0, len(pieces), 4):
        group = places[n : n + 4]
        rows = jnp.concatenate([stack_ref[n + k] for k in range(4)], axis=0)
        normed, enc, masked = (
            jnp.concatenate([ref[p] for p in group], axis=1)
            for ref in (normed_ref, enc_ref, masked_ref)
        )
        new = (
            nn(normed, rows[:, :width]),
            nn(enc, rows[:, width : 2 * width]),
            nn(enc, rows[:, 2 * width : 3 * width]),
            nn(masked, rows[:, 3 * width :]),
        )
        out = new if out is None else tuple(o + v for o, v in zip(out, new))
    return out


def one(ref):
    return lambda: ref[...]


def at(ref, n):
    return lambda: ref[n]


def both(low, high):
    return lambda: jnp.concatenate([low[...], high[...]], axis=0)


def own_kernel(normed_ref, masked_ref, enc_ref, *refs):
    own, high, low, across, acc_ref, stack_ref = refs
    pieces = [one(own), one(high), one(across), one(low)]
    acc = project(blocks_at(0), pieces, normed_ref, masked_ref, enc_ref, stack_ref, None)
    for n in range(4):
        acc_ref[n] = acc[n]


def near_kernel(normed_ref, masked_ref, enc_ref, *refs):
    pair, high, low, across_b, across_a, acc_in, acc_ref, stack_ref = refs
    pieces = [at(pair, 0), at(high, 0), one(across_b), at(low, 0)]
    pieces += [at(pair, 1), at(high, 1), one(across_a), at(low, 1)]
    places = blocks_at(3) + blocks_at(1)
    init = [acc_in[n] for n in range(4)]
    acc = project(places, pieces, normed_ref, masked_ref, enc_ref, stack_ref, init)
    for n in range(4):
        acc_ref[n] = acc[n]


def far_kernel(scale, len_ref, normed_ref, masked_ref, enc_ref, *refs):
    far, high, low, across_low, across_high, acc_in = refs[:6]
    qg_ref, kv_ref, at_ref, qgt_ref, kvt_ref, att_ref, stat_ref, stack_ref = refs[6:]
    pieces = [one(far), one(high), both(across_low, across_high), one(low)]
    init = [acc_in[n] for n in range(4)]
    acc = project(blocks_at(2), pieces, normed_ref, masked_ref, enc_ref, stack_ref, init)
    out = attention(scale, len_ref[0], *(value.astype(BF) for value in acc))
    q_grad, k_grad, v_grad, attended, stat = out
    width = q_grad.shape[1]
    qg_ref[...] = q_grad
    kv_ref[:, :width] = k_grad
    kv_ref[:, width:] = v_grad
    at_ref[...] = attended
    qgt_ref[...] = q_grad.T
    kvt_ref[:width] = k_grad.T
    kvt_ref[width:] = v_grad.T
    att_ref[...] = attended.T
    row = jnp.broadcast_to(stat, (stat.shape[0], 128)).T[0:1]
    stat_ref[...] = pack_stat(row, stat_ref.shape)


def weight_grad_kernel(dz, normed_ref, masked_ref, enc_ref, *refs):
    qgt_ref, kvt_ref, att_ref = refs[:3]
    outs = list(refs[3:])
    width = qgt_ref.shape[0]
    for n in range(4):
        place = dp_block(n, dz)
        query = nn(qgt_ref[...], normed_ref[place]).astype(BF)
        pair = nn(kvt_ref[...], enc_ref[place]).astype(BF)
        attn = nn(att_ref[...], masked_ref[place]).astype(BF)
        if n == 2 and len(outs) == 3:
            low, high = outs.pop(0), outs.pop(0)
            low[:width] = query
            low[width:] = pair[:width]
            high[:width] = pair[width:]
            high[width:] = attn
        else:
            out = outs.pop(0)
            out[:width] = query
            out[width : 3 * width] = pair
            out[3 * width :] = attn


def partial_kernel(qg_ref, kv_ref, at_ref, stat_ref, *refs):
    stacks, outs, enc_buf = refs[:3], refs[3:5], refs[5]
    tokens, width = qg_ref.shape
    keys, feat = enc_buf.shape
    erows = keys // NB
    a, b, c = mp_place()
    for out in outs:
        for xr in range(4):
            for zr in range(2):
                out[xr, zr, 3 * tokens :, :] = stat_ref[...]
    for stack, shifts in zip(stacks, ((0, 0), (3, 1), (2, 2))):

        def body(n, carry, stack=stack, shifts=shifts):
            place = dp_block(lax.rem(n, 4), jnp.where(n < 4, shifts[0], shifts[1]))
            weight = stack[n]
            norm_part = nt(qg_ref[...], weight[:, :width]).astype(BF)
            out_part = nt(at_ref[...], weight[:, 3 * width :]).astype(BF)
            enc_buf[...] = nt(kv_ref[...], weight[:, width : 3 * width]).astype(BF)
            xr = lax.bitwise_xor(lax.rem(lax.div(place, 2), 4), b)
            zr = lax.rem(lax.div(place, 8) + 2 - a, 2)
            cr = lax.rem(lax.rem(place, 2) + 2 - c, 2)
            line = pl.multiple_of(2 * tokens + place * erows, erows)
            for k, out in enumerate(outs):

                @pl.when(cr == k)
                def _():
                    out[xr, zr, :tokens, :] = norm_part
                    out[xr, zr, tokens : 2 * tokens, :] = out_part

                for x in range(4):
                    for z in range(2):
                        owner = lax.rem(a + z, 2) * 8 + lax.bitwise_xor(b, x) * 2 + lax.rem(c + k, 2)
                        start = pl.multiple_of(owner * erows, erows)
                        out[x, z, pl.ds(line, erows), :] = enc_buf[pl.ds(start, erows), :]
            return carry

        lax.fori_loop(0, stack.shape[0], body, 0, unroll=2)


def add_rows(ins, out):
    rows, feat = out.shape[0] - EXTRA, out.shape[1]

    def body(step, carry):
        part = pl.ds(pl.multiple_of(step * CHUNK, CHUNK), CHUNK)
        total = ins[0][part, :].astype(F32)
        for ref in ins[1:]:
            total += ref[part, :].astype(F32)
        out[part, :] = total.astype(BF)
        return carry

    lax.fori_loop(0, rows // CHUNK, body, 0)
    stat = stat_of(ins[0][rows:])
    for ref in ins[1:]:
        stat += stat_of(ref[rows:])
    out[rows:] = pack_stat(stat, (EXTRA, feat))


def core_sum_kernel(keep_ref, got_ref, near_ref, far_ref):
    for x, out in enumerate((near_ref.at[0], near_ref.at[1], far_ref.at[0], far_ref.at[1])):
        for z in range(2):
            add_rows([keep_ref.at[x, z], got_ref.at[x, z]], out.at[z])


def split_sum_kernel(first_ref, second_ref, *outs):
    for n, out in enumerate(outs):
        if len(out.shape) == 2:
            add_rows([first_ref.at[n], second_ref.at[n]], out)
        else:
            for z in range(2):
                add_rows([first_ref.at[n, z], second_ref.at[n, z]], out.at[z])


def share_kernel(*refs):
    ins, outs = refs[:-4], refs[-4:]
    total = ins[0][...].astype(F32)
    for ref in ins[1:]:
        total += ref[...].astype(F32)
    total = total.astype(BF)
    width = outs[0].shape[1]
    for n, out in enumerate(outs[:3]):
        out[...] = total[n * width : (n + 1) * width].T
    outs[3][...] = total[3 * width :]


def last_kernel(len_ref, own_ref, got_ref, acts_ref, inv_ref, out_ref, in_ref, enc_ref):
    tokens, feat = out_ref.shape[1:]
    rows = 3 * tokens
    stat = stat_of(own_ref[rows:]) + stat_of(got_ref[rows:])
    stat = jnp.broadcast_to(stat, (128, tokens)).T[:, :1] / (NB * feat)
    total = [
        own_ref[n * tokens : (n + 1) * tokens].astype(F32)
        + got_ref[n * tokens : (n + 1) * tokens].astype(F32)
        for n in range(3)
    ]
    inv_rms = inv_ref[:, :1]
    dec = acts_ref[:tokens].astype(F32)
    out_ref[0] = (dec + total[1]).astype(BF)
    keep = lax.broadcasted_iota(jnp.int32, (tokens, feat), 0) < len_ref[0]
    masked = jnp.where(keep, acts_ref[tokens : 2 * tokens].astype(F32), 0.0)
    in_grad = masked + inv_rms * total[0] - dec * (inv_rms * inv_rms * stat)
    in_ref[0] = in_grad.astype(BF)
    erows = enc_ref.shape[1]
    for n in range(NB):
        enc_ref[0, :, n * feat : (n + 1) * feat] = total[2][n * erows : (n + 1) * erows].astype(BF)


def stack_pair(first, second):
    return call(pair_kernel, (first, second), [shape_of((2,) + first.shape)])[0]


def gather(block, acts):
    before, behind = send_z(block, 1), send_z(block, -1)
    low, high = send_y(block, 1), send_y(block, -1)
    other = send_mp(acts, 1, 0, 0)
    other, again = after((other, block), low, high)
    pair_acts = stack_pair(acts, other)
    next_acts = send_x(pair_acts, 1)
    across = send_y(again, 2)

    pair_acts, next_acts, far, before, behind = after(
        (pair_acts, next_acts, block, before, behind), across
    )
    quad = stack_pair(pair_acts, next_acts)
    far_quad = send_x(quad, 2)
    pair = stack_pair(before, behind)
    pair_low, pair_high = send_y(pair, 1), send_y(pair, -1)
    far = send_z(far, 2)

    pair_low, pair_high, far = after((pair_low, pair_high, far))
    to_low, to_high = call(pick_kernel, (pair_low, pair_high), [shape_of(block.shape)] * 2)
    across_b, across_a = send_y(to_low, 1), send_y(to_high, -1)
    f_low, f_high = send_y(far, 1), send_y(far, -1)

    quad, far_quad, f_low, f_high = after((quad, far_quad, f_low, f_high), across_a, across_b)
    pieces = [quad, far_quad, send_mp(quad, 0, 0, 1), send_mp(far_quad, 0, 0, 1)]
    half = shape_of((block.shape[0] // 2, block.shape[1]))
    to_low, to_high = call(halves_kernel, (f_low, f_high), [half] * 2)
    last_low, last_high = send_y(to_low, 1), send_y(to_high, -1)
    return (
        (block, high, low, across),
        (pair, pair_high, pair_low, across_b, across_a),
        (far, f_high, f_low, last_low, last_high),
        pieces,
    )


CHUNK = 128


def summed(out, put, *terms):
    def body(step, carry):
        rows = pl.ds(pl.multiple_of(step * CHUNK, CHUNK), CHUNK)
        total = terms[0](rows).astype(F32)
        for term in terms[1:]:
            total += term(rows).astype(F32)
        put(out, rows, total.astype(BF))
        return carry

    lax.fori_loop(0, out.shape[-2] // CHUNK, body, 0)


def plain(ref):
    return lambda rows: ref[rows, :]


def of(ref, n):
    return lambda rows: ref[n, rows, :]


def put_plain(out, rows, value):
    out[rows, :] = value


def put_at(n):
    def put(out, rows, value):
        out[n, rows, :] = value

    return put


def far_kernel_sum(far1, far3, low, high, out1, out3):
    half = low.shape[0]
    for ref, part, out, first in ((far1, low, out1, 0), (far3, high, out3, half)):
        for begin in range(0, 2 * half, CHUNK):
            rows = slice(begin, begin + CHUNK)
            if first <= begin < first + half:
                other = part[begin - first : begin - first + CHUNK].astype(F32)
                out[rows] = (ref[rows].astype(F32) + other).astype(BF)
            else:
                out[rows] = ref[rows]


def second_sum_kernel(far0, far1, far3, bf1, bf2, bf3, bh1, bh2, bh3, up, down, far):
    summed(up, put_at(0), plain(bf1), plain(bf2))
    summed(up, put_at(1), plain(bh1))
    summed(down, put_at(0), plain(bf3))
    summed(down, put_at(1), plain(bh3), plain(bh2))
    summed(far, put_plain, plain(far0), plain(far1), plain(far3))


def third_sum_kernel(bf0, bh0, up, down, before, behind):
    summed(before, put_plain, plain(bf0), of(up, 0), of(down, 0))
    summed(behind, put_plain, plain(bh0), of(up, 1), of(down, 1))


def scatter(grads, partials):
    far0, far1, far2_low, far2_high, far3 = grads(2, ())
    full = shape_of(far0.shape)
    pair = shape_of((2,) + far0.shape)
    far2_low, far2_high = send_y(far2_low, 1), send_y(far2_high, -1)
    bf0, bf1, bf2, bf3 = grads(1, (far0,))
    bh0, bh1, bh2, bh3 = grads(3, (bf0,))
    keep, send = partials((bh0,))

    far2_low, far2_high, bf2, bh2, send = after((far2_low, far2_high, bf2, bh2, send))
    bf2, bh2 = send_y(bf2, 1), send_y(bh2, -1)
    far1, far3 = call(far_kernel_sum, (far1, far3, far2_low, far2_high), [full] * 2)
    far1, far3 = send_y(far1, 1), send_y(far3, -1)
    core = send_mp(send, 0, 0, 1)
    part = shape_of((2,) + keep.shape[1:])
    near_x, far_x = call(core_sum_kernel, (keep, core), [part] * 2, moved=9 * MIB)
    far_x = send_x(far_x, 2)
    own0, own1, own2, own3 = grads(0, (core,))

    far1, far3, bf2, bh2 = after((far1, far3, bf2, bh2), own0)
    up, down, far = call(
        second_sum_kernel, (far0, far1, far3, bf1, bf2, bf3, bh1, bh2, bh3), [pair, pair, full]
    )
    up, down, far = send_y(up, 1), send_y(down, -1), send_z(far, 2)
    part = shape_of(keep.shape[1:])
    near_x, next_x = call(split_sum_kernel, (near_x, far_x), [part] * 2, moved=6 * MIB)
    next_x = send_x(next_x, 1)

    up, down, far, own1, own2, own3 = after((up, down, far, own1, own2, own3))
    before, behind = call(third_sum_kernel, (bf0, bh0, up, down), [full] * 2)
    own2 = send_y(own2, 2)
    own1, own3 = send_y(own1, 1), send_y(own3, -1)
    before, behind = send_z(before, 1), send_z(behind, -1)
    part = shape_of(keep.shape[2:])
    own, other = call(split_sum_kernel, (near_x, next_x), [part] * 2, moved=4 * MIB)
    return (own0, far, own1, own2, own3, before, behind), (own, send_mp(other, 1, 0, 0))


def local(
    dec_input,
    enc_output,
    query_weight,
    key_weight,
    value_weight,
    output_weight,
    cotangent,
    enc_lengths,
    dec_lengths,
):
    tokens, feat = dec_input.shape[1:]
    width = query_weight.shape[1]
    erows = enc_output.shape[1]
    keys = erows * NB
    scale = width ** (-0.5)
    unit = 2 * tokens * feat * width

    hbm = pl.BlockSpec(memory_space=pltpu.HBM)
    vmem = pl.BlockSpec(memory_space=pltpu.VMEM)
    weights, acts = pl.pallas_call(
        assemble_kernel,
        in_specs=[hbm] * 7,
        out_specs=[vmem] * 2,
        out_shape=[shape_of((feat, 4 * width)), shape_of((2 * tokens + keys, feat))],
        scratch_shapes=[
            pltpu.VMEM((width, feat), BF), pltpu.VMEM((erows, NB * feat), BF),
            pltpu.SemaphoreType.DMA((7,)),
        ],
        compiler_params=pltpu.CompilerParams(vmem_limit_bytes=56 * MIB),
    )(query_weight, key_weight, value_weight, output_weight, dec_input, cotangent, enc_output)
    own_group, near_group, far_group, pieces = gather(weights, acts)

    normed, masked, encoded, inv_rms = call(
        prepare_kernel, pieces,
        [
            shape_of((NB, tokens, feat)), shape_of((NB, tokens, feat)),
            shape_of((NB, keys, feat)), shape_of((tokens, 128), F32),
        ],
        (dec_lengths,), moved=12 * MIB,
    )
    stacked = (normed, masked, encoded)
    acc_shape = shape_of((4, tokens, width), F32)
    stack_shape = shape_of((4, feat, 4 * width))
    acc, own_stack = call(
        own_kernel, (*stacked, *own_group), [acc_shape, stack_shape],
        flops=16 * unit, moved=4 * MIB,
    )
    acc, near_stack = call(
        near_kernel, (*stacked, *near_group, acc),
        [acc_shape, shape_of((8, feat, 4 * width))], flops=32 * unit, moved=8 * MIB,
    )
    tshape, kshape = shape_of((tokens, width)), shape_of((keys, 2 * width))
    q_grad, kv_grad, attended, q_t, kv_t, at_t, stat, far_stack = call(
        functools.partial(far_kernel, scale), (*stacked, *far_group, acc),
        [
            tshape, kshape, tshape, shape_of((width, tokens)), shape_of((2 * width, keys)),
            shape_of((width, tokens)), shape_of((EXTRA, tokens)), stack_shape,
        ],
        (enc_lengths,), flops=24 * unit, moved=4 * MIB,
    )

    def grads(dz, others):
        (normed_in,) = after((normed,), *others) if others else (normed,)
        full, part = shape_of((4 * width, feat)), shape_of((2 * width, feat))
        outs = [full, full, part, part, full] if dz == 2 else [full] * 4
        return call(
            functools.partial(weight_grad_kernel, dz), (normed_in, masked, encoded, q_t, kv_t, at_t),
            outs, flops=16 * unit, moved=4 * MIB,
        )

    def partials(others):
        (q_in,) = after((q_grad,), *others)
        out = shape_of((4, 2, 3 * tokens + EXTRA, feat))
        return call(
            partial_kernel, (q_in, kv_grad, attended, stat, own_stack, near_stack, far_stack),
            [out, out], scratch=[pltpu.VMEM((keys, feat), BF)], flops=64 * unit, moved=14 * MIB,
        )

    shares, (line, got) = scatter(grads, partials)
    query_grad, key_grad, value_grad, output_grad = call_out(
        share_kernel, shares, [shape_of((feat, width))] * 4
    )
    stack = shape_of((1, tokens, feat))
    layer_out, input_grad, enc_grad = call_out(
        last_kernel, (line, got, acts, inv_rms),
        [stack, stack, shape_of((1, erows, NB * feat))], (dec_lengths,),
    )
    return (layer_out, input_grad, enc_grad, query_grad, key_grad, value_grad, output_grad)


def solution(mesh):
    in_specs = (
        P("dp", None, "mp"),
        P("dp", "mp", None),
        P("dp", "mp"),
        P("dp", "mp"),
        P("dp", "mp"),
        P("mp", "dp"),
        P("dp", None, "mp"),
        P("dp"),
        P("dp"),
    )
    out_specs = (
        P("dp", None, "mp"),
        P("dp", None, "mp"),
        P("dp", "mp", None),
        P("dp", "mp"),
        P("dp", "mp"),
        P("dp", "mp"),
        P("mp", "dp"),
    )
    return jax.shard_map(local, mesh=mesh, in_specs=in_specs, out_specs=out_specs, check_vma=False)
```

time: 775 us -> 235 us (0.30)
  waiting for transfers between devices: 708 us -> 113 us
  starting transfers between devices: 0.61 us -> 95 us
  matrix products: 27.7 us -> 0 us
  Pallas kernels: 0 us -> 23.8 us
  other arithmetic: 15 us -> 0 us
  between operations: 15.4 us -> 2.37 us
    all_gather x7 -> x0, waiting for transfers between devices: 352 us -> none  [the longest x1 61 us: local(): lax.all_gather(key_weight, 'dp', axis=0, tiled=True)]
    reduce_scatter x3 -> x0, waiting for transfers between devices: 246 us -> none  [the longest x1 123 us: local(): lax.psum_scatter(jnp.concatenate([jnp.dot(normed.T, q_grad, preferred_ele...]
    ppermute x0 -> x37, waiting for transfers between devices: none -> 113 us  [the longest x6 51.9 us: send_z(): lax.ppermute(value, 'dp', [(dp_index(y, z), dp_index(y, z + d)) for y, z...]
    psum x1 -> x0, waiting for transfers between devices: 105 us -> none  [local(): lax.psum(normed_part.astype(jnp.bfloat16), 'mp').astype(jnp.float32)]
    ppermute x0 -> x37, starting transfers between devices: none -> 95 us  [the longest x6 36.3 us: send_z(): lax.ppermute(value, 'dp', [(dp_index(y, z), dp_index(y, z + d)) for y, z...]
    dot_general x18 -> x0, matrix products: 27.7 us -> none  [the longest x1 3.67 us: local(): jnp.dot(attended, output_full, preferred_element_type=jnp.float32)]
    pallas_call x0 -> x23, Pallas kernels: none -> 23.8 us  [the longest x20 19.4 us: call(): pl.pallas_call(kernel, in_specs=[pl.BlockSpec(memory_space=pltpu.SMEM)] *...]
  transfers between devices with their start and end apart: 11 -> 37, of which waited for: 11 -> 18; matrix products, arithmetic and copies ran while one was open for 5% -> 0% of each run, Pallas kernels for 0% -> 7%
where the time goes in v2:
time: 235 us
  waiting for transfers between devices  113 us (48%)
  starting transfers between devices  95 us (40%)
  Pallas kernels  23.8 us (10%)
  between operations  2.37 us (1%)
    ppermute x6, waiting for transfers between devices, send_z(): lax.ppermute(value, 'dp', [(dp_index(y, z), dp_index(y, z + d)) for y, z...  51.9 us
    ppermute x22, waiting for transfers between devices, send_y(): lax.ppermute(value, 'dp', [(dp_index(y, z), dp_index(y + d, z)) for y, z...  38.9 us
    ppermute x6, starting transfers between devices, send_z(): lax.ppermute(value, 'dp', [(dp_index(y, z), dp_index(y, z + d)) for y, z...  36.3 us
    ppermute x5, starting transfers between devices, send_mp(): return lax.ppermute(value, 'mp', pairs)  27 us
    ppermute x22, starting transfers between devices, send_y(): lax.ppermute(value, 'dp', [(dp_index(y, z), dp_index(y + d, z)) for y, z...  26.9 us
    ppermute x5, waiting for transfers between devices, send_mp(): return lax.ppermute(value, 'mp', pairs)  22.1 us
    pallas_call x20, Pallas kernels, call(): pl.pallas_call(kernel, in_specs=[pl.BlockSpec(memory_space=pltpu.SMEM)] *...  19.4 us
    ppermute x4, starting transfers between devices, send_x(): return lax.ppermute(value, 'mp', pairs)  4.78 us
  transfers between devices with their start and end apart: 37, of which 18 were waited for; matrix products, arithmetic and copies ran while one was open for 0% of the time, Pallas kernels for 7%

profile of v2, /device:TPU:1, one launch (start us, length us, event | category | flops | bytes accessed | tf_op | source)
XLA Modules:
  0.0 235.1 jit_solution(5270105054912759682)
XLA Ops:
  2.9 3.6 %collective-permute-start.1 = (bf16[256,1024]{1,0:T(8,128)(2,1)}, bf16[256,1024]{1,0:T(8,128)(2,1)S(1)}, u32[]{:S(2)}, u32[]{:S(2)}) collective-permute-start(bf16[256,1024]{1,0:T(8,128)(2,1)} %get-tuple-element.107.refs_0_), channel_id=1, source_target_pairs={{0,192},{16,208},{32,224},{48,240},{64,0},{80,16},{96,32},{112,48}... | collective-permute-start | bytes 1572872 | tf_op jit(solution)/shard_map/ppermute | solution.py:30
  8.2 7.8 %collective-permute-done.2.second = bf16[768,256]{1,0:T(8,128)(2,1)S(1)} collective-permute-done((bf16[768,256]{1,0:T(8,128)(2,1)}, bf16[768,256]{1,0:T(8,128)(2,1)S(1)}, u32[]{:S(2)}, u32[]{:S(2)}) %collective-permute-start.2) | collective-permute-done | bytes 393248 | tf_op jit(solution)/shard_map/ppermute | solution.py:39
  17.4 3.0 %collective-permute-done.refs_2_ = bf16[256,1024]{1,0:T(8,128)(2,1)S(1)} collective-permute-done((bf16[256,1024]{1,0:T(8,128)(2,1)}, bf16[256,1024]{1,0:T(8,128)(2,1)S(1)}, u32[]{:S(2)}, u32[]{:S(2)}) %collective-permute-start) | collective-permute-done | bytes 524320 | tf_op jit(solution)/shard_map/ppermute | solution.py:30
  22.8 6.0 %collective-permute-start.6 = (bf16[256,1024]{1,0:T(8,128)(2,1)}, bf16[256,1024]{1,0:T(8,128)(2,1)S(1)}, u32[]{:S(2)}, u32[]{:S(2)}) collective-permute-start(bf16[256,1024]{1,0:T(8,128)(2,1)} %get-tuple-element.107.refs_0_), channel_id=1, source_target_pairs={{0,48},{16,0},{32,16},{48,32},{64,112},{80,64},{96,80},{112,96},{1... | collective-permute-start | bytes 1572872 | tf_op jit(solution)/shard_map/ppermute | solution.py:34
  28.8 19.7 %collective-permute-done.6.second = bf16[256,1024]{1,0:T(8,128)(2,1)S(1)} collective-permute-done((bf16[256,1024]{1,0:T(8,128)(2,1)}, bf16[256,1024]{1,0:T(8,128)(2,1)S(1)}, u32[]{:S(2)}, u32[]{:S(2)}) %collective-permute-start.6) | collective-permute-done | bytes 524320 | tf_op jit(solution)/shard_map/ppermute | solution.py:34
  52.8 5.9 %collective-permute-start.9 = (bf16[256,1024]{1,0:T(8,128)(2,1)S(1)}, bf16[256,1024]{1,0:T(8,128)(2,1)S(1)}, u32[]{:S(2)}, u32[]{:S(2)}) collective-permute-start(bf16[256,1024]{1,0:T(8,128)(2,1)S(1)} %copy-done.2), channel_id=1, source_target_pairs={{0,32},{16,48},{32,0},{48,16},{64,96},{80,112},{96,64},{112,80},{1... | collective-permute-start | bytes 1572872 | tf_op jit(solution)/shard_map/ppermute | solution.py:34
  58.7 13.3 %collective-permute-done.9.refs_0_ = bf16[256,1024]{1,0:T(8,128)(2,1)S(1)} collective-permute-done((bf16[256,1024]{1,0:T(8,128)(2,1)S(1)}, bf16[256,1024]{1,0:T(8,128)(2,1)S(1)}, u32[]{:S(2)}, u32[]{:S(2)}) %collective-permute-start.9) | collective-permute-done | bytes 524320 | tf_op jit(solution)/shard_map/ppermute | solution.py:34
  74.3 2.8 %collective-permute-start.10 = (bf16[256,1024]{1,0:T(8,128)(2,1)S(1)}, bf16[256,1024]{1,0:T(8,128)(2,1)S(1)}, u32[]{:S(2)}, u32[]{:S(2)}) collective-permute-start(bf16[256,1024]{1,0:T(8,128)(2,1)S(1)} %get-tuple-element.110), channel_id=1, source_target_pairs={{0,192},{16,208},{32,224},{48,240},{64,0},{80,16},{96,32},{112,48}... | collective-permute-start | bytes 1572872 | tf_op jit(solution)/shard_map/ppermute | solution.py:30
  77.0 3.3 %collective-permute-done.14.second.refs_1_ = bf16[256,1024]{1,0:T(8,128)(2,1)S(1)} collective-permute-done((bf16[256,1024]{1,0:T(8,128)(2,1)S(1)}, bf16[256,1024]{1,0:T(8,128)(2,1)S(1)}, u32[]{:S(2)}, u32[]{:S(2)}) %collective-permute-start.14) | collective-permute-done | bytes 524320 | tf_op jit(solution)/shard_map/ppermute | solution.py:30
  80.3 3.4 %collective-permute-done.13.first.refs_2_ = bf16[256,1024]{1,0:T(8,128)(2,1)S(1)} collective-permute-done((bf16[256,1024]{1,0:T(8,128)(2,1)S(1)}, bf16[256,1024]{1,0:T(8,128)(2,1)S(1)}, u32[]{:S(2)}, u32[]{:S(2)}) %collective-permute-start.13) | collective-permute-done | bytes 524320 | tf_op jit(solution)/shard_map/ppermute | solution.py:30
  83.7 3.2 %collective-permute-done.10.refs_4_ = bf16[256,1024]{1,0:T(8,128)(2,1)S(1)} collective-permute-done((bf16[256,1024]{1,0:T(8,128)(2,1)S(1)}, bf16[256,1024]{1,0:T(8,128)(2,1)S(1)}, u32[]{:S(2)}, u32[]{:S(2)}) %collective-permute-start.10) | collective-permute-done | bytes 524320 | tf_op jit(solution)/shard_map/ppermute | solution.py:30
  87.0 3.1 %collective-permute-done.11.refs_3_ = bf16[256,1024]{1,0:T(8,128)(2,1)S(1)} collective-permute-done((bf16[256,1024]{1,0:T(8,128)(2,1)S(1)}, bf16[256,1024]{1,0:T(8,128)(2,1)S(1)}, u32[]{:S(2)}, u32[]{:S(2)}) %collective-permute-start.11) | collective-permute-done | bytes 524320 | tf_op jit(solution)/shard_map/ppermute | solution.py:30
  90.1 10.9 %collective-permute-start.15 = (bf16[2,2,768,256]{3,2,1,0:T(8,128)(2,1)S(1)}, bf16[2,2,768,256]{3,2,1,0:T(8,128)(2,1)S(1)}, u32[]{:S(2)}, u32[]{:S(2)}) collective-permute-start(bf16[2,2,768,256]{3,2,1,0:T(8,128)(2,1)S(1)} %shard_map.148.refs_0_), channel_id=1, source_target_pairs={{0,1},{1,0},{2,3},{3,2},{4,5},{5,4},{6,7},{7,6},{8,9},{9,8},{10,11... | collective-permute-start | bytes 4718600 | tf_op jit(solution)/shard_map/ppermute | solution.py:39
  106.3 3.6 %shard_map.149 = (bf16[16,256,256]{2,1,0:T(8,128)(2,1)S(1)}, bf16[16,256,256]{2,1,0:T(8,128)(2,1)S(1)}, bf16[16,256,256]{2,1,0:T(8,128)(2,1)S(1)}, f32[256,128]{1,0:T(8,128)S(1)}) custom-call(s32[1]{0:T(128)S(6)} %copy.17.len_ref.refs_0_, bf16[2,2,768,256]{3,2,1,0:T(8,128)(2,1)S(1)} %shard_map.148.refs_0_, ...), custom_call_target="tpu_custom_call" | custom-call | bytes 12582912 | tf_op jit(solution)/shard_map/pallas_call | solution.py:65
  118.5 5.9 %shard_map.157 = (bf16[4,2,784,256]{3,2,1,0:T(8,128)(2,1)S(1)}, bf16[4,2,784,256]{3,2,1,0:T(8,128)(2,1)S(1)}) custom-call(bf16[256,256]{1,0:T(8,128)(2,1)S(1)} %get-tuple-element.135.qg_ref, bf16[256,512]{1,0:T(8,128)(2,1)S(1)} %get-tuple-element.136.kv_ref, bf16[256,256]{1,0:T(8,128)(2,1)S(1)} %get-tuple-element.137.at_ref, ...), custom_call_target="tpu_custom_call" | custom-call | flops 34359738368 | bytes 14680064 | tf_op jit(solution)/shard_map/pallas_call | solution.py:65
  125.6 5.4 %collective-permute-done.21.got_ref = bf16[4,2,784,256]{3,2,1,0:T(8,128)(2,1)S(1)} collective-permute-done((bf16[4,2,784,256]{3,2,1,0:T(8,128)(2,1)S(1)}, bf16[4,2,784,256]{3,2,1,0:T(8,128)(2,1)S(1)}, u32[]{:S(2)}, u32[]{:S(2)}) %collective-permute-start.21) | collective-permute-done | bytes 3211296 | tf_op jit(solution)/shard_map/ppermute | solution.py:39
  138.9 7.9 %collective-permute-done.25.far1 = bf16[1024,256]{1,0:T(8,128)(2,1)S(1)} collective-permute-done((bf16[1024,256]{1,0:T(8,128)(2,1)S(1)}, bf16[1024,256]{1,0:T(8,128)(2,1)S(1)}, u32[]{:S(2)}, u32[]{:S(2)}) %collective-permute-start.25) | collective-permute-done | bytes 524320 | tf_op jit(solution)/shard_map/ppermute | solution.py:30
  146.9 11.2 %collective-permute-done.27.bf2 = bf16[1024,256]{1,0:T(8,128)(2,1)S(1)} collective-permute-done((bf16[1024,256]{1,0:T(8,128)(2,1)S(1)}, bf16[1024,256]{1,0:T(8,128)(2,1)S(1)}, u32[]{:S(2)}, u32[]{:S(2)}) %collective-permute-start.27) | collective-permute-done | bytes 524320 | tf_op jit(solution)/shard_map/ppermute | solution.py:30
  161.5 8.9 %collective-permute-start.31 = (bf16[1024,256]{1,0:T(8,128)(2,1)S(1)}, bf16[1024,256]{1,0:T(8,128)(2,1)S(1)}, u32[]{:S(2)}, u32[]{:S(2)}) collective-permute-start(bf16[1024,256]{1,0:T(8,128)(2,1)S(1)} %get-tuple-element.179), channel_id=1, source_target_pairs={{0,32},{16,48},{32,0},{48,16},{64,96},{80,112},{96,64},{112,80},{1... | collective-permute-start | bytes 1572872 | tf_op jit(solution)/shard_map/ppermute | solution.py:34
  171.2 9.8 %collective-permute-done.31.refs_1_ = bf16[1024,256]{1,0:T(8,128)(2,1)S(1)} collective-permute-done((bf16[1024,256]{1,0:T(8,128)(2,1)S(1)}, bf16[1024,256]{1,0:T(8,128)(2,1)S(1)}, u32[]{:S(2)}, u32[]{:S(2)}) %collective-permute-start.31) | collective-permute-done | bytes 524320 | tf_op jit(solution)/shard_map/ppermute | solution.py:34
  183.6 12.8 %collective-permute-start.35 = (bf16[1024,256]{1,0:T(8,128)(2,1)S(1)}, bf16[1024,256]{1,0:T(8,128)(2,1)S(1)}, u32[]{:S(2)}, u32[]{:S(2)}) collective-permute-start(bf16[1024,256]{1,0:T(8,128)(2,1)S(1)} %get-tuple-element.189), channel_id=1, source_target_pairs={{0,16},{16,32},{32,48},{48,0},{64,80},{80,96},{96,112},{112,64},{1... | collective-permute-start | bytes 1572872 | tf_op jit(solution)/shard_map/ppermute | solution.py:34
  202.3 9.1 %collective-permute-done.35.refs_5_ = bf16[1024,256]{1,0:T(8,128)(2,1)S(1)} collective-permute-done((bf16[1024,256]{1,0:T(8,128)(2,1)S(1)}, bf16[1024,256]{1,0:T(8,128)(2,1)S(1)}, u32[]{:S(2)}, u32[]{:S(2)}) %collective-permute-start.35) | collective-permute-done | bytes 524320 | tf_op jit(solution)/shard_map/ppermute | solution.py:34
  211.4 13.4 %collective-permute-start.24 = (bf16[784,256]{1,0:T(8,128)(2,1)S(1)}, bf16[784,256]{1,0:T(8,128)(2,1)S(1)}, u32[]{:S(2)}, u32[]{:S(2)}) collective-permute-start(bf16[784,256]{1,0:T(8,128)(2,1)S(1)} %get-tuple-element.154), channel_id=1, source_target_pairs={{0,8},{1,9},{2,10},{3,11},{4,12},{5,13},{6,14},{7,15},{8,0},{9,1},... | collective-permute-start | bytes 1204232 | tf_op jit(solution)/shard_map/ppermute | solution.py:39
  226.1 7.9 %collective-permute-done.24.refs_2_ = bf16[784,256]{1,0:T(8,128)(2,1)S(1)} collective-permute-done((bf16[784,256]{1,0:T(8,128)(2,1)S(1)}, bf16[784,256]{1,0:T(8,128)(2,1)S(1)}, u32[]{:S(2)}, u32[]{:S(2)}) %collective-permute-start.24) | collective-permute-done | bytes 401440 | tf_op jit(solution)/shard_map/ppermute | solution.py:39
  (79 shorter events, 50.8 us)
Async XLA Ops:
  2.9 14.5 %collective-permute-start.1 = (bf16[256,1024]{1,0:T(8,128)(2,1)}, bf16[256,1024]{1,0:T(8,128)(2,1)S(1)}, u32[]{:S(2)}, u32[]{:S(2)}) collective-permute-start(bf16[256,1024]{1,0:T(8,128)(2,1)} %get-tuple-element.107.refs_0_), channel_id=1, source_target_pairs={{0,192},{16,208},{32,224},{48,240},{64,0},{80,16},{96,32},{112,48}... | collective-permute-start | bytes 1572872 | tf_op jit(solution)/shard_map/ppermute | solution.py:30
  21.5 27.0 %collective-permute-start.4 = (bf16[2,768,256]{2,1,0:T(8,128)(2,1)S(1)}, bf16[2,768,256]{2,1,0:T(8,128)(2,1)S(1)}, u32[]{:S(2)}, u32[]{:S(2)}) collective-permute-start(bf16[2,768,256]{2,1,0:T(8,128)(2,1)S(1)} %shard_map.145.first), channel_id=1, source_target_pairs={{0,2},{1,3},{2,0},{3,1},{4,6},{5,7},{6,4},{7,5},{8,10},{9,11},{10,... | collective-permute-start | bytes 2359304 | tf_op jit(solution)/shard_map/ppermute | solution.py:44
  22.8 25.7 %collective-permute-start.6 = (bf16[256,1024]{1,0:T(8,128)(2,1)}, bf16[256,1024]{1,0:T(8,128)(2,1)S(1)}, u32[]{:S(2)}, u32[]{:S(2)}) collective-permute-start(bf16[256,1024]{1,0:T(8,128)(2,1)} %get-tuple-element.107.refs_0_), channel_id=1, source_target_pairs={{0,48},{16,0},{32,16},{48,32},{64,112},{80,64},{96,80},{112,96},{1... | collective-permute-start | bytes 1572872 | tf_op jit(solution)/shard_map/ppermute | solution.py:34
  28.8 19.7 %collective-permute-start.5 = (bf16[256,1024]{1,0:T(8,128)(2,1)}, bf16[256,1024]{1,0:T(8,128)(2,1)S(1)}, u32[]{:S(2)}, u32[]{:S(2)}) collective-permute-start(bf16[256,1024]{1,0:T(8,128)(2,1)} %get-tuple-element.107.refs_0_), channel_id=1, source_target_pairs={{0,16},{16,32},{32,48},{48,0},{64,80},{80,96},{96,112},{112,64},{1... | collective-permute-start | bytes 1572872 | tf_op jit(solution)/shard_map/ppermute | solution.py:34
  28.8 19.7 %collective-permute-start.3 = (bf16[256,1024]{1,0:T(8,128)(2,1)}, bf16[256,1024]{1,0:T(8,128)(2,1)S(1)}, u32[]{:S(2)}, u32[]{:S(2)}) collective-permute-start(bf16[256,1024]{1,0:T(8,128)(2,1)} %get-tuple-element.107.refs_0_), channel_id=1, source_target_pairs={{0,128},{16,144},{32,160},{48,176},{64,192},{80,208},{96,224},{112... | collective-permute-start | bytes 1572872 | tf_op jit(solution)/shard_map/ppermute | solution.py:30
  48.6 23.4 %collective-permute-start.8 = (bf16[2,256,1024]{2,1,0:T(8,128)(2,1)S(1)}, bf16[2,256,1024]{2,1,0:T(8,128)(2,1)S(1)}, u32[]{:S(2)}, u32[]{:S(2)}) collective-permute-start(bf16[2,256,1024]{2,1,0:T(8,128)(2,1)S(1)} %shard_map.146.refs_0_), channel_id=1, source_target_pairs={{0,192},{16,208},{32,224},{48,240},{64,0},{80,16},{96,32},{112,48}... | collective-permute-start | bytes 3145736 | tf_op jit(solution)/shard_map/ppermute | solution.py:30
  49.0 23.0 %collective-permute-start.7 = (bf16[2,256,1024]{2,1,0:T(8,128)(2,1)S(1)}, bf16[2,256,1024]{2,1,0:T(8,128)(2,1)S(1)}, u32[]{:S(2)}, u32[]{:S(2)}) collective-permute-start(bf16[2,256,1024]{2,1,0:T(8,128)(2,1)S(1)} %shard_map.146.refs_0_), channel_id=1, source_target_pairs={{0,64},{16,80},{32,96},{48,112},{64,128},{80,144},{96,160},{112,17... | collective-permute-start | bytes 3145736 | tf_op jit(solution)/shard_map/ppermute | solution.py:30
  50.2 39.8 %collective-permute-start.12 = (bf16[2,2,768,256]{3,2,1,0:T(8,128)(2,1)S(1)}, bf16[2,2,768,256]{3,2,1,0:T(8,128)(2,1)S(1)}, u32[]{:S(2)}, u32[]{:S(2)}) collective-permute-start(bf16[2,2,768,256]{3,2,1,0:T(8,128)(2,1)S(1)} %shard_map.148.refs_0_), channel_id=1, source_target_pairs={{0,4},{1,5},{2,6},{3,7},{4,0},{5,1},{6,2},{7,3},{8,12},{9,13},{10,... | collective-permute-start | bytes 4718600 | tf_op jit(solution)/shard_map/ppermute | solution.py:44
  52.8 19.2 %collective-permute-start.9 = (bf16[256,1024]{1,0:T(8,128)(2,1)S(1)}, bf16[256,1024]{1,0:T(8,128)(2,1)S(1)}, u32[]{:S(2)}, u32[]{:S(2)}) collective-permute-start(bf16[256,1024]{1,0:T(8,128)(2,1)S(1)} %copy-done.2), channel_id=1, source_target_pairs={{0,32},{16,48},{32,0},{48,16},{64,96},{80,112},{96,64},{112,80},{1... | collective-permute-start | bytes 1572872 | tf_op jit(solution)/shard_map/ppermute | solution.py:34
  90.1 15.2 %collective-permute-start.15 = (bf16[2,2,768,256]{3,2,1,0:T(8,128)(2,1)S(1)}, bf16[2,2,768,256]{3,2,1,0:T(8,128)(2,1)S(1)}, u32[]{:S(2)}, u32[]{:S(2)}) collective-permute-start(bf16[2,2,768,256]{3,2,1,0:T(8,128)(2,1)S(1)} %shard_map.148.refs_0_), channel_id=1, source_target_pairs={{0,1},{1,0},{2,3},{3,2},{4,5},{5,4},{6,7},{7,6},{8,9},{9,8},{10,11... | collective-permute-start | bytes 4718600 | tf_op jit(solution)/shard_map/ppermute | solution.py:39
  132.0 38.3 %collective-permute-start.22 = (bf16[2,2,784,256]{3,2,1,0:T(8,128)(2,1)S(1)}, bf16[2,2,784,256]{3,2,1,0:T(8,128)(2,1)S(1)}, u32[]{:S(2)}, u32[]{:S(2)}) collective-permute-start(bf16[2,2,784,256]{3,2,1,0:T(8,128)(2,1)S(1)} %get-tuple-element.150), channel_id=1, source_target_pairs={{0,4},{1,5},{2,6},{3,7},{4,0},{5,1},{6,2},{7,3},{8,12},{9,13},{10,... | collective-permute-start | bytes 4816904 | tf_op jit(solution)/shard_map/ppermute | solution.py:44
  132.7 14.1 %collective-permute-start.25 = (bf16[1024,256]{1,0:T(8,128)(2,1)S(1)}, bf16[1024,256]{1,0:T(8,128)(2,1)S(1)}, u32[]{:S(2)}, u32[]{:S(2)}) collective-permute-start(bf16[1024,256]{1,0:T(8,128)(2,1)S(1)} %get-tuple-element.165), channel_id=1, source_target_pairs={{0,64},{16,80},{32,96},{48,112},{64,128},{80,144},{96,160},{112,17... | collective-permute-start | bytes 1572872 | tf_op jit(solution)/shard_map/ppermute | solution.py:30
  135.5 22.6 %collective-permute-start.27 = (bf16[1024,256]{1,0:T(8,128)(2,1)S(1)}, bf16[1024,256]{1,0:T(8,128)(2,1)S(1)}, u32[]{:S(2)}, u32[]{:S(2)}) collective-permute-start(bf16[1024,256]{1,0:T(8,128)(2,1)S(1)} %get-tuple-element.167), channel_id=1, source_target_pairs={{0,64},{16,80},{32,96},{48,112},{64,128},{80,144},{96,160},{112,17... | collective-permute-start | bytes 1572872 | tf_op jit(solution)/shard_map/ppermute | solution.py:30
  135.5 22.6 %collective-permute-start.28 = (bf16[1024,256]{1,0:T(8,128)(2,1)S(1)}, bf16[1024,256]{1,0:T(8,128)(2,1)S(1)}, u32[]{:S(2)}, u32[]{:S(2)}) collective-permute-start(bf16[1024,256]{1,0:T(8,128)(2,1)S(1)} %get-tuple-element.168), channel_id=1, source_target_pairs={{0,192},{16,208},{32,224},{48,240},{64,0},{80,16},{96,32},{112,48}... | collective-permute-start | bytes 1572872 | tf_op jit(solution)/shard_map/ppermute | solution.py:30
  158.7 24.4 %collective-permute-start.29 = (bf16[2,1024,256]{2,1,0:T(8,128)(2,1)S(1)}, bf16[2,1024,256]{2,1,0:T(8,128)(2,1)S(1)}, u32[]{:S(2)}, u32[]{:S(2)}) collective-permute-start(bf16[2,1024,256]{2,1,0:T(8,128)(2,1)S(1)} %get-tuple-element.177), channel_id=1, source_target_pairs={{0,64},{16,80},{32,96},{48,112},{64,128},{80,144},{96,160},{112,17... | collective-permute-start | bytes 3145736 | tf_op jit(solution)/shard_map/ppermute | solution.py:30
  158.8 24.3 %collective-permute-start.30 = (bf16[2,1024,256]{2,1,0:T(8,128)(2,1)S(1)}, bf16[2,1024,256]{2,1,0:T(8,128)(2,1)S(1)}, u32[]{:S(2)}, u32[]{:S(2)}) collective-permute-start(bf16[2,1024,256]{2,1,0:T(8,128)(2,1)S(1)} %get-tuple-element.178), channel_id=1, source_target_pairs={{0,192},{16,208},{32,224},{48,240},{64,0},{80,16},{96,32},{112,48}... | collective-permute-start | bytes 3145736 | tf_op jit(solution)/shard_map/ppermute | solution.py:30
  161.5 19.5 %collective-permute-start.31 = (bf16[1024,256]{1,0:T(8,128)(2,1)S(1)}, bf16[1024,256]{1,0:T(8,128)(2,1)S(1)}, u32[]{:S(2)}, u32[]{:S(2)}) collective-permute-start(bf16[1024,256]{1,0:T(8,128)(2,1)S(1)} %get-tuple-element.179), channel_id=1, source_target_pairs={{0,32},{16,48},{32,0},{48,16},{64,96},{80,112},{96,64},{112,80},{1... | collective-permute-start | bytes 1572872 | tf_op jit(solution)/shard_map/ppermute | solution.py:34
  170.8 30.6 %collective-permute-start.23 = (bf16[2,784,256]{2,1,0:T(8,128)(2,1)S(1)}, bf16[2,784,256]{2,1,0:T(8,128)(2,1)S(1)}, u32[]{:S(2)}, u32[]{:S(2)}) collective-permute-start(bf16[2,784,256]{2,1,0:T(8,128)(2,1)S(1)} %get-tuple-element.152), channel_id=1, source_target_pairs={{0,2},{1,3},{2,0},{3,1},{4,6},{5,7},{6,4},{7,5},{8,10},{9,11},{10,... | collective-permute-start | bytes 2408456 | tf_op jit(solution)/shard_map/ppermute | solution.py:44
  183.6 27.8 %collective-permute-start.35 = (bf16[1024,256]{1,0:T(8,128)(2,1)S(1)}, bf16[1024,256]{1,0:T(8,128)(2,1)S(1)}, u32[]{:S(2)}, u32[]{:S(2)}) collective-permute-start(bf16[1024,256]{1,0:T(8,128)(2,1)S(1)} %get-tuple-element.189), channel_id=1, source_target_pairs={{0,16},{16,32},{32,48},{48,0},{64,80},{80,96},{96,112},{112,64},{1... | collective-permute-start | bytes 1572872 | tf_op jit(solution)/shard_map/ppermute | solution.py:34
  196.4 28.4 %collective-permute-start.36 = (bf16[1024,256]{1,0:T(8,128)(2,1)S(1)}, bf16[1024,256]{1,0:T(8,128)(2,1)S(1)}, u32[]{:S(2)}, u32[]{:S(2)}) collective-permute-start(bf16[1024,256]{1,0:T(8,128)(2,1)S(1)} %get-tuple-element.190), channel_id=1, source_target_pairs={{0,48},{16,0},{32,16},{48,32},{64,112},{80,64},{96,80},{112,96},{1... | collective-permute-start | bytes 1572872 | tf_op jit(solution)/shard_map/ppermute | solution.py:34
  199.1 25.7 %collective-permute-start.32 = (bf16[1024,256]{1,0:T(8,128)(2,1)S(1)}, bf16[1024,256]{1,0:T(8,128)(2,1)S(1)}, u32[]{:S(2)}, u32[]{:S(2)}) collective-permute-start(bf16[1024,256]{1,0:T(8,128)(2,1)S(1)} %get-tuple-element.184), channel_id=1, source_target_pairs={{0,64},{16,80},{32,96},{48,112},{64,128},{80,144},{96,160},{112,17... | collective-permute-start | bytes 1572872 | tf_op jit(solution)/shard_map/ppermute | solution.py:30
  199.1 25.7 %collective-permute-start.33 = (bf16[1024,256]{1,0:T(8,128)(2,1)S(1)}, bf16[1024,256]{1,0:T(8,128)(2,1)S(1)}, u32[]{:S(2)}, u32[]{:S(2)}) collective-permute-start(bf16[1024,256]{1,0:T(8,128)(2,1)S(1)} %get-tuple-element.185), channel_id=1, source_target_pairs={{0,128},{16,144},{32,160},{48,176},{64,192},{80,208},{96,224},{112... | collective-permute-start | bytes 1572872 | tf_op jit(solution)/shard_map/ppermute | solution.py:30
  201.4 23.5 %collective-permute-start.34 = (bf16[1024,256]{1,0:T(8,128)(2,1)S(1)}, bf16[1024,256]{1,0:T(8,128)(2,1)S(1)}, u32[]{:S(2)}, u32[]{:S(2)}) collective-permute-start(bf16[1024,256]{1,0:T(8,128)(2,1)S(1)} %get-tuple-element.186), channel_id=1, source_target_pairs={{0,192},{16,208},{32,224},{48,240},{64,0},{80,16},{96,32},{112,48}... | collective-permute-start | bytes 1572872 | tf_op jit(solution)/shard_map/ppermute | solution.py:30
  211.4 22.6 %collective-permute-start.24 = (bf16[784,256]{1,0:T(8,128)(2,1)S(1)}, bf16[784,256]{1,0:T(8,128)(2,1)S(1)}, u32[]{:S(2)}, u32[]{:S(2)}) collective-permute-start(bf16[784,256]{1,0:T(8,128)(2,1)S(1)} %get-tuple-element.154), channel_id=1, source_target_pairs={{0,8},{1,9},{2,10},{3,11},{4,12},{5,13},{6,14},{7,15},{8,0},{9,1},... | collective-permute-start | bytes 1204232 | tf_op jit(solution)/shard_map/ppermute | solution.py:39
  (16 other events, 196.2 us)

commit v3 on v2

--- a/solution.py
+++ b/solution.py
@@ -158,34 +158,43 @@
     out_second[...] = second[1]
 
 
+def join_kernel(first, second, out_ref):
+    half = first.shape[0]
+    out_ref[:half] = first[...]
+    out_ref[half:] = second[...]
+
+
 def halves_kernel(first, second, out_first, out_second):
     half = out_first.shape[0]
     out_first[...] = first[:half]
     out_second[...] = second[half:]
 
 
-def prepare_kernel(len_ref, *refs):
-    pieces, (normed_ref, masked_ref, enc_ref, inv_ref) = refs[:4], refs[4:]
+def quad_kernel(*refs):
+    for n, ref in enumerate(refs[:4]):
+        refs[4][n] = ref[...]
+
+
+def prepare_kernel(len_ref, own_ref, other_ref, normed_ref, masked_ref, enc_ref, inv_ref):
     tokens, feat = normed_ref.shape[1:]
     erows = enc_ref.shape[1] // NB
     a, b, c = mp_place()
     square = jnp.zeros((tokens, 1), F32)
-    for piece in pieces:
+    for piece in (own_ref, other_ref):
 
         def add_squares(k, total, piece=piece):
             hidden = piece[lax.div(k, 2), lax.rem(k, 2), :tokens].astype(F32)
             return total + jnp.sum(hidden * hidden, axis=1, keepdims=True)
 
-        square = lax.fori_loop(0, 4, add_squares, square)
+        square = lax.fori_loop(0, 8, add_squares, square)
     inv_rms = lax.rsqrt(square / (NB * feat) + 1e-06)
     inv_ref[...] = jnp.broadcast_to(inv_rms, inv_ref.shape)
     keep = lax.broadcasted_iota(jnp.int32, (tokens, feat), 0) < len_ref[0]
-    for n, piece in enumerate(pieces):
+    for n, piece in enumerate((own_ref, other_ref)):
 
         def write(k, carry, n=n, piece=piece):
             x, z = lax.div(k, 2), lax.rem(k, 2)
-            spot = lax.bitwise_xor(b, x + 2 * (n % 2))
-            place = lax.rem(a + z, 2) * 8 + spot * 2 + lax.rem(c + n // 2, 2)
+            place = lax.rem(a + z, 2) * 8 + lax.rem(b + 4 - x, 4) * 2 + lax.rem(c + n, 2)
             normed_ref[place] = (piece[x, z, :tokens].astype(F32) * inv_ref[:, :1]).astype(BF)
             rows = piece[x, z, tokens : 2 * tokens]
             masked_ref[place] = jnp.where(keep, rows.astype(F32), 0.0).astype(BF)
@@ -195,7 +204,7 @@
                 enc_ref[m, pl.ds(start, erows), :] = piece[x, z, line : line + erows]
             return carry
 
-        lax.fori_loop(0, 4, write, 0)
+        lax.fori_loop(0, 8, write, 0)
 
 
 def attention(scale, enc_len, query, keyed, valued, attended_grad):
@@ -271,17 +280,15 @@
 
 def far_kernel(scale, len_ref, normed_ref, masked_ref, enc_ref, *refs):
     far, high, low, across_low, across_high, acc_in = refs[:6]
-    qg_ref, kv_ref, at_ref, qgt_ref, kvt_ref, att_ref, stat_ref, stack_ref = refs[6:]
+    kv_ref, qgt_ref, kvt_ref, att_ref, stat_ref, stack_ref = refs[6:]
     pieces = [one(far), one(high), both(across_low, across_high), one(low)]
     init = [acc_in[n] for n in range(4)]
     acc = project(blocks_at(2), pieces, normed_ref, masked_ref, enc_ref, stack_ref, init)
     out = attention(scale, len_ref[0], *(value.astype(BF) for value in acc))
     q_grad, k_grad, v_grad, attended, stat = out
     width = q_grad.shape[1]
-    qg_ref[...] = q_grad
     kv_ref[:, :width] = k_grad
     kv_ref[:, width:] = v_grad
-    at_ref[...] = attended
     qgt_ref[...] = q_grad.T
     kvt_ref[:width] = k_grad.T
     kvt_ref[width:] = v_grad.T
@@ -312,43 +319,51 @@
             out[3 * width :] = attn
 
 
-def partial_kernel(qg_ref, kv_ref, at_ref, stat_ref, *refs):
-    stacks, outs, enc_buf = refs[:3], refs[3:5], refs[5]
-    tokens, width = qg_ref.shape
-    keys, feat = enc_buf.shape
-    erows = keys // NB
+def partial_kernel(side, q_t_ref, kv_ref, at_t_ref, stat_ref, own, near, far, out, kv_buf):
+    width, tokens = q_t_ref.shape
+    erows = kv_ref.shape[0] // NB
     a, b, c = mp_place()
-    for out in outs:
-        for xr in range(4):
-            for zr in range(2):
-                out[xr, zr, 3 * tokens :, :] = stat_ref[...]
-    for stack, shifts in zip(stacks, ((0, 0), (3, 1), (2, 2))):
-
-        def body(n, carry, stack=stack, shifts=shifts):
-            place = dp_block(lax.rem(n, 4), jnp.where(n < 4, shifts[0], shifts[1]))
-            weight = stack[n]
-            norm_part = nt(qg_ref[...], weight[:, :width]).astype(BF)
-            out_part = nt(at_ref[...], weight[:, 3 * width :]).astype(BF)
-            enc_buf[...] = nt(kv_ref[...], weight[:, width : 3 * width]).astype(BF)
-            xr = lax.bitwise_xor(lax.rem(lax.div(place, 2), 4), b)
-            zr = lax.rem(lax.div(place, 8) + 2 - a, 2)
-            cr = lax.rem(lax.rem(place, 2) + 2 - c, 2)
-            line = pl.multiple_of(2 * tokens + place * erows, erows)
-            for k, out in enumerate(outs):
-
-                @pl.when(cr == k)
-                def _():
-                    out[xr, zr, :tokens, :] = norm_part
-                    out[xr, zr, tokens : 2 * tokens, :] = out_part
-
-                for x in range(4):
-                    for z in range(2):
-                        owner = lax.rem(a + z, 2) * 8 + lax.bitwise_xor(b, x) * 2 + lax.rem(c + k, 2)
-                        start = pl.multiple_of(owner * erows, erows)
-                        out[x, z, pl.ds(line, erows), :] = enc_buf[pl.ds(start, erows), :]
+    core = lax.rem(c + side, 2)
+    for x in range(4):
+        for z in range(2):
+            out[z, x, 3 * tokens :, :] = stat_ref[...]
+            owner = lax.rem(a + z, 2) * 8 + lax.bitwise_xor(b, x) * 2 + core
+            start = pl.multiple_of(owner * erows, erows)
+            line = (x * 2 + z) * erows
+            kv_buf[line : line + erows, :] = kv_ref[pl.ds(start, erows), :]
+
+    def block_of(n, shifts):
+        return dp_block(lax.rem(n, 4), jnp.where(n < 4, shifts[0], shifts[1]))
+
+    stacks = ((own, (0, 0)), (near, (3, 1)), (far, (2, 2)))
+    for stack, shifts in stacks:
+
+        def enc_part(n, carry, stack=stack, shifts=shifts):
+            line = pl.multiple_of(2 * tokens + block_of(n, shifts) * erows, erows)
+            enc = nt(kv_buf[...], stack[n, :, width : 3 * width]).astype(BF)
+            for x in range(4):
+                for z in range(2):
+                    first = (x * 2 + z) * erows
+                    out[z, x, pl.ds(line, erows), :] = enc[first : first + erows]
             return carry
 
-        lax.fori_loop(0, stack.shape[0], body, 0, unroll=2)
+        lax.fori_loop(0, stack.shape[0], enc_part, 0, unroll=2)
+
+    odd = lax.rem(lax.axis_index("dp") + core, 2)
+    for stack, shifts in stacks:
+
+        @pl.when(odd == shifts[0] % 2)
+        def _():
+            def parts(n, carry):
+                place = block_of(n, shifts)
+                xr = lax.bitwise_xor(lax.rem(lax.div(place, 2), 4), b)
+                zr = lax.rem(lax.div(place, 8) + 2 - a, 2)
+                out[zr, xr, :tokens, :] = nn(stack[n, :, :width], q_t_ref[...]).astype(BF)
+                out_part = nn(stack[n, :, 3 * width :], at_t_ref[...]).astype(BF)
+                out[zr, xr, tokens : 2 * tokens, :] = out_part
+                return carry
+
+            lax.fori_loop(0, stack.shape[0], parts, 0, unroll=2)
 
 
 def add_rows(ins, out):
@@ -369,19 +384,20 @@
     out[rows:] = pack_stat(stat, (EXTRA, feat))
 
 
-def core_sum_kernel(keep_ref, got_ref, near_ref, far_ref):
+def core_sum_kernel(keep_ref, got_ref, *outs):
+    for z, out in enumerate(outs):
+        for x in range(4):
+            add_rows([keep_ref.at[z, x], got_ref.at[z, x]], out.at[x])
+
+
+def z_sum_kernel(keep_ref, got_ref, near_ref, far_ref):
     for x, out in enumerate((near_ref.at[0], near_ref.at[1], far_ref.at[0], far_ref.at[1])):
-        for z in range(2):
-            add_rows([keep_ref.at[x, z], got_ref.at[x, z]], out.at[z])
-
-
-def split_sum_kernel(first_ref, second_ref, *outs):
+        add_rows([keep_ref.at[x], got_ref.at[x]], out)
+
+
+def x_sum_kernel(first_ref, second_ref, *outs):
     for n, out in enumerate(outs):
-        if len(out.shape) == 2:
-            add_rows([first_ref.at[n], second_ref.at[n]], out)
-        else:
-            for z in range(2):
-                add_rows([first_ref.at[n, z], second_ref.at[n, z]], out.at[z])
+        add_rows([first_ref.at[n], second_ref.at[n]], out)
 
 
 def share_kernel(*refs):
@@ -396,16 +412,14 @@
     outs[3][...] = total[3 * width :]
 
 
-def last_kernel(len_ref, own_ref, got_ref, acts_ref, inv_ref, out_ref, in_ref, enc_ref):
+def last_kernel(len_ref, *refs):
+    terms, (acts_ref, inv_ref, out_ref, in_ref, enc_ref) = refs[:2], refs[2:]
     tokens, feat = out_ref.shape[1:]
     rows = 3 * tokens
-    stat = stat_of(own_ref[rows:]) + stat_of(got_ref[rows:])
+    total = [sum(ref[n * tokens : (n + 1) * tokens].astype(F32) for ref in terms) for n in range(3)]
+    total[0], total[1] = total[0].T, total[1].T
+    stat = sum(stat_of(ref[rows:]) for ref in terms)
     stat = jnp.broadcast_to(stat, (128, tokens)).T[:, :1] / (NB * feat)
-    total = [
-        own_ref[n * tokens : (n + 1) * tokens].astype(F32)
-        + got_ref[n * tokens : (n + 1) * tokens].astype(F32)
-        for n in range(3)
-    ]
     inv_rms = inv_ref[:, :1]
     dec = acts_ref[:tokens].astype(F32)
     out_ref[0] = (dec + total[1]).astype(BF)
@@ -422,39 +436,40 @@
     return call(pair_kernel, (first, second), [shape_of((2,) + first.shape)])[0]
 
 
-def gather(block, acts):
+def halves(first, second):
+    half = shape_of((first.shape[0] // 2, first.shape[1]))
+    return call(halves_kernel, (first, second), [half] * 2)
+
+
+def gather(block, acts, begin):
     before, behind = send_z(block, 1), send_z(block, -1)
     low, high = send_y(block, 1), send_y(block, -1)
     other = send_mp(acts, 1, 0, 0)
     other, again = after((other, block), low, high)
     pair_acts = stack_pair(acts, other)
-    next_acts = send_x(pair_acts, 1)
+    x1, x3 = send_mp(pair_acts, 0, 1, 0), send_mp(pair_acts, 0, 3, 0)
     across = send_y(again, 2)
 
-    pair_acts, next_acts, far, before, behind = after(
-        (pair_acts, next_acts, block, before, behind), across
-    )
-    quad = stack_pair(pair_acts, next_acts)
-    far_quad = send_x(quad, 2)
+    pair_acts, x1, x3, before, behind = after((pair_acts, x1, x3, before, behind), across)
+    x2 = send_mp(pair_acts, 0, 2, 0)
     pair = stack_pair(before, behind)
     pair_low, pair_high = send_y(pair, 1), send_y(pair, -1)
-    far = send_z(far, 2)
-
-    pair_low, pair_high, far = after((pair_low, pair_high, far))
+    to_low, to_high = halves(before, behind)
+    far_low, far_high = send_z(to_low, 1), send_z(to_high, -1)
+    (far,) = call(join_kernel, (far_low, far_high), [shape_of(block.shape)])
+    f_low, f_high = send_y(far, 1), send_y(far, -1)
+
+    x2, pair_low, pair_high, f_low, f_high = after((x2, pair_low, pair_high, f_low, f_high))
+    (line,) = call(quad_kernel, (pair_acts, x1, x2, x3), [shape_of((4,) + pair_acts.shape)])
+    sibling = send_mp(line, 0, 0, 1)
     to_low, to_high = call(pick_kernel, (pair_low, pair_high), [shape_of(block.shape)] * 2)
     across_b, across_a = send_y(to_low, 1), send_y(to_high, -1)
-    f_low, f_high = send_y(far, 1), send_y(far, -1)
-
-    quad, far_quad, f_low, f_high = after((quad, far_quad, f_low, f_high), across_a, across_b)
-    pieces = [quad, far_quad, send_mp(quad, 0, 0, 1), send_mp(far_quad, 0, 0, 1)]
-    half = shape_of((block.shape[0] // 2, block.shape[1]))
-    to_low, to_high = call(halves_kernel, (f_low, f_high), [half] * 2)
+    to_low, to_high = halves(f_low, f_high)
     last_low, last_high = send_y(to_low, 1), send_y(to_high, -1)
     return (
-        (block, high, low, across),
         (pair, pair_high, pair_low, across_b, across_a),
         (far, f_high, f_low, last_low, last_high),
-        pieces,
+        begin((line, sibling), (block, high, low, across)),
     )
 
 
@@ -504,55 +519,83 @@
                 out[rows] = ref[rows]
 
 
-def second_sum_kernel(far0, far1, far3, bf1, bf2, bf3, bh1, bh2, bh3, up, down, far):
+def second_sum_kernel(far0, far1, far3, bf1, bf2, bf3, bh1, bh2, bh3, up, down, far_low, far_high):
     summed(up, put_at(0), plain(bf1), plain(bf2))
     summed(up, put_at(1), plain(bh1))
     summed(down, put_at(0), plain(bf3))
     summed(down, put_at(1), plain(bh3), plain(bh2))
-    summed(far, put_plain, plain(far0), plain(far1), plain(far3))
-
-
-def third_sum_kernel(bf0, bh0, up, down, before, behind):
-    summed(before, put_plain, plain(bf0), of(up, 0), of(down, 0))
-    summed(behind, put_plain, plain(bh0), of(up, 1), of(down, 1))
+    half = far_low.shape[0]
+    for out, first in ((far_low, 0), (far_high, half)):
+        summed(out, put_plain, *(plain(ref.at[first : first + half]) for ref in (far0, far1, far3)))
+
+
+def third_sum_kernel(bf0, bh0, up, down, low, high, before, behind):
+    half = low.shape[0]
+    for out, ref, n, part, first in ((before, bf0, 0, low, 0), (behind, bh0, 1, high, half)):
+
+        def body(step, carry, out=out, ref=ref, n=n, part=part, first=first):
+            begin = pl.multiple_of(step * CHUNK, CHUNK)
+            rows, here = pl.ds(begin + first, CHUNK), pl.ds(begin, CHUNK)
+            rest = pl.ds(begin + half - first, CHUNK)
+            total = ref[rows, :].astype(F32) + up[n, rows, :].astype(F32)
+            total += down[n, rows, :].astype(F32) + part[here, :].astype(F32)
+            out[rows, :] = total.astype(BF)
+            total = ref[rest, :].astype(F32) + up[n, rest, :].astype(F32)
+            total += down[n, rest, :].astype(F32)
+            out[rest, :] = total.astype(BF)
+            return carry
+
+        lax.fori_loop(0, half // CHUNK, body, 0)
 
 
 def scatter(grads, partials):
-    far0, far1, far2_low, far2_high, far3 = grads(2, ())
+    send = partials(1)
+    core = send_mp(send, 0, 0, 1)
+    far0, far1, far2_low, far2_high, far3 = grads(2, (send,))
     full = shape_of(far0.shape)
     pair = shape_of((2,) + far0.shape)
+    own0, own1, own2, own3 = grads(0, (far0,))
     far2_low, far2_high = send_y(far2_low, 1), send_y(far2_high, -1)
-    bf0, bf1, bf2, bf3 = grads(1, (far0,))
+    bf0, bf1, bf2, bf3 = grads(1, (own0,))
     bh0, bh1, bh2, bh3 = grads(3, (bf0,))
-    keep, send = partials((bh0,))
-
-    far2_low, far2_high, bf2, bh2, send = after((far2_low, far2_high, bf2, bh2, send))
+    keep = partials(0)
+
+    core, keep, far2_low, far2_high, bf2, bh2 = after(
+        (core, keep, far2_low, far2_high, bf2, bh2)
+    )
+    part = shape_of(keep.shape[1:])
+    own_z, other_z = call(core_sum_kernel, (keep, core), [part] * 2, moved=9 * MIB)
+    other_z = send_mp(other_z, 1, 0, 0)
     bf2, bh2 = send_y(bf2, 1), send_y(bh2, -1)
     far1, far3 = call(far_kernel_sum, (far1, far3, far2_low, far2_high), [full] * 2)
     far1, far3 = send_y(far1, 1), send_y(far3, -1)
-    core = send_mp(send, 0, 0, 1)
-    part = shape_of((2,) + keep.shape[1:])
-    near_x, far_x = call(core_sum_kernel, (keep, core), [part] * 2, moved=9 * MIB)
+
+    far1, far3, bf2, bh2 = after((far1, far3, bf2, bh2))
+    half = shape_of(far2_low.shape)
+    up, down, far_low, far_high = call(
+        second_sum_kernel, (far0, far1, far3, bf1, bf2, bf3, bh1, bh2, bh3),
+        [pair, pair, half, half],
+    )
+    up, down = send_y(up, 1), send_y(down, -1)
+    far_low, far_high = send_z(far_low, 1), send_z(far_high, -1)
+    (other_z,) = after((other_z,), far_low, far_high)
+    part = shape_of((2,) + keep.shape[2:])
+    near_x, far_x = call(z_sum_kernel, (own_z, other_z), [part] * 2, moved=6 * MIB)
     far_x = send_x(far_x, 2)
-    own0, own1, own2, own3 = grads(0, (core,))
-
-    far1, far3, bf2, bh2 = after((far1, far3, bf2, bh2), own0)
-    up, down, far = call(
-        second_sum_kernel, (far0, far1, far3, bf1, bf2, bf3, bh1, bh2, bh3), [pair, pair, full]
-    )
-    up, down, far = send_y(up, 1), send_y(down, -1), send_z(far, 2)
-    part = shape_of(keep.shape[1:])
-    near_x, next_x = call(split_sum_kernel, (near_x, far_x), [part] * 2, moved=6 * MIB)
-    next_x = send_x(next_x, 1)
-
-    up, down, far, own1, own2, own3 = after((up, down, far, own1, own2, own3))
-    before, behind = call(third_sum_kernel, (bf0, bh0, up, down), [full] * 2)
+
+    up, down, far_low, far_high, own1, own2, own3 = after(
+        (up, down, far_low, far_high, own1, own2, own3)
+    )
+    before, behind = call(
+        third_sum_kernel, (bf0, bh0, up, down, far_low, far_high), [full] * 2
+    )
+    before, behind = send_z(before, 1), send_z(behind, -1)
+    own1, own3 = send_y(own1, 1), send_y(own3, -1)
+    own2, own1, own3 = after((own2, own1, own3))
     own2 = send_y(own2, 2)
-    own1, own3 = send_y(own1, 1), send_y(own3, -1)
-    before, behind = send_z(before, 1), send_z(behind, -1)
     part = shape_of(keep.shape[2:])
-    own, other = call(split_sum_kernel, (near_x, next_x), [part] * 2, moved=4 * MIB)
-    return (own0, far, own1, own2, own3, before, behind), (own, send_mp(other, 1, 0, 0))
+    own_x, next_x = call(x_sum_kernel, (near_x, far_x), [part] * 2, moved=3 * MIB)
+    return (own0, own1, own2, own3, before, behind), (own_x, send_x(next_x, 1))
 
 
 def local(
@@ -586,32 +629,36 @@
         ],
         compiler_params=pltpu.CompilerParams(vmem_limit_bytes=56 * MIB),
     )(query_weight, key_weight, value_weight, output_weight, dec_input, cotangent, enc_output)
-    own_group, near_group, far_group, pieces = gather(weights, acts)
-
-    normed, masked, encoded, inv_rms = call(
-        prepare_kernel, pieces,
-        [
-            shape_of((NB, tokens, feat)), shape_of((NB, tokens, feat)),
-            shape_of((NB, keys, feat)), shape_of((tokens, 128), F32),
-        ],
-        (dec_lengths,), moved=12 * MIB,
-    )
-    stacked = (normed, masked, encoded)
     acc_shape = shape_of((4, tokens, width), F32)
     stack_shape = shape_of((4, feat, 4 * width))
-    acc, own_stack = call(
-        own_kernel, (*stacked, *own_group), [acc_shape, stack_shape],
-        flops=16 * unit, moved=4 * MIB,
-    )
+
+    def begin(pieces, own_group):
+        normed, masked, encoded, inv_rms = call(
+            prepare_kernel, pieces,
+            [
+                shape_of((NB, tokens, feat)), shape_of((NB, tokens, feat)),
+                shape_of((NB, keys, feat)), shape_of((tokens, 128), F32),
+            ],
+            (dec_lengths,), moved=12 * MIB,
+        )
+        acc, own_stack = call(
+            own_kernel, (normed, masked, encoded, *own_group), [acc_shape, stack_shape],
+            flops=16 * unit, moved=4 * MIB,
+        )
+        return normed, masked, encoded, inv_rms, own_stack, acc
+
+    near_group, far_group, start = gather(weights, acts, begin)
+    normed, masked, encoded, inv_rms, own_stack, acc = start
+    stacked = (normed, masked, encoded)
     acc, near_stack = call(
-        near_kernel, (*stacked, *near_group, acc),
-        [acc_shape, shape_of((8, feat, 4 * width))], flops=32 * unit, moved=8 * MIB,
-    )
-    tshape, kshape = shape_of((tokens, width)), shape_of((keys, 2 * width))
-    q_grad, kv_grad, attended, q_t, kv_t, at_t, stat, far_stack = call(
+        near_kernel, (*stacked, *near_group, acc), [acc_shape, shape_of((8, feat, 4 * width))],
+        flops=32 * unit, moved=8 * MIB,
+    )
+    kshape = shape_of((keys, 2 * width))
+    kv_grad, q_t, kv_t, at_t, stat, far_stack = call(
         functools.partial(far_kernel, scale), (*stacked, *far_group, acc),
         [
-            tshape, kshape, tshape, shape_of((width, tokens)), shape_of((2 * width, keys)),
+            kshape, shape_of((width, tokens)), shape_of((2 * width, keys)),
             shape_of((width, tokens)), shape_of((EXTRA, tokens)), stack_shape,
         ],
         (enc_lengths,), flops=24 * unit, moved=4 * MIB,
@@ -626,21 +673,21 @@
             outs, flops=16 * unit, moved=4 * MIB,
         )
 
-    def partials(others):
-        (q_in,) = after((q_grad,), *others)
-        out = shape_of((4, 2, 3 * tokens + EXTRA, feat))
+    def partials(side):
+        out = shape_of((2, 4, 3 * tokens + EXTRA, feat))
         return call(
-            partial_kernel, (q_in, kv_grad, attended, stat, own_stack, near_stack, far_stack),
-            [out, out], scratch=[pltpu.VMEM((keys, feat), BF)], flops=64 * unit, moved=14 * MIB,
-        )
-
-    shares, (line, got) = scatter(grads, partials)
+            functools.partial(partial_kernel, side),
+            (q_t, kv_grad, at_t, stat, own_stack, near_stack, far_stack),
+            [out], scratch=[pltpu.VMEM((keys // 2, 2 * width), BF)], flops=32 * unit, moved=14 * MIB,
+        )[0]
+
+    shares, terms = scatter(grads, partials)
     query_grad, key_grad, value_grad, output_grad = call_out(
         share_kernel, shares, [shape_of((feat, width))] * 4
     )
     stack = shape_of((1, tokens, feat))
     layer_out, input_grad, enc_grad = call_out(
-        last_kernel, (line, got, acts, inv_rms),
+        last_kernel, (*terms, acts, inv_rms),
         [stack, stack, shape_of((1, erows, NB * feat))], (dec_lengths,),
     )
     return (layer_out, input_grad, enc_grad, query_grad, key_grad, value_grad, output_grad)

time: 235 us -> 231 us (0.983); the launches traced: 235 us -> 228 us
  starting transfers between devices: 95 us -> 71.3 us
  Pallas kernels: 23.8 us -> 35.4 us
  waiting for transfers between devices: 113 us -> 117 us
    ppermute x6 -> x8, starting transfers between devices: 36.3 us -> 17.8 us  [send_z(): lax.ppermute(value, 'dp', [(dp_index(y, z), dp_index(y, z + d)) for y, z...]
    ppermute x22, waiting for transfers between devices: 38.9 us -> 57.1 us  [send_y(): lax.ppermute(value, 'dp', [(dp_index(y, z), dp_index(y + d, z)) for y, z...]
    ppermute x5 -> x7, waiting for transfers between devices: 22.1 us -> 7.85 us  [send_mp(): return lax.ppermute(value, 'mp', pairs)]
    pallas_call x20 -> x23, Pallas kernels: 19.4 us -> 31 us  [call(): pl.pallas_call(kernel, in_specs=[pl.BlockSpec(memory_space=pltpu.SMEM)] *...]
    ppermute x5 -> x7, starting transfers between devices: 27 us -> 22.6 us  [send_mp(): return lax.ppermute(value, 'mp', pairs)]
    ppermute x4 -> x2, starting transfers between devices: 4.78 us -> 2.2 us  [send_x(): return lax.ppermute(value, 'mp', pairs)]
    ppermute x6 -> x8, waiting for transfers between devices: 51.9 us -> 50.3 us  [send_z(): lax.ppermute(value, 'dp', [(dp_index(y, z), dp_index(y, z + d)) for y, z...]
  transfers between devices with their start and end apart: 37 -> 39, of which waited for: 18 -> 17; matrix products, arithmetic and copies ran while one was open for 0% -> 0% of each run, Pallas kernels for 7% -> 11%
where the time goes in v3:
time: 231 us; the launch traced here: 228 us
  waiting for transfers between devices  117 us (51%)
  starting transfers between devices  71.3 us (31%)
  Pallas kernels  35.4 us (15%)
  between operations  2.46 us (1%)
    ppermute x22, waiting for transfers between devices, send_y(): lax.ppermute(value, 'dp', [(dp_index(y, z), dp_index(y + d, z)) for y, z...  57.1 us
    ppermute x8, waiting for transfers between devices, send_z(): lax.ppermute(value, 'dp', [(dp_index(y, z), dp_index(y, z + d)) for y, z...  50.3 us
    pallas_call x23, Pallas kernels, call(): pl.pallas_call(kernel, in_specs=[pl.BlockSpec(memory_space=pltpu.SMEM)] *...  31 us
    ppermute x22, starting transfers between devices, send_y(): lax.ppermute(value, 'dp', [(dp_index(y, z), dp_index(y + d, z)) for y, z...  28.7 us
    ppermute x7, starting transfers between devices, send_mp(): return lax.ppermute(value, 'mp', pairs)  22.6 us
    ppermute x8, starting transfers between devices, send_z(): lax.ppermute(value, 'dp', [(dp_index(y, z), dp_index(y, z + d)) for y, z...  17.8 us
    ppermute x7, waiting for transfers between devices, send_mp(): return lax.ppermute(value, 'mp', pairs)  7.85 us
  transfers between devices with their start and end apart: 39, of which 17 were waited for; matrix products, arithmetic and copies ran while one was open for 0% of the time, Pallas kernels for 11%

profile of v3, /device:TPU:1, one launch (start us, length us, event | category | flops | bytes accessed | tf_op | source)
XLA Modules:
  0.0 227.5 jit_solution(11738637528823841359)
XLA Ops:
  2.9 3.6 %collective-permute-start.1 = (bf16[256,1024]{1,0:T(8,128)(2,1)}, bf16[256,1024]{1,0:T(8,128)(2,1)S(1)}, u32[]{:S(2)}, u32[]{:S(2)}) collective-permute-start(bf16[256,1024]{1,0:T(8,128)(2,1)} %get-tuple-element.106.refs_0_), channel_id=1, source_target_pairs={{0,192},{16,208},{32,224},{48,240},{64,0},{80,16},{96,32},{112,48}... | collective-permute-start | bytes 1572872 | tf_op jit(solution)/shard_map/ppermute | solution.py:30
  8.2 7.8 %collective-permute-done.2.second = bf16[768,256]{1,0:T(8,128)(2,1)S(1)} collective-permute-done((bf16[768,256]{1,0:T(8,128)(2,1)}, bf16[768,256]{1,0:T(8,128)(2,1)S(1)}, u32[]{:S(2)}, u32[]{:S(2)}) %collective-permute-start.2) | collective-permute-done | bytes 393248 | tf_op jit(solution)/shard_map/ppermute | solution.py:39
  17.4 3.0 %collective-permute-done.refs_2_ = bf16[256,1024]{1,0:T(8,128)(2,1)S(1)} collective-permute-done((bf16[256,1024]{1,0:T(8,128)(2,1)}, bf16[256,1024]{1,0:T(8,128)(2,1)S(1)}, u32[]{:S(2)}, u32[]{:S(2)}) %collective-permute-start) | collective-permute-done | bytes 524320 | tf_op jit(solution)/shard_map/ppermute | solution.py:30
  24.0 6.0 %collective-permute-start.7 = (bf16[256,1024]{1,0:T(8,128)(2,1)}, bf16[256,1024]{1,0:T(8,128)(2,1)S(1)}, u32[]{:S(2)}, u32[]{:S(2)}) collective-permute-start(bf16[256,1024]{1,0:T(8,128)(2,1)} %get-tuple-element.106.refs_0_), channel_id=1, source_target_pairs={{0,48},{16,0},{32,16},{48,32},{64,112},{80,64},{96,80},{112,96},{1... | collective-permute-start | bytes 1572872 | tf_op jit(solution)/shard_map/ppermute | solution.py:34
  30.1 19.7 %collective-permute-done.7.second = bf16[256,1024]{1,0:T(8,128)(2,1)S(1)} collective-permute-done((bf16[256,1024]{1,0:T(8,128)(2,1)}, bf16[256,1024]{1,0:T(8,128)(2,1)S(1)}, u32[]{:S(2)}, u32[]{:S(2)}) %collective-permute-start.7) | collective-permute-done | bytes 524320 | tf_op jit(solution)/shard_map/ppermute | solution.py:34
  51.4 4.5 %collective-permute-start.11 = (bf16[128,1024]{1,0:T(8,128)(2,1)S(1)}, bf16[128,1024]{1,0:T(8,128)(2,1)S(1)}, u32[]{:S(2)}, u32[]{:S(2)}) collective-permute-start(bf16[128,1024]{1,0:T(8,128)(2,1)S(1)} %get-tuple-element.112), channel_id=1, source_target_pairs={{0,16},{16,32},{32,48},{48,0},{64,80},{80,96},{96,112},{112,64},{1... | collective-permute-start | bytes 786440 | tf_op jit(solution)/shard_map/ppermute | solution.py:34
  64.6 13.5 %collective-permute-done.14.second.refs_1_ = bf16[256,1024]{1,0:T(8,128)(2,1)S(1)} collective-permute-done((bf16[256,1024]{1,0:T(8,128)(2,1)S(1)}, bf16[256,1024]{1,0:T(8,128)(2,1)S(1)}, u32[]{:S(2)}, u32[]{:S(2)}) %collective-permute-start.14) | collective-permute-done | bytes 524320 | tf_op jit(solution)/shard_map/ppermute | solution.py:30
  80.0 8.6 %collective-permute-start.15 = (bf16[4,2,768,256]{3,2,1,0:T(8,128)(2,1)S(1)}, bf16[4,2,768,256]{3,2,1,0:T(8,128)(2,1)S(1)}, u32[]{:S(2)}, u32[]{:S(2)}) collective-permute-start(bf16[4,2,768,256]{3,2,1,0:T(8,128)(2,1)S(1)} %shard_map.149.own_ref), channel_id=1, source_target_pairs={{0,1},{1,0},{2,3},{3,2},{4,5},{5,4},{6,7},{7,6},{8,9},{9,8},{10,11... | collective-permute-start | bytes 9437192 | tf_op jit(solution)/shard_map/ppermute | solution.py:39
  90.3 2.7 %collective-permute-start.17 = (bf16[128,1024]{1,0:T(8,128)(2,1)S(1)}, bf16[128,1024]{1,0:T(8,128)(2,1)S(1)}, u32[]{:S(2)}, u32[]{:S(2)}) collective-permute-start(bf16[128,1024]{1,0:T(8,128)(2,1)S(1)} %get-tuple-element.122), channel_id=1, source_target_pairs={{0,192},{16,208},{32,224},{48,240},{64,0},{80,16},{96,32},{112,48}... | collective-permute-start | bytes 786440 | tf_op jit(solution)/shard_map/ppermute | solution.py:30
  95.8 3.6 %shard_map.150 = (bf16[16,256,256]{2,1,0:T(8,128)(2,1)S(1)}, bf16[16,256,256]{2,1,0:T(8,128)(2,1)S(1)}, bf16[16,256,256]{2,1,0:T(8,128)(2,1)S(1)}, f32[256,128]{1,0:T(8,128)S(1)}) custom-call(s32[1]{0:T(128)S(6)} %copy.17.len_ref.refs_0_, bf16[4,2,768,256]{3,2,1,0:T(8,128)(2,1)S(1)} %shard_map.149.own_ref, ...), custom_call_target="tpu_custom_call" | custom-call | bytes 12582912 | tf_op jit(solution)/shard_map/pallas_call | solution.py:65
  100.1 10.6 %collective-permute-done.18.refs_3_ = bf16[256,1024]{1,0:T(8,128)(2,1)S(1)} collective-permute-done((bf16[256,1024]{1,0:T(8,128)(2,1)S(1)}, bf16[256,1024]{1,0:T(8,128)(2,1)S(1)}, u32[]{:S(2)}, u32[]{:S(2)}) %collective-permute-start.18) | collective-permute-done | bytes 524320 | tf_op jit(solution)/shard_map/ppermute | solution.py:30
  113.4 3.8 %shard_map.156 = bf16[2,4,784,256]{3,2,1,0:T(8,128)(2,1)S(1)} custom-call(bf16[256,256]{1,0:T(8,128)(2,1)S(1)} %get-tuple-element.129.q_t_ref.refs_0_, bf16[256,512]{1,0:T(8,128)(2,1)S(1)} %get-tuple-element.130.kv_ref, bf16[256,256]{1,0:T(8,128)(2,1)S(1)} %get-tuple-element.131.at_t_ref.refs_2_, bf16[16,256]{1,0:T(8,128)(2,1)S(1)} %get-tuple-element.132.stat_ref, ...), custom_call_target="tpu_custom_call" | custom-call | flops 17179869184 | bytes 14680064 | tf_op jit(solution)/shard_map/pallas_call | solution.py:65
  118.9 2.7 %collective-permute-start.22 = (bf16[512,256]{1,0:T(8,128)(2,1)S(1)}, bf16[512,256]{1,0:T(8,128)(2,1)S(1)}, u32[]{:S(2)}, u32[]{:S(2)}) collective-permute-start(bf16[512,256]{1,0:T(8,128)(2,1)S(1)} %get-tuple-element.139), channel_id=1, source_target_pairs={{0,192},{16,208},{32,224},{48,240},{64,0},{80,16},{96,32},{112,48}... | collective-permute-start | bytes 786440 | tf_op jit(solution)/shard_map/ppermute | solution.py:30
  123.1 13.7 %shard_map.157.keep_ref = bf16[2,4,784,256]{3,2,1,0:T(8,128)(2,1)S(1)} custom-call(bf16[256,256]{1,0:T(8,128)(2,1)S(1)} %get-tuple-element.129.q_t_ref.refs_0_, bf16[256,512]{1,0:T(8,128)(2,1)S(1)} %get-tuple-element.130.kv_ref, bf16[256,256]{1,0:T(8,128)(2,1)S(1)} %get-tuple-element.131.at_t_ref.refs_2_, bf16[16,256]{1,0:T(8,128)(2,1)S(1)} %get-tuple-element.132.stat_ref, ...), custom_call_target="tpu_custom_call" | custom-call | flops 17179869184 | bytes 14680064 | tf_op jit(solution)/shard_map/pallas_call | solution.py:65
  138.6 7.3 %collective-permute-start.29 = (bf16[4,784,256]{2,1,0:T(8,128)(2,1)S(1)}, bf16[4,784,256]{2,1,0:T(8,128)(2,1)S(1)}, u32[]{:S(2)}, u32[]{:S(2)}) collective-permute-start(bf16[4,784,256]{2,1,0:T(8,128)(2,1)S(1)} %get-tuple-element.169), channel_id=1, source_target_pairs={{0,8},{1,9},{2,10},{3,11},{4,12},{5,13},{6,14},{7,15},{8,0},{9,1},... | collective-permute-start | bytes 4816904 | tf_op jit(solution)/shard_map/ppermute | solution.py:39
  148.9 2.7 %collective-permute-start.26 = (bf16[1024,256]{1,0:T(8,128)(2,1)S(1)}, bf16[1024,256]{1,0:T(8,128)(2,1)S(1)}, u32[]{:S(2)}, u32[]{:S(2)}) collective-permute-start(bf16[1024,256]{1,0:T(8,128)(2,1)S(1)} %get-tuple-element.158), channel_id=1, source_target_pairs={{0,192},{16,208},{32,224},{48,240},{64,0},{80,16},{96,32},{112,48}... | collective-permute-start | bytes 1572872 | tf_op jit(solution)/shard_map/ppermute | solution.py:30
  151.6 8.5 %collective-permute-done.23.far1 = bf16[1024,256]{1,0:T(8,128)(2,1)S(1)} collective-permute-done((bf16[1024,256]{1,0:T(8,128)(2,1)S(1)}, bf16[1024,256]{1,0:T(8,128)(2,1)S(1)}, u32[]{:S(2)}, u32[]{:S(2)}) %collective-permute-start.23) | collective-permute-done | bytes 524320 | tf_op jit(solution)/shard_map/ppermute | solution.py:30
  160.1 11.2 %collective-permute-done.25.bf2 = bf16[1024,256]{1,0:T(8,128)(2,1)S(1)} collective-permute-done((bf16[1024,256]{1,0:T(8,128)(2,1)S(1)}, bf16[1024,256]{1,0:T(8,128)(2,1)S(1)}, u32[]{:S(2)}, u32[]{:S(2)}) %collective-permute-start.25) | collective-permute-done | bytes 524320 | tf_op jit(solution)/shard_map/ppermute | solution.py:30
  174.7 3.6 %collective-permute-start.28 = (bf16[512,256]{1,0:T(8,128)(2,1)S(1)}, bf16[512,256]{1,0:T(8,128)(2,1)S(1)}, u32[]{:S(2)}, u32[]{:S(2)}) collective-permute-start(bf16[512,256]{1,0:T(8,128)(2,1)S(1)} %get-tuple-element.168), channel_id=1, source_target_pairs={{0,48},{16,0},{32,16},{48,32},{64,112},{80,64},{96,80},{112,96},{1... | collective-permute-start | bytes 786440 | tf_op jit(solution)/shard_map/ppermute | solution.py:34
  178.3 13.7 %collective-permute-done.27.low = bf16[512,256]{1,0:T(8,128)(2,1)S(1)} collective-permute-done((bf16[512,256]{1,0:T(8,128)(2,1)S(1)}, bf16[512,256]{1,0:T(8,128)(2,1)S(1)}, u32[]{:S(2)}, u32[]{:S(2)}) %collective-permute-start.27) | collective-permute-done | bytes 262176 | tf_op jit(solution)/shard_map/ppermute | solution.py:34
  199.9 3.2 %collective-permute-start.38 = (bf16[1024,256]{1,0:T(8,128)(2,1)S(1)}, bf16[1024,256]{1,0:T(8,128)(2,1)S(1)}, u32[]{:S(2)}, u32[]{:S(2)}) collective-permute-start(bf16[1024,256]{1,0:T(8,128)(2,1)S(1)} %get-tuple-element.196), channel_id=1, source_target_pairs={{0,48},{16,0},{32,16},{48,32},{64,112},{80,64},{96,80},{112,96},{1... | collective-permute-start | bytes 1572872 | tf_op jit(solution)/shard_map/ppermute | solution.py:34
  203.1 5.2 %collective-permute-done.34.refs_1_ = bf16[1024,256]{1,0:T(8,128)(2,1)S(1)} collective-permute-done((bf16[1024,256]{1,0:T(8,128)(2,1)S(1)}, bf16[1024,256]{1,0:T(8,128)(2,1)S(1)}, u32[]{:S(2)}, u32[]{:S(2)}) %collective-permute-start.34) | collective-permute-done | bytes 524320 | tf_op jit(solution)/shard_map/ppermute | solution.py:30
  212.8 5.5 %collective-permute-done.37.refs_4_ = bf16[1024,256]{1,0:T(8,128)(2,1)S(1)} collective-permute-done((bf16[1024,256]{1,0:T(8,128)(2,1)S(1)}, bf16[1024,256]{1,0:T(8,128)(2,1)S(1)}, u32[]{:S(2)}, u32[]{:S(2)}) %collective-permute-start.37) | collective-permute-done | bytes 524320 | tf_op jit(solution)/shard_map/ppermute | solution.py:34
  218.3 6.7 %collective-permute-done.38.refs_5_ = bf16[1024,256]{1,0:T(8,128)(2,1)S(1)} collective-permute-done((bf16[1024,256]{1,0:T(8,128)(2,1)S(1)}, bf16[1024,256]{1,0:T(8,128)(2,1)S(1)}, u32[]{:S(2)}, u32[]{:S(2)}) %collective-permute-start.38) | collective-permute-done | bytes 524320 | tf_op jit(solution)/shard_map/ppermute | solution.py:34
  (86 shorter events, 53.6 us)
Async XLA Ops:
  21.5 28.3 %collective-permute-start.5 = (bf16[2,768,256]{2,1,0:T(8,128)(2,1)S(1)}, bf16[2,768,256]{2,1,0:T(8,128)(2,1)S(1)}, u32[]{:S(2)}, u32[]{:S(2)}) collective-permute-start(bf16[2,768,256]{2,1,0:T(8,128)(2,1)S(1)} %shard_map.145.refs_0_), channel_id=1, source_target_pairs={{0,6},{1,7},{2,0},{3,1},{4,2},{5,3},{6,4},{7,5},{8,14},{9,15},{10,... | collective-permute-start | bytes 2359304 | tf_op jit(solution)/shard_map/ppermute | solution.py:39
  24.0 25.7 %collective-permute-start.4 = (bf16[2,768,256]{2,1,0:T(8,128)(2,1)S(1)}, bf16[2,768,256]{2,1,0:T(8,128)(2,1)S(1)}, u32[]{:S(2)}, u32[]{:S(2)}) collective-permute-start(bf16[2,768,256]{2,1,0:T(8,128)(2,1)S(1)} %shard_map.145.refs_0_), channel_id=1, source_target_pairs={{0,2},{1,3},{2,4},{3,5},{4,6},{5,7},{6,0},{7,1},{8,10},{9,11},{10,... | collective-permute-start | bytes 2359304 | tf_op jit(solution)/shard_map/ppermute | solution.py:39
  24.0 25.7 %collective-permute-start.7 = (bf16[256,1024]{1,0:T(8,128)(2,1)}, bf16[256,1024]{1,0:T(8,128)(2,1)S(1)}, u32[]{:S(2)}, u32[]{:S(2)}) collective-permute-start(bf16[256,1024]{1,0:T(8,128)(2,1)} %get-tuple-element.106.refs_0_), channel_id=1, source_target_pairs={{0,48},{16,0},{32,16},{48,32},{64,112},{80,64},{96,80},{112,96},{1... | collective-permute-start | bytes 1572872 | tf_op jit(solution)/shard_map/ppermute | solution.py:34
  30.1 19.7 %collective-permute-start.6 = (bf16[256,1024]{1,0:T(8,128)(2,1)}, bf16[256,1024]{1,0:T(8,128)(2,1)S(1)}, u32[]{:S(2)}, u32[]{:S(2)}) collective-permute-start(bf16[256,1024]{1,0:T(8,128)(2,1)} %get-tuple-element.106.refs_0_), channel_id=1, source_target_pairs={{0,16},{16,32},{32,48},{48,0},{64,80},{80,96},{96,112},{112,64},{1... | collective-permute-start | bytes 1572872 | tf_op jit(solution)/shard_map/ppermute | solution.py:34
  30.1 19.7 %collective-permute-start.3 = (bf16[256,1024]{1,0:T(8,128)(2,1)}, bf16[256,1024]{1,0:T(8,128)(2,1)S(1)}, u32[]{:S(2)}, u32[]{:S(2)}) collective-permute-start(bf16[256,1024]{1,0:T(8,128)(2,1)} %get-tuple-element.106.refs_0_), channel_id=1, source_target_pairs={{0,128},{16,144},{32,160},{48,176},{64,192},{80,208},{96,224},{112... | collective-permute-start | bytes 1572872 | tf_op jit(solution)/shard_map/ppermute | solution.py:30
  49.9 29.9 %collective-permute-start.10 = (bf16[2,256,1024]{2,1,0:T(8,128)(2,1)S(1)}, bf16[2,256,1024]{2,1,0:T(8,128)(2,1)S(1)}, u32[]{:S(2)}, u32[]{:S(2)}) collective-permute-start(bf16[2,256,1024]{2,1,0:T(8,128)(2,1)S(1)} %shard_map.146.refs_0_), channel_id=1, source_target_pairs={{0,192},{16,208},{32,224},{48,240},{64,0},{80,16},{96,32},{112,48}... | collective-permute-start | bytes 3145736 | tf_op jit(solution)/shard_map/ppermute | solution.py:30
  50.3 29.5 %collective-permute-start.9 = (bf16[2,256,1024]{2,1,0:T(8,128)(2,1)S(1)}, bf16[2,256,1024]{2,1,0:T(8,128)(2,1)S(1)}, u32[]{:S(2)}, u32[]{:S(2)}) collective-permute-start(bf16[2,256,1024]{2,1,0:T(8,128)(2,1)S(1)} %shard_map.146.refs_0_), channel_id=1, source_target_pairs={{0,64},{16,80},{32,96},{48,112},{64,128},{80,144},{96,160},{112,17... | collective-permute-start | bytes 3145736 | tf_op jit(solution)/shard_map/ppermute | solution.py:30
  55.9 23.8 %collective-permute-start.8 = (bf16[2,768,256]{2,1,0:T(8,128)(2,1)S(1)}, bf16[2,768,256]{2,1,0:T(8,128)(2,1)S(1)}, u32[]{:S(2)}, u32[]{:S(2)}) collective-permute-start(bf16[2,768,256]{2,1,0:T(8,128)(2,1)S(1)} %shard_map.145.refs_0_), channel_id=1, source_target_pairs={{0,4},{1,5},{2,6},{3,7},{4,0},{5,1},{6,2},{7,3},{8,12},{9,13},{10,... | collective-permute-start | bytes 2359304 | tf_op jit(solution)/shard_map/ppermute | solution.py:39
  89.9 22.0 %collective-permute-start.16 = (bf16[128,1024]{1,0:T(8,128)(2,1)S(1)}, bf16[128,1024]{1,0:T(8,128)(2,1)S(1)}, u32[]{:S(2)}, u32[]{:S(2)}) collective-permute-start(bf16[128,1024]{1,0:T(8,128)(2,1)S(1)} %get-tuple-element.121), channel_id=1, source_target_pairs={{0,64},{16,80},{32,96},{48,112},{64,128},{80,144},{96,160},{112,17... | collective-permute-start | bytes 786440 | tf_op jit(solution)/shard_map/ppermute | solution.py:30
  90.3 21.7 %collective-permute-start.17 = (bf16[128,1024]{1,0:T(8,128)(2,1)S(1)}, bf16[128,1024]{1,0:T(8,128)(2,1)S(1)}, u32[]{:S(2)}, u32[]{:S(2)}) collective-permute-start(bf16[128,1024]{1,0:T(8,128)(2,1)S(1)} %get-tuple-element.122), channel_id=1, source_target_pairs={{0,192},{16,208},{32,224},{48,240},{64,0},{80,16},{96,32},{112,48}... | collective-permute-start | bytes 786440 | tf_op jit(solution)/shard_map/ppermute | solution.py:30
  93.0 17.6 %collective-permute-start.18 = (bf16[256,1024]{1,0:T(8,128)(2,1)S(1)}, bf16[256,1024]{1,0:T(8,128)(2,1)S(1)}, u32[]{:S(2)}, u32[]{:S(2)}) collective-permute-start(bf16[256,1024]{1,0:T(8,128)(2,1)S(1)} %get-tuple-element.125), channel_id=1, source_target_pairs={{0,64},{16,80},{32,96},{48,112},{64,128},{80,144},{96,160},{112,17... | collective-permute-start | bytes 1572872 | tf_op jit(solution)/shard_map/ppermute | solution.py:30
  93.1 17.5 %collective-permute-start.19 = (bf16[256,1024]{1,0:T(8,128)(2,1)S(1)}, bf16[256,1024]{1,0:T(8,128)(2,1)S(1)}, u32[]{:S(2)}, u32[]{:S(2)}) collective-permute-start(bf16[256,1024]{1,0:T(8,128)(2,1)S(1)} %get-tuple-element.126), channel_id=1, source_target_pairs={{0,192},{16,208},{32,224},{48,240},{64,0},{80,16},{96,32},{112,48}... | collective-permute-start | bytes 1572872 | tf_op jit(solution)/shard_map/ppermute | solution.py:30
  117.2 20.4 %collective-permute-start.20 = (bf16[2,4,784,256]{3,2,1,0:T(8,128)(2,1)S(1)}, bf16[2,4,784,256]{3,2,1,0:T(8,128)(2,1)S(1)}, u32[]{:S(2)}, u32[]{:S(2)}) collective-permute-start(bf16[2,4,784,256]{3,2,1,0:T(8,128)(2,1)S(1)} %shard_map.156), channel_id=1, source_target_pairs={{0,1},{1,0},{2,3},{3,2},{4,5},{5,4},{6,7},{7,6},{8,9},{9,8},{10,11... | collective-permute-start | bytes 9633800 | tf_op jit(solution)/shard_map/ppermute | solution.py:39
  118.8 18.8 %collective-permute-start.21 = (bf16[512,256]{1,0:T(8,128)(2,1)S(1)}, bf16[512,256]{1,0:T(8,128)(2,1)S(1)}, u32[]{:S(2)}, u32[]{:S(2)}) collective-permute-start(bf16[512,256]{1,0:T(8,128)(2,1)S(1)} %get-tuple-element.138), channel_id=1, source_target_pairs={{0,64},{16,80},{32,96},{48,112},{64,128},{80,144},{96,160},{112,17... | collective-permute-start | bytes 786440 | tf_op jit(solution)/shard_map/ppermute | solution.py:30
  118.9 18.7 %collective-permute-start.22 = (bf16[512,256]{1,0:T(8,128)(2,1)S(1)}, bf16[512,256]{1,0:T(8,128)(2,1)S(1)}, u32[]{:S(2)}, u32[]{:S(2)}) collective-permute-start(bf16[512,256]{1,0:T(8,128)(2,1)S(1)} %get-tuple-element.139), channel_id=1, source_target_pairs={{0,192},{16,208},{32,224},{48,240},{64,0},{80,16},{96,32},{112,48}... | collective-permute-start | bytes 786440 | tf_op jit(solution)/shard_map/ppermute | solution.py:30
  138.6 53.3 %collective-permute-start.29 = (bf16[4,784,256]{2,1,0:T(8,128)(2,1)S(1)}, bf16[4,784,256]{2,1,0:T(8,128)(2,1)S(1)}, u32[]{:S(2)}, u32[]{:S(2)}) collective-permute-start(bf16[4,784,256]{2,1,0:T(8,128)(2,1)S(1)} %get-tuple-element.169), channel_id=1, source_target_pairs={{0,8},{1,9},{2,10},{3,11},{4,12},{5,13},{6,14},{7,15},{8,0},{9,1},... | collective-permute-start | bytes 4816904 | tf_op jit(solution)/shard_map/ppermute | solution.py:39
  148.9 22.4 %collective-permute-start.25 = (bf16[1024,256]{1,0:T(8,128)(2,1)S(1)}, bf16[1024,256]{1,0:T(8,128)(2,1)S(1)}, u32[]{:S(2)}, u32[]{:S(2)}) collective-permute-start(bf16[1024,256]{1,0:T(8,128)(2,1)S(1)} %get-tuple-element.157), channel_id=1, source_target_pairs={{0,64},{16,80},{32,96},{48,112},{64,128},{80,144},{96,160},{112,17... | collective-permute-start | bytes 1572872 | tf_op jit(solution)/shard_map/ppermute | solution.py:30
  148.9 22.4 %collective-permute-start.26 = (bf16[1024,256]{1,0:T(8,128)(2,1)S(1)}, bf16[1024,256]{1,0:T(8,128)(2,1)S(1)}, u32[]{:S(2)}, u32[]{:S(2)}) collective-permute-start(bf16[1024,256]{1,0:T(8,128)(2,1)S(1)} %get-tuple-element.158), channel_id=1, source_target_pairs={{0,192},{16,208},{32,224},{48,240},{64,0},{80,16},{96,32},{112,48}... | collective-permute-start | bytes 1572872 | tf_op jit(solution)/shard_map/ppermute | solution.py:30
  172.0 24.3 %collective-permute-start.32 = (bf16[2,1024,256]{2,1,0:T(8,128)(2,1)S(1)}, bf16[2,1024,256]{2,1,0:T(8,128)(2,1)S(1)}, u32[]{:S(2)}, u32[]{:S(2)}) collective-permute-start(bf16[2,1024,256]{2,1,0:T(8,128)(2,1)S(1)} %get-tuple-element.179), channel_id=1, source_target_pairs={{0,64},{16,80},{32,96},{48,112},{64,128},{80,144},{96,160},{112,17... | collective-permute-start | bytes 3145736 | tf_op jit(solution)/shard_map/ppermute | solution.py:30
  172.0 24.2 %collective-permute-start.33 = (bf16[2,1024,256]{2,1,0:T(8,128)(2,1)S(1)}, bf16[2,1024,256]{2,1,0:T(8,128)(2,1)S(1)}, u32[]{:S(2)}, u32[]{:S(2)}) collective-permute-start(bf16[2,1024,256]{2,1,0:T(8,128)(2,1)S(1)} %get-tuple-element.180), channel_id=1, source_target_pairs={{0,192},{16,208},{32,224},{48,240},{64,0},{80,16},{96,32},{112,48}... | collective-permute-start | bytes 3145736 | tf_op jit(solution)/shard_map/ppermute | solution.py:30
  174.7 17.3 %collective-permute-start.27 = (bf16[512,256]{1,0:T(8,128)(2,1)S(1)}, bf16[512,256]{1,0:T(8,128)(2,1)S(1)}, u32[]{:S(2)}, u32[]{:S(2)}) collective-permute-start(bf16[512,256]{1,0:T(8,128)(2,1)S(1)} %get-tuple-element.167), channel_id=1, source_target_pairs={{0,16},{16,32},{32,48},{48,0},{64,80},{80,96},{96,112},{112,64},{1... | collective-permute-start | bytes 786440 | tf_op jit(solution)/shard_map/ppermute | solution.py:34
  192.5 19.6 %collective-permute-start.30 = (bf16[2,784,256]{2,1,0:T(8,128)(2,1)S(1)}, bf16[2,784,256]{2,1,0:T(8,128)(2,1)S(1)}, u32[]{:S(2)}, u32[]{:S(2)}) collective-permute-start(bf16[2,784,256]{2,1,0:T(8,128)(2,1)S(1)} %get-tuple-element.172), channel_id=1, source_target_pairs={{0,4},{1,5},{2,6},{3,7},{4,0},{5,1},{6,2},{7,3},{8,12},{9,13},{10,... | collective-permute-start | bytes 2408456 | tf_op jit(solution)/shard_map/ppermute | solution.py:44
  199.4 18.9 %collective-permute-start.37 = (bf16[1024,256]{1,0:T(8,128)(2,1)S(1)}, bf16[1024,256]{1,0:T(8,128)(2,1)S(1)}, u32[]{:S(2)}, u32[]{:S(2)}) collective-permute-start(bf16[1024,256]{1,0:T(8,128)(2,1)S(1)} %get-tuple-element.195), channel_id=1, source_target_pairs={{0,16},{16,32},{32,48},{48,0},{64,80},{80,96},{96,112},{112,64},{1... | collective-permute-start | bytes 1572872 | tf_op jit(solution)/shard_map/ppermute | solution.py:34
  199.9 25.2 %collective-permute-start.38 = (bf16[1024,256]{1,0:T(8,128)(2,1)S(1)}, bf16[1024,256]{1,0:T(8,128)(2,1)S(1)}, u32[]{:S(2)}, u32[]{:S(2)}) collective-permute-start(bf16[1024,256]{1,0:T(8,128)(2,1)S(1)} %get-tuple-element.196), channel_id=1, source_target_pairs={{0,48},{16,0},{32,16},{48,32},{64,112},{80,64},{96,80},{112,96},{1... | collective-permute-start | bytes 1572872 | tf_op jit(solution)/shard_map/ppermute | solution.py:34
  (18 other events, 220.1 us)

commit v4 on v3

--- a/solution.py
+++ b/solution.py
@@ -60,7 +60,7 @@
     return jax.ShapeDtypeStruct(shape, dtype)
 
 
-def call(kernel, args, outs, scalars=(), scratch=(), flops=0, moved=0, vmem=8):
+def call(kernel, args, outs, scalars=(), scratch=(), flops=0, moved=0, vmem=8, aliases=()):
     spec = pl.BlockSpec(memory_space=pltpu.VMEM)
     return pl.pallas_call(
         kernel,
@@ -68,6 +68,7 @@
         out_specs=[spec] * len(outs),
         out_shape=outs,
         scratch_shapes=scratch,
+        input_output_aliases=dict(aliases),
         compiler_params=pltpu.CompilerParams(vmem_limit_bytes=vmem * MIB),
         cost_estimate=pl.CostEstimate(flops=COST * flops, bytes_accessed=moved, transcendentals=0),
     )(*scalars, *args)
@@ -183,7 +184,7 @@
     for piece in (own_ref, other_ref):
 
         def add_squares(k, total, piece=piece):
-            hidden = piece[lax.div(k, 2), lax.rem(k, 2), :tokens].astype(F32)
+            hidden = piece[lax.div(k, 4), lax.rem(k, 4), :tokens].astype(F32)
             return total + jnp.sum(hidden * hidden, axis=1, keepdims=True)
 
         square = lax.fori_loop(0, 8, add_squares, square)
@@ -193,15 +194,15 @@
     for n, piece in enumerate((own_ref, other_ref)):
 
         def write(k, carry, n=n, piece=piece):
-            x, z = lax.div(k, 2), lax.rem(k, 2)
+            z, x = lax.div(k, 4), lax.rem(k, 4)
             place = lax.rem(a + z, 2) * 8 + lax.rem(b + 4 - x, 4) * 2 + lax.rem(c + n, 2)
-            normed_ref[place] = (piece[x, z, :tokens].astype(F32) * inv_ref[:, :1]).astype(BF)
-            rows = piece[x, z, tokens : 2 * tokens]
+            normed_ref[place] = (piece[z, x, :tokens].astype(F32) * inv_ref[:, :1]).astype(BF)
+            rows = piece[z, x, tokens : 2 * tokens]
             masked_ref[place] = jnp.where(keep, rows.astype(F32), 0.0).astype(BF)
             start = pl.multiple_of(place * erows, erows)
             for m in range(NB):
                 line = 2 * tokens + m * erows
-                enc_ref[m, pl.ds(start, erows), :] = piece[x, z, line : line + erows]
+                enc_ref[m, pl.ds(start, erows), :] = piece[z, x, line : line + erows]
             return carry
 
         lax.fori_loop(0, 8, write, 0)
@@ -225,14 +226,14 @@
     return q_grad, k_grad, v_grad, attended, stat
 
 
-def project(places, pieces, normed_ref, masked_ref, enc_ref, stack_ref, init):
+def project(places, pieces, normed_ref, masked_ref, enc_ref, stack_ref, init, first=0):
     width = stack_ref.shape[2] // 4
     for n, piece in enumerate(pieces):
-        stack_ref[n] = piece()
+        stack_ref[first + n] = piece()
     out = init
     for n in range(0, len(pieces), 4):
         group = places[n : n + 4]
-        rows = jnp.concatenate([stack_ref[n + k] for k in range(4)], axis=0)
+        rows = jnp.concatenate([stack_ref[first + n + k] for k in range(4)], axis=0)
         normed, enc, masked = (
             jnp.concatenate([ref[p] for p in group], axis=1)
             for ref in (normed_ref, enc_ref, masked_ref)
@@ -271,19 +272,32 @@
     pair, high, low, across_b, across_a, acc_in, acc_ref, stack_ref = refs
     pieces = [at(pair, 0), at(high, 0), one(across_b), at(low, 0)]
     pieces += [at(pair, 1), at(high, 1), one(across_a), at(low, 1)]
-    places = blocks_at(3) + blocks_at(1)
-    init = [acc_in[n] for n in range(4)]
-    acc = project(places, pieces, normed_ref, masked_ref, enc_ref, stack_ref, init)
+    width = stack_ref.shape[2] // 4
+    for n, piece in enumerate(pieces):
+        stack_ref[n] = piece()
     for n in range(4):
-        acc_ref[n] = acc[n]
+        acc_ref[n] = acc_in[n]
+
+    def body(group, carry):
+        places = [dp_block(dy, 3 - 2 * group) for dy in range(4)]
+        rows = jnp.concatenate([stack_ref[4 * group + k] for k in range(4)], axis=0)
+        normed, enc, masked = (
+            jnp.concatenate([ref[p] for p in places], axis=1)
+            for ref in (normed_ref, enc_ref, masked_ref)
+        )
+        for n, left in enumerate((normed, enc, enc, masked)):
+            acc_ref[n] += nn(left, rows[:, n * width : (n + 1) * width])
+        return carry
+
+    lax.fori_loop(0, 2, body, 0)
 
 
 def far_kernel(scale, len_ref, normed_ref, masked_ref, enc_ref, *refs):
     far, high, low, across_low, across_high, acc_in = refs[:6]
-    kv_ref, qgt_ref, kvt_ref, att_ref, stat_ref, stack_ref = refs[6:]
+    kv_ref, qgt_ref, kvt_ref, att_ref, stat_ref, stack_ref = refs[7:]
     pieces = [one(far), one(high), both(across_low, across_high), one(low)]
     init = [acc_in[n] for n in range(4)]
-    acc = project(blocks_at(2), pieces, normed_ref, masked_ref, enc_ref, stack_ref, init)
+    acc = project(blocks_at(2), pieces, normed_ref, masked_ref, enc_ref, stack_ref, init, 4)
     out = attention(scale, len_ref[0], *(value.astype(BF) for value in acc))
     q_grad, k_grad, v_grad, attended, stat = out
     width = q_grad.shape[1]
@@ -299,27 +313,31 @@
 
 def weight_grad_kernel(dz, normed_ref, masked_ref, enc_ref, *refs):
     qgt_ref, kvt_ref, att_ref = refs[:3]
-    outs = list(refs[3:])
+    outs, held = refs[3:-1], refs[-1]
     width = qgt_ref.shape[0]
-    for n in range(4):
+    targets = [outs[0], outs[1], outs[2:-1], outs[-1]]
+
+    def body(n, carry):
         place = dp_block(n, dz)
-        query = nn(qgt_ref[...], normed_ref[place]).astype(BF)
-        pair = nn(kvt_ref[...], enc_ref[place]).astype(BF)
-        attn = nn(att_ref[...], masked_ref[place]).astype(BF)
-        if n == 2 and len(outs) == 3:
-            low, high = outs.pop(0), outs.pop(0)
-            low[:width] = query
-            low[width:] = pair[:width]
-            high[:width] = pair[width:]
-            high[width:] = attn
-        else:
-            out = outs.pop(0)
-            out[:width] = query
-            out[width : 3 * width] = pair
-            out[3 * width :] = attn
-
-
-def partial_kernel(side, q_t_ref, kv_ref, at_t_ref, stat_ref, own, near, far, out, kv_buf):
+        held[:width] = nn(qgt_ref[...], normed_ref[place]).astype(BF)
+        held[width : 3 * width] = nn(kvt_ref[...], enc_ref[place]).astype(BF)
+        held[3 * width :] = nn(att_ref[...], masked_ref[place]).astype(BF)
+        for k, target in enumerate(targets):
+
+            @pl.when(n == k)
+            def _():
+                parts = target if isinstance(target, tuple) else (target,)
+                first = 0
+                for part in parts:
+                    part[...] = held[first : first + part.shape[0]]
+                    first += part.shape[0]
+
+        return carry
+
+    lax.fori_loop(0, 4, body, 0)
+
+
+def partial_kernel(side, q_t_ref, kv_ref, at_t_ref, stat_ref, even, odd, out, kv_buf):
     width, tokens = q_t_ref.shape
     erows = kv_ref.shape[0] // NB
     a, b, c = mp_place()
@@ -335,7 +353,7 @@
     def block_of(n, shifts):
         return dp_block(lax.rem(n, 4), jnp.where(n < 4, shifts[0], shifts[1]))
 
-    stacks = ((own, (0, 0)), (near, (3, 1)), (far, (2, 2)))
+    stacks = ((even, (0, 2)), (odd, (3, 1)))
     for stack, shifts in stacks:
 
         def enc_part(n, carry, stack=stack, shifts=shifts):
@@ -349,10 +367,10 @@
 
         lax.fori_loop(0, stack.shape[0], enc_part, 0, unroll=2)
 
-    odd = lax.rem(lax.axis_index("dp") + core, 2)
+    last = lax.rem(lax.axis_index("dp") + core, 2)
     for stack, shifts in stacks:
 
-        @pl.when(odd == shifts[0] % 2)
+        @pl.when(last == shifts[0] % 2)
         def _():
             def parts(n, carry):
                 place = block_of(n, shifts)
@@ -386,13 +404,22 @@
 
 def core_sum_kernel(keep_ref, got_ref, *outs):
     for z, out in enumerate(outs):
-        for x in range(4):
+
+        def body(x, carry, z=z, out=out):
             add_rows([keep_ref.at[z, x], got_ref.at[z, x]], out.at[x])
-
-
-def z_sum_kernel(keep_ref, got_ref, near_ref, far_ref):
-    for x, out in enumerate((near_ref.at[0], near_ref.at[1], far_ref.at[0], far_ref.at[1])):
-        add_rows([keep_ref.at[x], got_ref.at[x]], out)
+            return carry
+
+        lax.fori_loop(0, 4, body, 0)
+
+
+def z_sum_kernel(keep_ref, got_ref, *outs):
+    for n, out in enumerate(outs):
+
+        def body(x, carry, n=n, out=out):
+            add_rows([keep_ref.at[2 * n + x], got_ref.at[2 * n + x]], out.at[x])
+            return carry
+
+        lax.fori_loop(0, 2, body, 0)
 
 
 def x_sum_kernel(first_ref, second_ref, *outs):
@@ -442,28 +469,31 @@
 
 
 def gather(block, acts, begin):
+    x1, x3 = send_mp(acts, 0, 1, 0), send_mp(acts, 0, 3, 0)
     before, behind = send_z(block, 1), send_z(block, -1)
     low, high = send_y(block, 1), send_y(block, -1)
-    other = send_mp(acts, 1, 0, 0)
-    other, again = after((other, block), low, high)
-    pair_acts = stack_pair(acts, other)
-    x1, x3 = send_mp(pair_acts, 0, 1, 0), send_mp(pair_acts, 0, 3, 0)
+    x1, x3, to_x2, again = after((x1, x3, acts, block), low, high)
+    x2 = send_mp(to_x2, 0, 2, 0)
     across = send_y(again, 2)
 
-    pair_acts, x1, x3, before, behind = after((pair_acts, x1, x3, before, behind), across)
-    x2 = send_mp(pair_acts, 0, 2, 0)
+    x1, x2, x3, before, behind = after((x1, x2, x3, before, behind), across)
+    (quad,) = call(quad_kernel, (acts, x1, x2, x3), [shape_of((4,) + acts.shape)])
     pair = stack_pair(before, behind)
     pair_low, pair_high = send_y(pair, 1), send_y(pair, -1)
     to_low, to_high = halves(before, behind)
     far_low, far_high = send_z(to_low, 1), send_z(to_high, -1)
+    (to_other,) = after((quad,), far_low, far_high)
+    other = send_mp(to_other, 1, 0, 0)
+
+    pair_low, pair_high, far_low, far_high = after((pair_low, pair_high, far_low, far_high))
     (far,) = call(join_kernel, (far_low, far_high), [shape_of(block.shape)])
     f_low, f_high = send_y(far, 1), send_y(far, -1)
-
-    x2, pair_low, pair_high, f_low, f_high = after((x2, pair_low, pair_high, f_low, f_high))
-    (line,) = call(quad_kernel, (pair_acts, x1, x2, x3), [shape_of((4,) + pair_acts.shape)])
-    sibling = send_mp(line, 0, 0, 1)
     to_low, to_high = call(pick_kernel, (pair_low, pair_high), [shape_of(block.shape)] * 2)
     across_b, across_a = send_y(to_low, 1), send_y(to_high, -1)
+
+    quad, other, f_low, f_high = after((quad, other, f_low, f_high), across_a, across_b)
+    (line,) = call(pair_kernel, (quad, other), [shape_of((2,) + quad.shape)])
+    sibling = send_mp(line, 0, 0, 1)
     to_low, to_high = halves(f_low, f_high)
     last_low, last_high = send_y(to_low, 1), send_y(to_high, -1)
     return (
@@ -510,13 +540,10 @@
 def far_kernel_sum(far1, far3, low, high, out1, out3):
     half = low.shape[0]
     for ref, part, out, first in ((far1, low, out1, 0), (far3, high, out3, half)):
-        for begin in range(0, 2 * half, CHUNK):
-            rows = slice(begin, begin + CHUNK)
-            if first <= begin < first + half:
-                other = part[begin - first : begin - first + CHUNK].astype(F32)
-                out[rows] = (ref[rows].astype(F32) + other).astype(BF)
-            else:
-                out[rows] = ref[rows]
+        rest = slice(half - first, 2 * half - first)
+        out[rest] = ref[rest]
+        here = ref.at[first : first + half]
+        summed(out.at[first : first + half], put_plain, plain(here), plain(part))
 
 
 def second_sum_kernel(far0, far1, far3, bf1, bf2, bf3, bh1, bh2, bh3, up, down, far_low, far_high):
@@ -630,7 +657,7 @@
         compiler_params=pltpu.CompilerParams(vmem_limit_bytes=56 * MIB),
     )(query_weight, key_weight, value_weight, output_weight, dec_input, cotangent, enc_output)
     acc_shape = shape_of((4, tokens, width), F32)
-    stack_shape = shape_of((4, feat, 4 * width))
+    stack_shape = shape_of((8, feat, 4 * width))
 
     def begin(pieces, own_group):
         normed, masked, encoded, inv_rms = call(
@@ -651,17 +678,17 @@
     normed, masked, encoded, inv_rms, own_stack, acc = start
     stacked = (normed, masked, encoded)
     acc, near_stack = call(
-        near_kernel, (*stacked, *near_group, acc), [acc_shape, shape_of((8, feat, 4 * width))],
+        near_kernel, (*stacked, *near_group, acc), [acc_shape, stack_shape],
         flops=32 * unit, moved=8 * MIB,
     )
     kshape = shape_of((keys, 2 * width))
-    kv_grad, q_t, kv_t, at_t, stat, far_stack = call(
-        functools.partial(far_kernel, scale), (*stacked, *far_group, acc),
+    kv_grad, q_t, kv_t, at_t, stat, even_stack = call(
+        functools.partial(far_kernel, scale), (*stacked, *far_group, acc, own_stack),
         [
             kshape, shape_of((width, tokens)), shape_of((2 * width, keys)),
             shape_of((width, tokens)), shape_of((EXTRA, tokens)), stack_shape,
         ],
-        (enc_lengths,), flops=24 * unit, moved=4 * MIB,
+        (enc_lengths,), flops=24 * unit, moved=4 * MIB, aliases=((10, 5),),
     )
 
     def grads(dz, others):
@@ -670,14 +697,14 @@
         outs = [full, full, part, part, full] if dz == 2 else [full] * 4
         return call(
             functools.partial(weight_grad_kernel, dz), (normed_in, masked, encoded, q_t, kv_t, at_t),
-            outs, flops=16 * unit, moved=4 * MIB,
+            outs, scratch=[pltpu.VMEM((4 * width, feat), BF)], flops=16 * unit, moved=4 * MIB,
         )
 
     def partials(side):
         out = shape_of((2, 4, 3 * tokens + EXTRA, feat))
         return call(
             functools.partial(partial_kernel, side),
-            (q_t, kv_grad, at_t, stat, own_stack, near_stack, far_stack),
+            (q_t, kv_grad, at_t, stat, even_stack, near_stack),
             [out], scratch=[pltpu.VMEM((keys // 2, 2 * width), BF)], flops=32 * unit, moved=14 * MIB,
         )[0]
 

time: 231 us -> 217 us (0.939); the launches traced: 228 us -> 217 us
  starting transfers between devices: 71.3 us -> 64.3 us
  Pallas kernels: 35.4 us -> 29.1 us
  waiting for transfers between devices: 117 us -> 121 us
    ppermute x22, waiting for transfers between devices: 57.1 us -> 43.4 us  [send_y(): lax.ppermute(value, 'dp', [(dp_index(y, z), dp_index(y + d, z)) for y, z...]
    ppermute x7, waiting for transfers between devices: 7.85 us -> 17.9 us  [send_mp(): return lax.ppermute(value, 'mp', pairs)]
    ppermute x7, starting transfers between devices: 22.6 us -> 12.6 us  [send_mp(): return lax.ppermute(value, 'mp', pairs)]
    ppermute x8, waiting for transfers between devices: 50.3 us -> 57.1 us  [send_z(): lax.ppermute(value, 'dp', [(dp_index(y, z), dp_index(y, z + d)) for y, z...]
    pallas_call x23, Pallas kernels: 31 us -> 24.6 us  [call(): pl.pallas_call(kernel, in_specs=[pl.BlockSpec(memory_space=pltpu.SMEM)] *...]
  transfers between devices with their start and end apart: 39 -> 39, of which waited for: 17 -> 20; matrix products, arithmetic and copies ran while one was open for 0% -> 0% of each run, Pallas kernels for 11% -> 9%
where the time goes in v4:
time: 217 us
  waiting for transfers between devices  121 us (56%)
  starting transfers between devices  64.3 us (30%)
  Pallas kernels  29.1 us (13%)
  between operations  2.42 us (1%)
    ppermute x8, waiting for transfers between devices, send_z(): lax.ppermute(value, 'dp', [(dp_index(y, z), dp_index(y, z + d)) for y, z...  57.1 us
    ppermute x22, waiting for transfers between devices, send_y(): lax.ppermute(value, 'dp', [(dp_index(y, z), dp_index(y + d, z)) for y, z...  43.4 us
    ppermute x22, starting transfers between devices, send_y(): lax.ppermute(value, 'dp', [(dp_index(y, z), dp_index(y + d, z)) for y, z...  28.3 us
    pallas_call x23, Pallas kernels, call(): pl.pallas_call(kernel, in_specs=[pl.BlockSpec(memory_space=pltpu.SMEM)] *...  24.6 us
    ppermute x8, starting transfers between devices, send_z(): lax.ppermute(value, 'dp', [(dp_index(y, z), dp_index(y, z + d)) for y, z...  19.9 us
    ppermute x7, waiting for transfers between devices, send_mp(): return lax.ppermute(value, 'mp', pairs)  17.9 us
    ppermute x7, starting transfers between devices, send_mp(): return lax.ppermute(value, 'mp', pairs)  12.6 us
  transfers between devices with their start and end apart: 39, of which 20 were waited for; matrix products, arithmetic and copies ran while one was open for 0% of the time, Pallas kernels for 9%

profile of v4, /device:TPU:1, one launch (start us, length us, event | category | flops | bytes accessed | tf_op | source)
XLA Modules:
  0.0 216.5 jit_solution(8044094627669894919)
XLA Ops:
  2.9 3.6 %collective-permute-start.1 = (bf16[256,1024]{1,0:T(8,128)(2,1)}, bf16[256,1024]{1,0:T(8,128)(2,1)S(1)}, u32[]{:S(2)}, u32[]{:S(2)}) collective-permute-start(bf16[256,1024]{1,0:T(8,128)(2,1)} %get-tuple-element.112.refs_0_), channel_id=1, source_target_pairs={{0,192},{16,208},{32,224},{48,240},{64,0},{80,16},{96,32},{112,48}... | collective-permute-start | bytes 1572872 | tf_op jit(solution)/shard_map/ppermute | solution.py:30
  9.0 6.0 %collective-permute-start.7 = (bf16[256,1024]{1,0:T(8,128)(2,1)}, bf16[256,1024]{1,0:T(8,128)(2,1)S(1)}, u32[]{:S(2)}, u32[]{:S(2)}) collective-permute-start(bf16[256,1024]{1,0:T(8,128)(2,1)} %get-tuple-element.112.refs_0_), channel_id=1, source_target_pairs={{0,48},{16,0},{32,16},{48,32},{64,112},{80,64},{96,80},{112,96},{1... | collective-permute-start | bytes 1572872 | tf_op jit(solution)/shard_map/ppermute | solution.py:34
  16.8 3.0 %collective-permute-start.6 = (bf16[256,1024]{1,0:T(8,128)(2,1)}, bf16[256,1024]{1,0:T(8,128)(2,1)S(1)}, u32[]{:S(2)}, u32[]{:S(2)}) collective-permute-start(bf16[256,1024]{1,0:T(8,128)(2,1)} %get-tuple-element.112.refs_0_), channel_id=1, source_target_pairs={{0,16},{16,32},{32,48},{48,0},{64,80},{80,96},{96,112},{112,64},{1... | collective-permute-start | bytes 1572872 | tf_op jit(solution)/shard_map/ppermute | solution.py:34
  23.6 11.2 %collective-permute-done.7.second = bf16[256,1024]{1,0:T(8,128)(2,1)S(1)} collective-permute-done((bf16[256,1024]{1,0:T(8,128)(2,1)}, bf16[256,1024]{1,0:T(8,128)(2,1)S(1)}, u32[]{:S(2)}, u32[]{:S(2)}) %collective-permute-start.7) | collective-permute-done | bytes 524320 | tf_op jit(solution)/shard_map/ppermute | solution.py:34
  43.5 7.0 %collective-permute-done.10.first = bf16[128,1024]{1,0:T(8,128)(2,1)S(1)} collective-permute-done((bf16[128,1024]{1,0:T(8,128)(2,1)S(1)}, bf16[128,1024]{1,0:T(8,128)(2,1)S(1)}, u32[]{:S(2)}, u32[]{:S(2)}) %collective-permute-start.10) | collective-permute-done | bytes 262176 | tf_op jit(solution)/shard_map/ppermute | solution.py:34
  50.5 11.2 %collective-permute-done.11.second = bf16[128,1024]{1,0:T(8,128)(2,1)S(1)} collective-permute-done((bf16[128,1024]{1,0:T(8,128)(2,1)S(1)}, bf16[128,1024]{1,0:T(8,128)(2,1)S(1)}, u32[]{:S(2)}, u32[]{:S(2)}) %collective-permute-start.11) | collective-permute-done | bytes 262176 | tf_op jit(solution)/shard_map/ppermute | solution.py:34
  64.9 7.1 %collective-permute-done.16.second.refs_1_ = bf16[256,1024]{1,0:T(8,128)(2,1)S(1)} collective-permute-done((bf16[256,1024]{1,0:T(8,128)(2,1)S(1)}, bf16[256,1024]{1,0:T(8,128)(2,1)S(1)}, u32[]{:S(2)}, u32[]{:S(2)}) %collective-permute-start.16) | collective-permute-done | bytes 524320 | tf_op jit(solution)/shard_map/ppermute | solution.py:30
  72.0 3.1 %collective-permute-done.15.first.refs_2_ = bf16[256,1024]{1,0:T(8,128)(2,1)S(1)} collective-permute-done((bf16[256,1024]{1,0:T(8,128)(2,1)S(1)}, bf16[256,1024]{1,0:T(8,128)(2,1)S(1)}, u32[]{:S(2)}, u32[]{:S(2)}) %collective-permute-start.15) | collective-permute-done | bytes 524320 | tf_op jit(solution)/shard_map/ppermute | solution.py:30
  75.1 3.9 %collective-permute-done.12.refs_4_ = bf16[256,1024]{1,0:T(8,128)(2,1)S(1)} collective-permute-done((bf16[256,1024]{1,0:T(8,128)(2,1)S(1)}, bf16[256,1024]{1,0:T(8,128)(2,1)S(1)}, u32[]{:S(2)}, u32[]{:S(2)}) %collective-permute-start.12) | collective-permute-done | bytes 524320 | tf_op jit(solution)/shard_map/ppermute | solution.py:30
  79.0 3.1 %collective-permute-done.13.refs_3_ = bf16[256,1024]{1,0:T(8,128)(2,1)S(1)} collective-permute-done((bf16[256,1024]{1,0:T(8,128)(2,1)S(1)}, bf16[256,1024]{1,0:T(8,128)(2,1)S(1)}, u32[]{:S(2)}, u32[]{:S(2)}) %collective-permute-start.13) | collective-permute-done | bytes 524320 | tf_op jit(solution)/shard_map/ppermute | solution.py:30
  82.2 15.0 %collective-permute-done.14.second = bf16[4,768,256]{2,1,0:T(8,128)(2,1)S(1)} collective-permute-done((bf16[4,768,256]{2,1,0:T(8,128)(2,1)S(1)}, bf16[4,768,256]{2,1,0:T(8,128)(2,1)S(1)}, u32[]{:S(2)}, u32[]{:S(2)}) %collective-permute-start.14) | collective-permute-done | bytes 1572896 | tf_op jit(solution)/shard_map/ppermute | solution.py:39
  104.1 3.6 %shard_map.151 = (bf16[16,256,256]{2,1,0:T(8,128)(2,1)S(1)}, bf16[16,256,256]{2,1,0:T(8,128)(2,1)S(1)}, bf16[16,256,256]{2,1,0:T(8,128)(2,1)S(1)}, f32[256,128]{1,0:T(8,128)S(1)}) custom-call(s32[1]{0:T(128)S(6)} %copy.19.len_ref.refs_0_, bf16[2,4,768,256]{3,2,1,0:T(8,128)(2,1)S(1)} %shard_map.150.own_ref, ...), custom_call_target="tpu_custom_call" | custom-call | bytes 12582912 | tf_op jit(solution)/shard_map/pallas_call | solution.py:65
  111.7 3.8 %shard_map.156 = bf16[2,4,784,256]{3,2,1,0:T(8,128)(2,1)S(1)} custom-call(bf16[256,256]{1,0:T(8,128)(2,1)S(1)} %get-tuple-element.142.q_t_ref.refs_0_, bf16[256,512]{1,0:T(8,128)(2,1)S(1)} %get-tuple-element.143.kv_ref, bf16[256,256]{1,0:T(8,128)(2,1)S(1)} %get-tuple-element.144.at_t_ref.refs_2_, bf16[16,256]{1,0:T(8,128)(2,1)S(1)} %get-tuple-element.145.stat_ref, ...), custom_call_target="tpu_custom_call" | custom-call | flops 17179869184 | bytes 14680064 | tf_op jit(solution)/shard_map/pallas_call | solution.py:65
  117.5 2.7 %collective-permute-start.22 = (bf16[512,256]{1,0:T(8,128)(2,1)S(1)}, bf16[512,256]{1,0:T(8,128)(2,1)S(1)}, u32[]{:S(2)}, u32[]{:S(2)}) collective-permute-start(bf16[512,256]{1,0:T(8,128)(2,1)S(1)} %get-tuple-element.151), channel_id=1, source_target_pairs={{0,192},{16,208},{32,224},{48,240},{64,0},{80,16},{96,32},{112,48}... | collective-permute-start | bytes 786440 | tf_op jit(solution)/shard_map/ppermute | solution.py:30
  123.0 3.8 %shard_map.157.keep_ref = bf16[2,4,784,256]{3,2,1,0:T(8,128)(2,1)S(1)} custom-call(bf16[256,256]{1,0:T(8,128)(2,1)S(1)} %get-tuple-element.142.q_t_ref.refs_0_, bf16[256,512]{1,0:T(8,128)(2,1)S(1)} %get-tuple-element.143.kv_ref, bf16[256,256]{1,0:T(8,128)(2,1)S(1)} %get-tuple-element.144.at_t_ref.refs_2_, bf16[16,256]{1,0:T(8,128)(2,1)S(1)} %get-tuple-element.145.stat_ref, ...), custom_call_target="tpu_custom_call" | custom-call | flops 17179869184 | bytes 14680064 | tf_op jit(solution)/shard_map/pallas_call | solution.py:65
  129.4 5.8 %collective-permute-start.29 = (bf16[4,784,256]{2,1,0:T(8,128)(2,1)S(1)}, bf16[4,784,256]{2,1,0:T(8,128)(2,1)S(1)}, u32[]{:S(2)}, u32[]{:S(2)}) collective-permute-start(bf16[4,784,256]{2,1,0:T(8,128)(2,1)S(1)} %get-tuple-element.181), channel_id=1, source_target_pairs={{0,8},{1,9},{2,10},{3,11},{4,12},{5,13},{6,14},{7,15},{8,0},{9,1},... | collective-permute-start | bytes 4816904 | tf_op jit(solution)/shard_map/ppermute | solution.py:39
  138.4 2.7 %collective-permute-start.26 = (bf16[1024,256]{1,0:T(8,128)(2,1)S(1)}, bf16[1024,256]{1,0:T(8,128)(2,1)S(1)}, u32[]{:S(2)}, u32[]{:S(2)}) collective-permute-start(bf16[1024,256]{1,0:T(8,128)(2,1)S(1)} %get-tuple-element.170), channel_id=1, source_target_pairs={{0,192},{16,208},{32,224},{48,240},{64,0},{80,16},{96,32},{112,48}... | collective-permute-start | bytes 1572872 | tf_op jit(solution)/shard_map/ppermute | solution.py:30
  141.1 8.3 %collective-permute-done.23.far1 = bf16[1024,256]{1,0:T(8,128)(2,1)S(1)} collective-permute-done((bf16[1024,256]{1,0:T(8,128)(2,1)S(1)}, bf16[1024,256]{1,0:T(8,128)(2,1)S(1)}, u32[]{:S(2)}, u32[]{:S(2)}) %collective-permute-start.23) | collective-permute-done | bytes 524320 | tf_op jit(solution)/shard_map/ppermute | solution.py:30
  149.3 11.2 %collective-permute-done.25.bf2 = bf16[1024,256]{1,0:T(8,128)(2,1)S(1)} collective-permute-done((bf16[1024,256]{1,0:T(8,128)(2,1)S(1)}, bf16[1024,256]{1,0:T(8,128)(2,1)S(1)}, u32[]{:S(2)}, u32[]{:S(2)}) %collective-permute-start.25) | collective-permute-done | bytes 524320 | tf_op jit(solution)/shard_map/ppermute | solution.py:30
  164.0 3.6 %collective-permute-start.28 = (bf16[512,256]{1,0:T(8,128)(2,1)S(1)}, bf16[512,256]{1,0:T(8,128)(2,1)S(1)}, u32[]{:S(2)}, u32[]{:S(2)}) collective-permute-start(bf16[512,256]{1,0:T(8,128)(2,1)S(1)} %get-tuple-element.180), channel_id=1, source_target_pairs={{0,48},{16,0},{32,16},{48,32},{64,112},{80,64},{96,80},{112,96},{1... | collective-permute-start | bytes 786440 | tf_op jit(solution)/shard_map/ppermute | solution.py:34
  167.5 13.6 %collective-permute-done.27.low = bf16[512,256]{1,0:T(8,128)(2,1)S(1)} collective-permute-done((bf16[512,256]{1,0:T(8,128)(2,1)S(1)}, bf16[512,256]{1,0:T(8,128)(2,1)S(1)}, u32[]{:S(2)}, u32[]{:S(2)}) %collective-permute-start.27) | collective-permute-done | bytes 262176 | tf_op jit(solution)/shard_map/ppermute | solution.py:34
  192.1 4.9 %collective-permute-done.34.refs_1_ = bf16[1024,256]{1,0:T(8,128)(2,1)S(1)} collective-permute-done((bf16[1024,256]{1,0:T(8,128)(2,1)S(1)}, bf16[1024,256]{1,0:T(8,128)(2,1)S(1)}, u32[]{:S(2)}, u32[]{:S(2)}) %collective-permute-start.34) | collective-permute-done | bytes 524320 | tf_op jit(solution)/shard_map/ppermute | solution.py:30
  202.4 7.5 %collective-permute-done.37.refs_4_ = bf16[1024,256]{1,0:T(8,128)(2,1)S(1)} collective-permute-done((bf16[1024,256]{1,0:T(8,128)(2,1)S(1)}, bf16[1024,256]{1,0:T(8,128)(2,1)S(1)}, u32[]{:S(2)}, u32[]{:S(2)}) %collective-permute-start.37) | collective-permute-done | bytes 524320 | tf_op jit(solution)/shard_map/ppermute | solution.py:34
  209.9 4.2 %collective-permute-done.38.refs_5_ = bf16[1024,256]{1,0:T(8,128)(2,1)S(1)} collective-permute-done((bf16[1024,256]{1,0:T(8,128)(2,1)S(1)}, bf16[1024,256]{1,0:T(8,128)(2,1)S(1)}, u32[]{:S(2)}, u32[]{:S(2)}) %collective-permute-start.38) | collective-permute-done | bytes 524320 | tf_op jit(solution)/shard_map/ppermute | solution.py:34
  (84 shorter events, 64.3 us)
Async XLA Ops:
  2.9 16.9 %collective-permute-start.1 = (bf16[256,1024]{1,0:T(8,128)(2,1)}, bf16[256,1024]{1,0:T(8,128)(2,1)S(1)}, u32[]{:S(2)}, u32[]{:S(2)}) collective-permute-start(bf16[256,1024]{1,0:T(8,128)(2,1)} %get-tuple-element.112.refs_0_), channel_id=1, source_target_pairs={{0,192},{16,208},{32,224},{48,240},{64,0},{80,16},{96,32},{112,48}... | collective-permute-start | bytes 1572872 | tf_op jit(solution)/shard_map/ppermute | solution.py:30
  9.0 25.7 %collective-permute-start.7 = (bf16[256,1024]{1,0:T(8,128)(2,1)}, bf16[256,1024]{1,0:T(8,128)(2,1)S(1)}, u32[]{:S(2)}, u32[]{:S(2)}) collective-permute-start(bf16[256,1024]{1,0:T(8,128)(2,1)} %get-tuple-element.112.refs_0_), channel_id=1, source_target_pairs={{0,48},{16,0},{32,16},{48,32},{64,112},{80,64},{96,80},{112,96},{1... | collective-permute-start | bytes 1572872 | tf_op jit(solution)/shard_map/ppermute | solution.py:34
  16.8 20.4 %collective-permute-start.6 = (bf16[256,1024]{1,0:T(8,128)(2,1)}, bf16[256,1024]{1,0:T(8,128)(2,1)S(1)}, u32[]{:S(2)}, u32[]{:S(2)}) collective-permute-start(bf16[256,1024]{1,0:T(8,128)(2,1)} %get-tuple-element.112.refs_0_), channel_id=1, source_target_pairs={{0,16},{16,32},{32,48},{48,0},{64,80},{80,96},{96,112},{112,64},{1... | collective-permute-start | bytes 1572872 | tf_op jit(solution)/shard_map/ppermute | solution.py:34
  20.4 16.8 %collective-permute-start.4 = (bf16[256,1024]{1,0:T(8,128)(2,1)}, bf16[256,1024]{1,0:T(8,128)(2,1)S(1)}, u32[]{:S(2)}, u32[]{:S(2)}) collective-permute-start(bf16[256,1024]{1,0:T(8,128)(2,1)} %get-tuple-element.112.refs_0_), channel_id=1, source_target_pairs={{0,128},{16,144},{32,160},{48,176},{64,192},{80,208},{96,224},{112... | collective-permute-start | bytes 1572872 | tf_op jit(solution)/shard_map/ppermute | solution.py:30
  21.3 15.9 %collective-permute-start.5 = (bf16[768,256]{1,0:T(8,128)(2,1)}, bf16[768,256]{1,0:T(8,128)(2,1)S(1)}, u32[]{:S(2)}, u32[]{:S(2)}) collective-permute-start(bf16[768,256]{1,0:T(8,128)(2,1)} %get-tuple-element.114.refs_0_.refs_3_), channel_id=1, source_target_pairs={{0,4},{1,5},{2,6},{3,7},{4,0},{5,1},{6,2},{7,3},{8,12},{9,13},{10,... | collective-permute-start | bytes 1179656 | tf_op jit(solution)/shard_map/ppermute | solution.py:39
  39.4 22.3 %collective-permute-start.11 = (bf16[128,1024]{1,0:T(8,128)(2,1)S(1)}, bf16[128,1024]{1,0:T(8,128)(2,1)S(1)}, u32[]{:S(2)}, u32[]{:S(2)}) collective-permute-start(bf16[128,1024]{1,0:T(8,128)(2,1)S(1)} %get-tuple-element.119), channel_id=1, source_target_pairs={{0,48},{16,0},{32,16},{48,32},{64,112},{80,64},{96,80},{112,96},{1... | collective-permute-start | bytes 786440 | tf_op jit(solution)/shard_map/ppermute | solution.py:34
  41.0 20.7 %collective-permute-start.9 = (bf16[2,256,1024]{2,1,0:T(8,128)(2,1)S(1)}, bf16[2,256,1024]{2,1,0:T(8,128)(2,1)S(1)}, u32[]{:S(2)}, u32[]{:S(2)}) collective-permute-start(bf16[2,256,1024]{2,1,0:T(8,128)(2,1)S(1)} %shard_map.145.refs_0_), channel_id=1, source_target_pairs={{0,192},{16,208},{32,224},{48,240},{64,0},{80,16},{96,32},{112,48}... | collective-permute-start | bytes 3145736 | tf_op jit(solution)/shard_map/ppermute | solution.py:30
  43.4 18.3 %collective-permute-start.8 = (bf16[2,256,1024]{2,1,0:T(8,128)(2,1)S(1)}, bf16[2,256,1024]{2,1,0:T(8,128)(2,1)S(1)}, u32[]{:S(2)}, u32[]{:S(2)}) collective-permute-start(bf16[2,256,1024]{2,1,0:T(8,128)(2,1)S(1)} %shard_map.145.refs_0_), channel_id=1, source_target_pairs={{0,64},{16,80},{32,96},{48,112},{64,128},{80,144},{96,160},{112,17... | collective-permute-start | bytes 3145736 | tf_op jit(solution)/shard_map/ppermute | solution.py:30
  61.7 35.4 %collective-permute-start.14 = (bf16[4,768,256]{2,1,0:T(8,128)(2,1)S(1)}, bf16[4,768,256]{2,1,0:T(8,128)(2,1)S(1)}, u32[]{:S(2)}, u32[]{:S(2)}) collective-permute-start(bf16[4,768,256]{2,1,0:T(8,128)(2,1)S(1)} %shard_map.148.first), channel_id=1, source_target_pairs={{0,8},{1,9},{2,10},{3,11},{4,12},{5,13},{6,14},{7,15},{8,0},{9,1},... | collective-permute-start | bytes 4718600 | tf_op jit(solution)/shard_map/ppermute | solution.py:39
  63.4 15.6 %collective-permute-start.12 = (bf16[256,1024]{1,0:T(8,128)(2,1)S(1)}, bf16[256,1024]{1,0:T(8,128)(2,1)S(1)}, u32[]{:S(2)}, u32[]{:S(2)}) collective-permute-start(bf16[256,1024]{1,0:T(8,128)(2,1)S(1)} %get-tuple-element.122), channel_id=1, source_target_pairs={{0,192},{16,208},{32,224},{48,240},{64,0},{80,16},{96,32},{112,48}... | collective-permute-start | bytes 1572872 | tf_op jit(solution)/shard_map/ppermute | solution.py:30
  64.8 17.4 %collective-permute-start.13 = (bf16[256,1024]{1,0:T(8,128)(2,1)S(1)}, bf16[256,1024]{1,0:T(8,128)(2,1)S(1)}, u32[]{:S(2)}, u32[]{:S(2)}) collective-permute-start(bf16[256,1024]{1,0:T(8,128)(2,1)S(1)} %get-tuple-element.123), channel_id=1, source_target_pairs={{0,64},{16,80},{32,96},{48,112},{64,128},{80,144},{96,160},{112,17... | collective-permute-start | bytes 1572872 | tf_op jit(solution)/shard_map/ppermute | solution.py:30
  129.4 51.7 %collective-permute-start.29 = (bf16[4,784,256]{2,1,0:T(8,128)(2,1)S(1)}, bf16[4,784,256]{2,1,0:T(8,128)(2,1)S(1)}, u32[]{:S(2)}, u32[]{:S(2)}) collective-permute-start(bf16[4,784,256]{2,1,0:T(8,128)(2,1)S(1)} %get-tuple-element.181), channel_id=1, source_target_pairs={{0,8},{1,9},{2,10},{3,11},{4,12},{5,13},{6,14},{7,15},{8,0},{9,1},... | collective-permute-start | bytes 4816904 | tf_op jit(solution)/shard_map/ppermute | solution.py:39
  135.4 13.9 %collective-permute-start.23 = (bf16[1024,256]{1,0:T(8,128)(2,1)S(1)}, bf16[1024,256]{1,0:T(8,128)(2,1)S(1)}, u32[]{:S(2)}, u32[]{:S(2)}) collective-permute-start(bf16[1024,256]{1,0:T(8,128)(2,1)S(1)} %get-tuple-element.167), channel_id=1, source_target_pairs={{0,64},{16,80},{32,96},{48,112},{64,128},{80,144},{96,160},{112,17... | collective-permute-start | bytes 1572872 | tf_op jit(solution)/shard_map/ppermute | solution.py:30
  138.4 22.2 %collective-permute-start.25 = (bf16[1024,256]{1,0:T(8,128)(2,1)S(1)}, bf16[1024,256]{1,0:T(8,128)(2,1)S(1)}, u32[]{:S(2)}, u32[]{:S(2)}) collective-permute-start(bf16[1024,256]{1,0:T(8,128)(2,1)S(1)} %get-tuple-element.169), channel_id=1, source_target_pairs={{0,64},{16,80},{32,96},{48,112},{64,128},{80,144},{96,160},{112,17... | collective-permute-start | bytes 1572872 | tf_op jit(solution)/shard_map/ppermute | solution.py:30
  138.4 22.2 %collective-permute-start.26 = (bf16[1024,256]{1,0:T(8,128)(2,1)S(1)}, bf16[1024,256]{1,0:T(8,128)(2,1)S(1)}, u32[]{:S(2)}, u32[]{:S(2)}) collective-permute-start(bf16[1024,256]{1,0:T(8,128)(2,1)S(1)} %get-tuple-element.170), channel_id=1, source_target_pairs={{0,192},{16,208},{32,224},{48,240},{64,0},{80,16},{96,32},{112,48}... | collective-permute-start | bytes 1572872 | tf_op jit(solution)/shard_map/ppermute | solution.py:30
  161.2 24.0 %collective-permute-start.32 = (bf16[2,1024,256]{2,1,0:T(8,128)(2,1)S(1)}, bf16[2,1024,256]{2,1,0:T(8,128)(2,1)S(1)}, u32[]{:S(2)}, u32[]{:S(2)}) collective-permute-start(bf16[2,1024,256]{2,1,0:T(8,128)(2,1)S(1)} %get-tuple-element.191), channel_id=1, source_target_pairs={{0,64},{16,80},{32,96},{48,112},{64,128},{80,144},{96,160},{112,17... | collective-permute-start | bytes 3145736 | tf_op jit(solution)/shard_map/ppermute | solution.py:30
  161.3 23.9 %collective-permute-start.33 = (bf16[2,1024,256]{2,1,0:T(8,128)(2,1)S(1)}, bf16[2,1024,256]{2,1,0:T(8,128)(2,1)S(1)}, u32[]{:S(2)}, u32[]{:S(2)}) collective-permute-start(bf16[2,1024,256]{2,1,0:T(8,128)(2,1)S(1)} %get-tuple-element.192), channel_id=1, source_target_pairs={{0,192},{16,208},{32,224},{48,240},{64,0},{80,16},{96,32},{112,48}... | collective-permute-start | bytes 3145736 | tf_op jit(solution)/shard_map/ppermute | solution.py:30
  164.0 17.2 %collective-permute-start.27 = (bf16[512,256]{1,0:T(8,128)(2,1)S(1)}, bf16[512,256]{1,0:T(8,128)(2,1)S(1)}, u32[]{:S(2)}, u32[]{:S(2)}) collective-permute-start(bf16[512,256]{1,0:T(8,128)(2,1)S(1)} %get-tuple-element.179), channel_id=1, source_target_pairs={{0,16},{16,32},{32,48},{48,0},{64,80},{80,96},{96,112},{112,64},{1... | collective-permute-start | bytes 786440 | tf_op jit(solution)/shard_map/ppermute | solution.py:34
  164.0 17.2 %collective-permute-start.28 = (bf16[512,256]{1,0:T(8,128)(2,1)S(1)}, bf16[512,256]{1,0:T(8,128)(2,1)S(1)}, u32[]{:S(2)}, u32[]{:S(2)}) collective-permute-start(bf16[512,256]{1,0:T(8,128)(2,1)S(1)} %get-tuple-element.180), channel_id=1, source_target_pairs={{0,48},{16,0},{32,16},{48,32},{64,112},{80,64},{96,80},{112,96},{1... | collective-permute-start | bytes 786440 | tf_op jit(solution)/shard_map/ppermute | solution.py:34
  181.7 19.4 %collective-permute-start.30 = (bf16[2,784,256]{2,1,0:T(8,128)(2,1)S(1)}, bf16[2,784,256]{2,1,0:T(8,128)(2,1)S(1)}, u32[]{:S(2)}, u32[]{:S(2)}) collective-permute-start(bf16[2,784,256]{2,1,0:T(8,128)(2,1)S(1)} %get-tuple-element.184), channel_id=1, source_target_pairs={{0,4},{1,5},{2,6},{3,7},{4,0},{5,1},{6,2},{7,3},{8,12},{9,13},{10,... | collective-permute-start | bytes 2408456 | tf_op jit(solution)/shard_map/ppermute | solution.py:44
  188.4 21.5 %collective-permute-start.37 = (bf16[1024,256]{1,0:T(8,128)(2,1)S(1)}, bf16[1024,256]{1,0:T(8,128)(2,1)S(1)}, u32[]{:S(2)}, u32[]{:S(2)}) collective-permute-start(bf16[1024,256]{1,0:T(8,128)(2,1)S(1)} %get-tuple-element.207), channel_id=1, source_target_pairs={{0,16},{16,32},{32,48},{48,0},{64,80},{80,96},{96,112},{112,64},{1... | collective-permute-start | bytes 1572872 | tf_op jit(solution)/shard_map/ppermute | solution.py:34
  189.5 24.6 %collective-permute-start.38 = (bf16[1024,256]{1,0:T(8,128)(2,1)S(1)}, bf16[1024,256]{1,0:T(8,128)(2,1)S(1)}, u32[]{:S(2)}, u32[]{:S(2)}) collective-permute-start(bf16[1024,256]{1,0:T(8,128)(2,1)S(1)} %get-tuple-element.208), channel_id=1, source_target_pairs={{0,48},{16,0},{32,16},{48,32},{64,112},{80,64},{96,80},{112,96},{1... | collective-permute-start | bytes 1572872 | tf_op jit(solution)/shard_map/ppermute | solution.py:34
  197.0 17.1 %collective-permute-start.36 = (bf16[1024,256]{1,0:T(8,128)(2,1)S(1)}, bf16[1024,256]{1,0:T(8,128)(2,1)S(1)}, u32[]{:S(2)}, u32[]{:S(2)}) collective-permute-start(bf16[1024,256]{1,0:T(8,128)(2,1)S(1)} %get-tuple-element.200), channel_id=1, source_target_pairs={{0,128},{16,144},{32,160},{48,176},{64,192},{80,208},{96,224},{112... | collective-permute-start | bytes 1572872 | tf_op jit(solution)/shard_map/ppermute | solution.py:30
  201.3 13.9 %collective-permute-start.31 = (bf16[784,256]{1,0:T(8,128)(2,1)S(1)}, bf16[784,256]{1,0:T(8,128)(2,1)S(1)}, u32[]{:S(2)}, u32[]{:S(2)}) collective-permute-start(bf16[784,256]{1,0:T(8,128)(2,1)S(1)} %get-tuple-element.186), channel_id=1, source_target_pairs={{0,2},{1,3},{2,0},{3,1},{4,6},{5,7},{6,4},{7,5},{8,10},{9,11},{10,... | collective-permute-start | bytes 1204232 | tf_op jit(solution)/shard_map/ppermute | solution.py:44
  (17 other events, 217.9 us)

commit v5 on v4

--- a/solution.py
+++ b/solution.py
@@ -11,7 +11,7 @@
 F32 = jnp.float32
 NB = 16
 MIB = 1024 * 1024
-COST = 16
+COST = 4
 EXTRA = 16
 
 YZ = [(y, z) for y in range(4) for z in range(4)]
@@ -469,11 +469,11 @@
 
 
 def gather(block, acts, begin):
-    x1, x3 = send_mp(acts, 0, 1, 0), send_mp(acts, 0, 3, 0)
+    x3 = send_mp(acts, 0, 3, 0)
     before, behind = send_z(block, 1), send_z(block, -1)
     low, high = send_y(block, 1), send_y(block, -1)
-    x1, x3, to_x2, again = after((x1, x3, acts, block), low, high)
-    x2 = send_mp(to_x2, 0, 2, 0)
+    x3, to_x, again = after((x3, acts, block), low, high)
+    x1, x2 = send_mp(to_x, 0, 1, 0), send_mp(to_x, 0, 2, 0)
     across = send_y(again, 2)
 
     x1, x2, x3, before, behind = after((x1, x2, x3, before, behind), across)
@@ -581,15 +581,15 @@
     far0, far1, far2_low, far2_high, far3 = grads(2, (send,))
     full = shape_of(far0.shape)
     pair = shape_of((2,) + far0.shape)
-    own0, own1, own2, own3 = grads(0, (far0,))
     far2_low, far2_high = send_y(far2_low, 1), send_y(far2_high, -1)
-    bf0, bf1, bf2, bf3 = grads(1, (own0,))
+    bf0, bf1, bf2, bf3 = grads(1, (far0,))
     bh0, bh1, bh2, bh3 = grads(3, (bf0,))
     keep = partials(0)
 
     core, keep, far2_low, far2_high, bf2, bh2 = after(
         (core, keep, far2_low, far2_high, bf2, bh2)
     )
+    own0, own1, own2, own3 = grads(0, (core,))
     part = shape_of(keep.shape[1:])
     own_z, other_z = call(core_sum_kernel, (keep, core), [part] * 2, moved=9 * MIB)
     other_z = send_mp(other_z, 1, 0, 0)

time: 217 us -> 214 us (0.986)
  starting transfers between devices: 64.3 us -> 56.3 us
  waiting for transfers between devices: 121 us -> 126 us
    ppermute x22, waiting for transfers between devices: 43.4 us -> 62.5 us  [send_y(): lax.ppermute(value, 'dp', [(dp_index(y, z), dp_index(y + d, z)) for y, z...]
    ppermute x7, waiting for transfers between devices: 17.9 us -> 9.79 us  [send_mp(): return lax.ppermute(value, 'mp', pairs)]
    ppermute x8, waiting for transfers between devices: 57.1 us -> 49.9 us  [send_z(): lax.ppermute(value, 'dp', [(dp_index(y, z), dp_index(y, z + d)) for y, z...]
    ppermute x2, starting transfers between devices: 3.55 us -> 0.27 us  [send_x(): return lax.ppermute(value, 'mp', pairs)]
    ppermute x7, starting transfers between devices: 12.6 us -> 10.1 us  [send_mp(): return lax.ppermute(value, 'mp', pairs)]
  transfers between devices with their start and end apart: 39 -> 39, of which waited for: 20 -> 21; matrix products, arithmetic and copies ran while one was open for 0% -> 0% of each run, Pallas kernels for 9% -> 9%
where the time goes in v5:
time: 214 us
  waiting for transfers between devices  126 us (59%)
  starting transfers between devices  56.3 us (26%)
  Pallas kernels  29.1 us (14%)
  between operations  2.42 us (1%)
    ppermute x22, waiting for transfers between devices, send_y(): lax.ppermute(value, 'dp', [(dp_index(y, z), dp_index(y + d, z)) for y, z...  62.5 us
    ppermute x8, waiting for transfers between devices, send_z(): lax.ppermute(value, 'dp', [(dp_index(y, z), dp_index(y, z + d)) for y, z...  49.9 us
    ppermute x22, starting transfers between devices, send_y(): lax.ppermute(value, 'dp', [(dp_index(y, z), dp_index(y + d, z)) for y, z...  26.6 us
    pallas_call x23, Pallas kernels, call(): pl.pallas_call(kernel, in_specs=[pl.BlockSpec(memory_space=pltpu.SMEM)] *...  24.6 us
    ppermute x8, starting transfers between devices, send_z(): lax.ppermute(value, 'dp', [(dp_index(y, z), dp_index(y, z + d)) for y, z...  19.4 us
    ppermute x7, starting transfers between devices, send_mp(): return lax.ppermute(value, 'mp', pairs)  10.1 us
    ppermute x7, waiting for transfers between devices, send_mp(): return lax.ppermute(value, 'mp', pairs)  9.79 us
  transfers between devices with their start and end apart: 39, of which 21 were waited for; matrix products, arithmetic and copies ran while one was open for 0% of the time, Pallas kernels for 9%

profile of v5, /device:TPU:1, one launch (start us, length us, event | category | flops | bytes accessed | tf_op | source)
XLA Modules:
  0.0 214.2 jit_solution(9334152580643137597)
XLA Ops:
  2.9 3.6 %collective-permute-start.1 = (bf16[256,1024]{1,0:T(8,128)(2,1)}, bf16[256,1024]{1,0:T(8,128)(2,1)S(1)}, u32[]{:S(2)}, u32[]{:S(2)}) collective-permute-start(bf16[256,1024]{1,0:T(8,128)(2,1)} %get-tuple-element.111.refs_0_), channel_id=1, source_target_pairs={{0,192},{16,208},{32,224},{48,240},{64,0},{80,16},{96,32},{112,48}... | collective-permute-start | bytes 1572872 | tf_op jit(solution)/shard_map/ppermute | solution.py:30
  9.0 6.0 %collective-permute-start.7 = (bf16[256,1024]{1,0:T(8,128)(2,1)}, bf16[256,1024]{1,0:T(8,128)(2,1)S(1)}, u32[]{:S(2)}, u32[]{:S(2)}) collective-permute-start(bf16[256,1024]{1,0:T(8,128)(2,1)} %get-tuple-element.111.refs_0_), channel_id=1, source_target_pairs={{0,48},{16,0},{32,16},{48,32},{64,112},{80,64},{96,80},{112,96},{1... | collective-permute-start | bytes 1572872 | tf_op jit(solution)/shard_map/ppermute | solution.py:34
  17.5 3.0 %collective-permute-done.refs_2_ = bf16[256,1024]{1,0:T(8,128)(2,1)S(1)} collective-permute-done((bf16[256,1024]{1,0:T(8,128)(2,1)}, bf16[256,1024]{1,0:T(8,128)(2,1)S(1)}, u32[]{:S(2)}, u32[]{:S(2)}) %collective-permute-start) | collective-permute-done | bytes 524320 | tf_op jit(solution)/shard_map/ppermute | solution.py:30
  20.5 2.7 %collective-permute-start.5 = (bf16[768,256]{1,0:T(8,128)(2,1)}, bf16[768,256]{1,0:T(8,128)(2,1)S(1)}, u32[]{:S(2)}, u32[]{:S(2)}) collective-permute-start(bf16[768,256]{1,0:T(8,128)(2,1)} %get-tuple-element.112.refs_0_.refs_3_), channel_id=1, source_target_pairs={{0,4},{1,5},{2,6},{3,7},{4,0},{5,1},{6,2},{7,3},{8,12},{9,13},{10,... | collective-permute-start | bytes 1179656 | tf_op jit(solution)/shard_map/ppermute | solution.py:39
  23.5 11.3 %collective-permute-done.7.second = bf16[256,1024]{1,0:T(8,128)(2,1)S(1)} collective-permute-done((bf16[256,1024]{1,0:T(8,128)(2,1)}, bf16[256,1024]{1,0:T(8,128)(2,1)S(1)}, u32[]{:S(2)}, u32[]{:S(2)}) %collective-permute-start.7) | collective-permute-done | bytes 524320 | tf_op jit(solution)/shard_map/ppermute | solution.py:34
  34.8 6.8 %collective-permute-done.4.refs_1_ = bf16[768,256]{1,0:T(8,128)(2,1)S(1)} collective-permute-done((bf16[768,256]{1,0:T(8,128)(2,1)}, bf16[768,256]{1,0:T(8,128)(2,1)S(1)}, u32[]{:S(2)}, u32[]{:S(2)}) %collective-permute-start.4) | collective-permute-done | bytes 393248 | tf_op jit(solution)/shard_map/ppermute | solution.py:39
  41.7 3.1 %collective-permute-start.10 = (bf16[128,1024]{1,0:T(8,128)(2,1)S(1)}, bf16[128,1024]{1,0:T(8,128)(2,1)S(1)}, u32[]{:S(2)}, u32[]{:S(2)}) collective-permute-start(bf16[128,1024]{1,0:T(8,128)(2,1)S(1)} %get-tuple-element.116), channel_id=1, source_target_pairs={{0,16},{16,32},{32,48},{48,0},{64,80},{80,96},{96,112},{112,64},{1... | collective-permute-start | bytes 786440 | tf_op jit(solution)/shard_map/ppermute | solution.py:34
  44.7 3.1 %collective-permute-start.11 = (bf16[128,1024]{1,0:T(8,128)(2,1)S(1)}, bf16[128,1024]{1,0:T(8,128)(2,1)S(1)}, u32[]{:S(2)}, u32[]{:S(2)}) collective-permute-start(bf16[128,1024]{1,0:T(8,128)(2,1)S(1)} %get-tuple-element.117), channel_id=1, source_target_pairs={{0,48},{16,0},{32,16},{48,32},{64,112},{80,64},{96,80},{112,96},{1... | collective-permute-start | bytes 786440 | tf_op jit(solution)/shard_map/ppermute | solution.py:34
  49.7 5.9 %collective-permute-done.10.first = bf16[128,1024]{1,0:T(8,128)(2,1)S(1)} collective-permute-done((bf16[128,1024]{1,0:T(8,128)(2,1)S(1)}, bf16[128,1024]{1,0:T(8,128)(2,1)S(1)}, u32[]{:S(2)}, u32[]{:S(2)}) %collective-permute-start.10) | collective-permute-done | bytes 262176 | tf_op jit(solution)/shard_map/ppermute | solution.py:34
  55.6 5.3 %collective-permute-done.11.second = bf16[128,1024]{1,0:T(8,128)(2,1)S(1)} collective-permute-done((bf16[128,1024]{1,0:T(8,128)(2,1)S(1)}, bf16[128,1024]{1,0:T(8,128)(2,1)S(1)}, u32[]{:S(2)}, u32[]{:S(2)}) %collective-permute-start.11) | collective-permute-done | bytes 262176 | tf_op jit(solution)/shard_map/ppermute | solution.py:34
  60.9 11.0 %collective-permute-done.9.second.refs_1_ = bf16[2,256,1024]{2,1,0:T(8,128)(2,1)S(1)} collective-permute-done((bf16[2,256,1024]{2,1,0:T(8,128)(2,1)S(1)}, bf16[2,256,1024]{2,1,0:T(8,128)(2,1)S(1)}, u32[]{:S(2)}, u32[]{:S(2)}) %collective-permute-start.9) | collective-permute-done | bytes 1048608 | tf_op jit(solution)/shard_map/ppermute | solution.py:30
  77.8 8.1 %collective-permute-done.16.second.refs_1_ = bf16[256,1024]{1,0:T(8,128)(2,1)S(1)} collective-permute-done((bf16[256,1024]{1,0:T(8,128)(2,1)S(1)}, bf16[256,1024]{1,0:T(8,128)(2,1)S(1)}, u32[]{:S(2)}, u32[]{:S(2)}) %collective-permute-start.16) | collective-permute-done | bytes 524320 | tf_op jit(solution)/shard_map/ppermute | solution.py:30
  87.4 9.8 %collective-permute-done.12.refs_4_ = bf16[256,1024]{1,0:T(8,128)(2,1)S(1)} collective-permute-done((bf16[256,1024]{1,0:T(8,128)(2,1)S(1)}, bf16[256,1024]{1,0:T(8,128)(2,1)S(1)}, u32[]{:S(2)}, u32[]{:S(2)}) %collective-permute-start.12) | collective-permute-done | bytes 524320 | tf_op jit(solution)/shard_map/ppermute | solution.py:30
  98.8 3.3 %collective-permute-start.17 = (bf16[2,4,768,256]{3,2,1,0:T(8,128)(2,1)S(1)}, bf16[2,4,768,256]{3,2,1,0:T(8,128)(2,1)S(1)}, u32[]{:S(2)}, u32[]{:S(2)}) collective-permute-start(bf16[2,4,768,256]{3,2,1,0:T(8,128)(2,1)S(1)} %shard_map.150.own_ref), channel_id=1, source_target_pairs={{0,1},{1,0},{2,3},{3,2},{4,5},{5,4},{6,7},{7,6},{8,9},{9,8},{10,11... | collective-permute-start | bytes 9437192 | tf_op jit(solution)/shard_map/ppermute | solution.py:39
  107.3 3.6 %shard_map.151 = (bf16[16,256,256]{2,1,0:T(8,128)(2,1)S(1)}, bf16[16,256,256]{2,1,0:T(8,128)(2,1)S(1)}, bf16[16,256,256]{2,1,0:T(8,128)(2,1)S(1)}, f32[256,128]{1,0:T(8,128)S(1)}) custom-call(s32[1]{0:T(128)S(6)} %copy.19.len_ref.refs_0_, bf16[2,4,768,256]{3,2,1,0:T(8,128)(2,1)S(1)} %shard_map.150.own_ref, ...), custom_call_target="tpu_custom_call" | custom-call | bytes 12582912 | tf_op jit(solution)/shard_map/pallas_call | solution.py:65
  114.9 3.8 %shard_map.156 = bf16[2,4,784,256]{3,2,1,0:T(8,128)(2,1)S(1)} custom-call(bf16[256,256]{1,0:T(8,128)(2,1)S(1)} %get-tuple-element.140.q_t_ref.refs_0_, bf16[256,512]{1,0:T(8,128)(2,1)S(1)} %get-tuple-element.141.kv_ref, bf16[256,256]{1,0:T(8,128)(2,1)S(1)} %get-tuple-element.142.at_t_ref.refs_2_, bf16[16,256]{1,0:T(8,128)(2,1)S(1)} %get-tuple-element.143.stat_ref, ...), custom_call_target="tpu_custom_call" | custom-call | flops 4294967296 | bytes 14680064 | tf_op jit(solution)/shard_map/pallas_call | solution.py:65
  123.4 3.8 %shard_map.157.keep_ref = bf16[2,4,784,256]{3,2,1,0:T(8,128)(2,1)S(1)} custom-call(bf16[256,256]{1,0:T(8,128)(2,1)S(1)} %get-tuple-element.140.q_t_ref.refs_0_, bf16[256,512]{1,0:T(8,128)(2,1)S(1)} %get-tuple-element.141.kv_ref, bf16[256,256]{1,0:T(8,128)(2,1)S(1)} %get-tuple-element.142.at_t_ref.refs_2_, bf16[16,256]{1,0:T(8,128)(2,1)S(1)} %get-tuple-element.143.stat_ref, ...), custom_call_target="tpu_custom_call" | custom-call | flops 4294967296 | bytes 14680064 | tf_op jit(solution)/shard_map/pallas_call | solution.py:65
  137.6 8.3 %collective-permute-done.23.far1 = bf16[1024,256]{1,0:T(8,128)(2,1)S(1)} collective-permute-done((bf16[1024,256]{1,0:T(8,128)(2,1)S(1)}, bf16[1024,256]{1,0:T(8,128)(2,1)S(1)}, u32[]{:S(2)}, u32[]{:S(2)}) %collective-permute-start.23) | collective-permute-done | bytes 524320 | tf_op jit(solution)/shard_map/ppermute | solution.py:30
  145.9 11.2 %collective-permute-done.25.bf2 = bf16[1024,256]{1,0:T(8,128)(2,1)S(1)} collective-permute-done((bf16[1024,256]{1,0:T(8,128)(2,1)S(1)}, bf16[1024,256]{1,0:T(8,128)(2,1)S(1)}, u32[]{:S(2)}, u32[]{:S(2)}) %collective-permute-start.25) | collective-permute-done | bytes 524320 | tf_op jit(solution)/shard_map/ppermute | solution.py:30
  164.1 15.6 %collective-permute-done.27.low = bf16[512,256]{1,0:T(8,128)(2,1)S(1)} collective-permute-done((bf16[512,256]{1,0:T(8,128)(2,1)S(1)}, bf16[512,256]{1,0:T(8,128)(2,1)S(1)}, u32[]{:S(2)}, u32[]{:S(2)}) %collective-permute-start.27) | collective-permute-done | bytes 262176 | tf_op jit(solution)/shard_map/ppermute | solution.py:34
  188.8 5.1 %collective-permute-done.34.refs_1_ = bf16[1024,256]{1,0:T(8,128)(2,1)S(1)} collective-permute-done((bf16[1024,256]{1,0:T(8,128)(2,1)S(1)}, bf16[1024,256]{1,0:T(8,128)(2,1)S(1)}, u32[]{:S(2)}, u32[]{:S(2)}) %collective-permute-start.34) | collective-permute-done | bytes 524320 | tf_op jit(solution)/shard_map/ppermute | solution.py:30
  195.4 4.2 %collective-permute-done.30.second_ref = bf16[2,784,256]{2,1,0:T(8,128)(2,1)S(1)} collective-permute-done((bf16[2,784,256]{2,1,0:T(8,128)(2,1)S(1)}, bf16[2,784,256]{2,1,0:T(8,128)(2,1)S(1)}, u32[]{:S(2)}, u32[]{:S(2)}) %collective-permute-start.30) | collective-permute-done | bytes 802848 | tf_op jit(solution)/shard_map/ppermute | solution.py:44
  199.9 5.1 %collective-permute-done.37.refs_4_ = bf16[1024,256]{1,0:T(8,128)(2,1)S(1)} collective-permute-done((bf16[1024,256]{1,0:T(8,128)(2,1)S(1)}, bf16[1024,256]{1,0:T(8,128)(2,1)S(1)}, u32[]{:S(2)}, u32[]{:S(2)}) %collective-permute-start.37) | collective-permute-done | bytes 524320 | tf_op jit(solution)/shard_map/ppermute | solution.py:34
  205.0 6.8 %collective-permute-done.38.refs_5_ = bf16[1024,256]{1,0:T(8,128)(2,1)S(1)} collective-permute-done((bf16[1024,256]{1,0:T(8,128)(2,1)S(1)}, bf16[1024,256]{1,0:T(8,128)(2,1)S(1)}, u32[]{:S(2)}, u32[]{:S(2)}) %collective-permute-start.38) | collective-permute-done | bytes 524320 | tf_op jit(solution)/shard_map/ppermute | solution.py:34
  (84 shorter events, 61.4 us)
Async XLA Ops:
  2.9 14.5 %collective-permute-start.1 = (bf16[256,1024]{1,0:T(8,128)(2,1)}, bf16[256,1024]{1,0:T(8,128)(2,1)S(1)}, u32[]{:S(2)}, u32[]{:S(2)}) collective-permute-start(bf16[256,1024]{1,0:T(8,128)(2,1)} %get-tuple-element.111.refs_0_), channel_id=1, source_target_pairs={{0,192},{16,208},{32,224},{48,240},{64,0},{80,16},{96,32},{112,48}... | collective-permute-start | bytes 1572872 | tf_op jit(solution)/shard_map/ppermute | solution.py:30
  9.0 25.7 %collective-permute-start.7 = (bf16[256,1024]{1,0:T(8,128)(2,1)}, bf16[256,1024]{1,0:T(8,128)(2,1)S(1)}, u32[]{:S(2)}, u32[]{:S(2)}) collective-permute-start(bf16[256,1024]{1,0:T(8,128)(2,1)} %get-tuple-element.111.refs_0_), channel_id=1, source_target_pairs={{0,48},{16,0},{32,16},{48,32},{64,112},{80,64},{96,80},{112,96},{1... | collective-permute-start | bytes 1572872 | tf_op jit(solution)/shard_map/ppermute | solution.py:34
  15.1 19.7 %collective-permute-start.6 = (bf16[256,1024]{1,0:T(8,128)(2,1)}, bf16[256,1024]{1,0:T(8,128)(2,1)S(1)}, u32[]{:S(2)}, u32[]{:S(2)}) collective-permute-start(bf16[256,1024]{1,0:T(8,128)(2,1)} %get-tuple-element.111.refs_0_), channel_id=1, source_target_pairs={{0,16},{16,32},{32,48},{48,0},{64,80},{80,96},{96,112},{112,64},{1... | collective-permute-start | bytes 1572872 | tf_op jit(solution)/shard_map/ppermute | solution.py:34
  20.4 21.2 %collective-permute-start.3 = (bf16[256,1024]{1,0:T(8,128)(2,1)}, bf16[256,1024]{1,0:T(8,128)(2,1)S(1)}, u32[]{:S(2)}, u32[]{:S(2)}) collective-permute-start(bf16[256,1024]{1,0:T(8,128)(2,1)} %get-tuple-element.111.refs_0_), channel_id=1, source_target_pairs={{0,128},{16,144},{32,160},{48,176},{64,192},{80,208},{96,224},{112... | collective-permute-start | bytes 1572872 | tf_op jit(solution)/shard_map/ppermute | solution.py:30
  20.5 14.3 %collective-permute-start.5 = (bf16[768,256]{1,0:T(8,128)(2,1)}, bf16[768,256]{1,0:T(8,128)(2,1)S(1)}, u32[]{:S(2)}, u32[]{:S(2)}) collective-permute-start(bf16[768,256]{1,0:T(8,128)(2,1)} %get-tuple-element.112.refs_0_.refs_3_), channel_id=1, source_target_pairs={{0,4},{1,5},{2,6},{3,7},{4,0},{5,1},{6,2},{7,3},{8,12},{9,13},{10,... | collective-permute-start | bytes 1179656 | tf_op jit(solution)/shard_map/ppermute | solution.py:39
  23.2 18.4 %collective-permute-start.4 = (bf16[768,256]{1,0:T(8,128)(2,1)}, bf16[768,256]{1,0:T(8,128)(2,1)S(1)}, u32[]{:S(2)}, u32[]{:S(2)}) collective-permute-start(bf16[768,256]{1,0:T(8,128)(2,1)} %get-tuple-element.112.refs_0_.refs_3_), channel_id=1, source_target_pairs={{0,2},{1,3},{2,4},{3,5},{4,6},{5,7},{6,0},{7,1},{8,10},{9,11},{10,... | collective-permute-start | bytes 1179656 | tf_op jit(solution)/shard_map/ppermute | solution.py:39
  41.7 13.9 %collective-permute-start.10 = (bf16[128,1024]{1,0:T(8,128)(2,1)S(1)}, bf16[128,1024]{1,0:T(8,128)(2,1)S(1)}, u32[]{:S(2)}, u32[]{:S(2)}) collective-permute-start(bf16[128,1024]{1,0:T(8,128)(2,1)S(1)} %get-tuple-element.116), channel_id=1, source_target_pairs={{0,16},{16,32},{32,48},{48,0},{64,80},{80,96},{96,112},{112,64},{1... | collective-permute-start | bytes 786440 | tf_op jit(solution)/shard_map/ppermute | solution.py:34
  44.7 16.1 %collective-permute-start.11 = (bf16[128,1024]{1,0:T(8,128)(2,1)S(1)}, bf16[128,1024]{1,0:T(8,128)(2,1)S(1)}, u32[]{:S(2)}, u32[]{:S(2)}) collective-permute-start(bf16[128,1024]{1,0:T(8,128)(2,1)S(1)} %get-tuple-element.117), channel_id=1, source_target_pairs={{0,48},{16,0},{32,16},{48,32},{64,112},{80,64},{96,80},{112,96},{1... | collective-permute-start | bytes 786440 | tf_op jit(solution)/shard_map/ppermute | solution.py:34
  47.9 24.0 %collective-permute-start.9 = (bf16[2,256,1024]{2,1,0:T(8,128)(2,1)S(1)}, bf16[2,256,1024]{2,1,0:T(8,128)(2,1)S(1)}, u32[]{:S(2)}, u32[]{:S(2)}) collective-permute-start(bf16[2,256,1024]{2,1,0:T(8,128)(2,1)S(1)} %shard_map.145.refs_0_), channel_id=1, source_target_pairs={{0,192},{16,208},{32,224},{48,240},{64,0},{80,16},{96,32},{112,48}... | collective-permute-start | bytes 3145736 | tf_op jit(solution)/shard_map/ppermute | solution.py:30
  49.5 24.8 %collective-permute-start.8 = (bf16[2,256,1024]{2,1,0:T(8,128)(2,1)S(1)}, bf16[2,256,1024]{2,1,0:T(8,128)(2,1)S(1)}, u32[]{:S(2)}, u32[]{:S(2)}) collective-permute-start(bf16[2,256,1024]{2,1,0:T(8,128)(2,1)S(1)} %shard_map.145.refs_0_), channel_id=1, source_target_pairs={{0,64},{16,80},{32,96},{48,112},{64,128},{80,144},{96,160},{112,17... | collective-permute-start | bytes 3145736 | tf_op jit(solution)/shard_map/ppermute | solution.py:30
  60.9 37.7 %collective-permute-start.14 = (bf16[4,768,256]{2,1,0:T(8,128)(2,1)S(1)}, bf16[4,768,256]{2,1,0:T(8,128)(2,1)S(1)}, u32[]{:S(2)}, u32[]{:S(2)}) collective-permute-start(bf16[4,768,256]{2,1,0:T(8,128)(2,1)S(1)} %shard_map.148.first), channel_id=1, source_target_pairs={{0,8},{1,9},{2,10},{3,11},{4,12},{5,13},{6,14},{7,15},{8,0},{9,1},... | collective-permute-start | bytes 4718600 | tf_op jit(solution)/shard_map/ppermute | solution.py:39
  76.0 21.1 %collective-permute-start.12 = (bf16[256,1024]{1,0:T(8,128)(2,1)S(1)}, bf16[256,1024]{1,0:T(8,128)(2,1)S(1)}, u32[]{:S(2)}, u32[]{:S(2)}) collective-permute-start(bf16[256,1024]{1,0:T(8,128)(2,1)S(1)} %get-tuple-element.120), channel_id=1, source_target_pairs={{0,192},{16,208},{32,224},{48,240},{64,0},{80,16},{96,32},{112,48}... | collective-permute-start | bytes 1572872 | tf_op jit(solution)/shard_map/ppermute | solution.py:30
  77.8 20.8 %collective-permute-start.13 = (bf16[256,1024]{1,0:T(8,128)(2,1)S(1)}, bf16[256,1024]{1,0:T(8,128)(2,1)S(1)}, u32[]{:S(2)}, u32[]{:S(2)}) collective-permute-start(bf16[256,1024]{1,0:T(8,128)(2,1)S(1)} %get-tuple-element.121), channel_id=1, source_target_pairs={{0,64},{16,80},{32,96},{48,112},{64,128},{80,144},{96,160},{112,17... | collective-permute-start | bytes 1572872 | tf_op jit(solution)/shard_map/ppermute | solution.py:30
  131.2 48.5 %collective-permute-start.29 = (bf16[4,784,256]{2,1,0:T(8,128)(2,1)S(1)}, bf16[4,784,256]{2,1,0:T(8,128)(2,1)S(1)}, u32[]{:S(2)}, u32[]{:S(2)}) collective-permute-start(bf16[4,784,256]{2,1,0:T(8,128)(2,1)S(1)} %get-tuple-element.177), channel_id=1, source_target_pairs={{0,8},{1,9},{2,10},{3,11},{4,12},{5,13},{6,14},{7,15},{8,0},{9,1},... | collective-permute-start | bytes 4816904 | tf_op jit(solution)/shard_map/ppermute | solution.py:39
  134.9 22.2 %collective-permute-start.25 = (bf16[1024,256]{1,0:T(8,128)(2,1)S(1)}, bf16[1024,256]{1,0:T(8,128)(2,1)S(1)}, u32[]{:S(2)}, u32[]{:S(2)}) collective-permute-start(bf16[1024,256]{1,0:T(8,128)(2,1)S(1)} %get-tuple-element.165), channel_id=1, source_target_pairs={{0,64},{16,80},{32,96},{48,112},{64,128},{80,144},{96,160},{112,17... | collective-permute-start | bytes 1572872 | tf_op jit(solution)/shard_map/ppermute | solution.py:30
  134.9 22.2 %collective-permute-start.26 = (bf16[1024,256]{1,0:T(8,128)(2,1)S(1)}, bf16[1024,256]{1,0:T(8,128)(2,1)S(1)}, u32[]{:S(2)}, u32[]{:S(2)}) collective-permute-start(bf16[1024,256]{1,0:T(8,128)(2,1)S(1)} %get-tuple-element.166), channel_id=1, source_target_pairs={{0,192},{16,208},{32,224},{48,240},{64,0},{80,16},{96,32},{112,48}... | collective-permute-start | bytes 1572872 | tf_op jit(solution)/shard_map/ppermute | solution.py:30
  157.8 24.1 %collective-permute-start.32 = (bf16[2,1024,256]{2,1,0:T(8,128)(2,1)S(1)}, bf16[2,1024,256]{2,1,0:T(8,128)(2,1)S(1)}, u32[]{:S(2)}, u32[]{:S(2)}) collective-permute-start(bf16[2,1024,256]{2,1,0:T(8,128)(2,1)S(1)} %get-tuple-element.189), channel_id=1, source_target_pairs={{0,64},{16,80},{32,96},{48,112},{64,128},{80,144},{96,160},{112,17... | collective-permute-start | bytes 3145736 | tf_op jit(solution)/shard_map/ppermute | solution.py:30
  157.9 24.0 %collective-permute-start.33 = (bf16[2,1024,256]{2,1,0:T(8,128)(2,1)S(1)}, bf16[2,1024,256]{2,1,0:T(8,128)(2,1)S(1)}, u32[]{:S(2)}, u32[]{:S(2)}) collective-permute-start(bf16[2,1024,256]{2,1,0:T(8,128)(2,1)S(1)} %get-tuple-element.190), channel_id=1, source_target_pairs={{0,192},{16,208},{32,224},{48,240},{64,0},{80,16},{96,32},{112,48}... | collective-permute-start | bytes 3145736 | tf_op jit(solution)/shard_map/ppermute | solution.py:30
  160.5 19.1 %collective-permute-start.27 = (bf16[512,256]{1,0:T(8,128)(2,1)S(1)}, bf16[512,256]{1,0:T(8,128)(2,1)S(1)}, u32[]{:S(2)}, u32[]{:S(2)}) collective-permute-start(bf16[512,256]{1,0:T(8,128)(2,1)S(1)} %get-tuple-element.175), channel_id=1, source_target_pairs={{0,16},{16,32},{32,48},{48,0},{64,80},{80,96},{96,112},{112,64},{1... | collective-permute-start | bytes 786440 | tf_op jit(solution)/shard_map/ppermute | solution.py:34
  161.6 18.1 %collective-permute-start.28 = (bf16[512,256]{1,0:T(8,128)(2,1)S(1)}, bf16[512,256]{1,0:T(8,128)(2,1)S(1)}, u32[]{:S(2)}, u32[]{:S(2)}) collective-permute-start(bf16[512,256]{1,0:T(8,128)(2,1)S(1)} %get-tuple-element.176), channel_id=1, source_target_pairs={{0,48},{16,0},{32,16},{48,32},{64,112},{80,64},{96,80},{112,96},{1... | collective-permute-start | bytes 786440 | tf_op jit(solution)/shard_map/ppermute | solution.py:34
  180.2 19.4 %collective-permute-start.30 = (bf16[2,784,256]{2,1,0:T(8,128)(2,1)S(1)}, bf16[2,784,256]{2,1,0:T(8,128)(2,1)S(1)}, u32[]{:S(2)}, u32[]{:S(2)}) collective-permute-start(bf16[2,784,256]{2,1,0:T(8,128)(2,1)S(1)} %get-tuple-element.180), channel_id=1, source_target_pairs={{0,4},{1,5},{2,6},{3,7},{4,0},{5,1},{6,2},{7,3},{8,12},{9,13},{10,... | collective-permute-start | bytes 2408456 | tf_op jit(solution)/shard_map/ppermute | solution.py:44
  185.1 19.9 %collective-permute-start.37 = (bf16[1024,256]{1,0:T(8,128)(2,1)S(1)}, bf16[1024,256]{1,0:T(8,128)(2,1)S(1)}, u32[]{:S(2)}, u32[]{:S(2)}) collective-permute-start(bf16[1024,256]{1,0:T(8,128)(2,1)S(1)} %get-tuple-element.205), channel_id=1, source_target_pairs={{0,16},{16,32},{32,48},{48,0},{64,80},{80,96},{96,112},{112,64},{1... | collective-permute-start | bytes 1572872 | tf_op jit(solution)/shard_map/ppermute | solution.py:34
  186.2 25.6 %collective-permute-start.38 = (bf16[1024,256]{1,0:T(8,128)(2,1)S(1)}, bf16[1024,256]{1,0:T(8,128)(2,1)S(1)}, u32[]{:S(2)}, u32[]{:S(2)}) collective-permute-start(bf16[1024,256]{1,0:T(8,128)(2,1)S(1)} %get-tuple-element.206), channel_id=1, source_target_pairs={{0,48},{16,0},{32,16},{48,32},{64,112},{80,64},{96,80},{112,96},{1... | collective-permute-start | bytes 1572872 | tf_op jit(solution)/shard_map/ppermute | solution.py:34
  193.9 17.9 %collective-permute-start.36 = (bf16[1024,256]{1,0:T(8,128)(2,1)S(1)}, bf16[1024,256]{1,0:T(8,128)(2,1)S(1)}, u32[]{:S(2)}, u32[]{:S(2)}) collective-permute-start(bf16[1024,256]{1,0:T(8,128)(2,1)S(1)} %get-tuple-element.198), channel_id=1, source_target_pairs={{0,128},{16,144},{32,160},{48,176},{64,192},{80,208},{96,224},{112... | collective-permute-start | bytes 1572872 | tf_op jit(solution)/shard_map/ppermute | solution.py:30
  (17 other events, 224.9 us)

commit v6 on v5

--- a/solution.py
+++ b/solution.py
@@ -616,9 +616,10 @@
     before, behind = call(
         third_sum_kernel, (bf0, bh0, up, down, far_low, far_high), [full] * 2
     )
+    own1, own3, before, behind = after((own1, own3, before, behind))
     before, behind = send_z(before, 1), send_z(behind, -1)
     own1, own3 = send_y(own1, 1), send_y(own3, -1)
-    own2, own1, own3 = after((own2, own1, own3))
+    own2, own1 = after((own2, own1))
     own2 = send_y(own2, 2)
     part = shape_of(keep.shape[2:])
     own_x, next_x = call(x_sum_kernel, (near_x, far_x), [part] * 2, moved=3 * MIB)

time: 214 us -> 214 us (level)
  no operation moved by 1% of the time
where the time goes in v6:
time: 214 us
  waiting for transfers between devices  128 us (60%)
  starting transfers between devices  54.7 us (26%)
  Pallas kernels  29.1 us (14%)
  between operations  2.43 us (1%)
    ppermute x22, waiting for transfers between devices, send_y(): lax.ppermute(value, 'dp', [(dp_index(y, z), dp_index(y + d, z)) for y, z...  63 us
    ppermute x8, waiting for transfers between devices, send_z(): lax.ppermute(value, 'dp', [(dp_index(y, z), dp_index(y, z + d)) for y, z...  50 us
    ppermute x22, starting transfers between devices, send_y(): lax.ppermute(value, 'dp', [(dp_index(y, z), dp_index(y + d, z)) for y, z...  25 us
    pallas_call x23, Pallas kernels, call(): pl.pallas_call(kernel, in_specs=[pl.BlockSpec(memory_space=pltpu.SMEM)] *...  24.6 us
    ppermute x8, starting transfers between devices, send_z(): lax.ppermute(value, 'dp', [(dp_index(y, z), dp_index(y, z + d)) for y, z...  19.4 us
    ppermute x7, starting transfers between devices, send_mp(): return lax.ppermute(value, 'mp', pairs)  10.1 us
    ppermute x7, waiting for transfers between devices, send_mp(): return lax.ppermute(value, 'mp', pairs)  9.79 us
    ppermute x2, waiting for transfers between devices, send_x(): return lax.ppermute(value, 'mp', pairs)  5.27 us
  transfers between devices with their start and end apart: 39, of which 21 were waited for; matrix products, arithmetic and copies ran while one was open for 0% of the time, Pallas kernels for 9%

profile of v6, /device:TPU:1, one launch (start us, length us, event | category | flops | bytes accessed | tf_op | source)
XLA Modules:
  0.0 214.3 jit_solution(18044582511462769688)
XLA Ops:
  2.9 3.6 %collective-permute-start.1 = (bf16[256,1024]{1,0:T(8,128)(2,1)}, bf16[256,1024]{1,0:T(8,128)(2,1)S(1)}, u32[]{:S(2)}, u32[]{:S(2)}) collective-permute-start(bf16[256,1024]{1,0:T(8,128)(2,1)} %get-tuple-element.114.refs_0_), channel_id=1, source_target_pairs={{0,192},{16,208},{32,224},{48,240},{64,0},{80,16},{96,32},{112,48}... | collective-permute-start | bytes 1572872 | tf_op jit(solution)/shard_map/ppermute | solution.py:30
  9.0 6.0 %collective-permute-start.7 = (bf16[256,1024]{1,0:T(8,128)(2,1)}, bf16[256,1024]{1,0:T(8,128)(2,1)S(1)}, u32[]{:S(2)}, u32[]{:S(2)}) collective-permute-start(bf16[256,1024]{1,0:T(8,128)(2,1)} %get-tuple-element.114.refs_0_), channel_id=1, source_target_pairs={{0,48},{16,0},{32,16},{48,32},{64,112},{80,64},{96,80},{112,96},{1... | collective-permute-start | bytes 1572872 | tf_op jit(solution)/shard_map/ppermute | solution.py:34
  17.5 3.0 %collective-permute-done.refs_2_ = bf16[256,1024]{1,0:T(8,128)(2,1)S(1)} collective-permute-done((bf16[256,1024]{1,0:T(8,128)(2,1)}, bf16[256,1024]{1,0:T(8,128)(2,1)S(1)}, u32[]{:S(2)}, u32[]{:S(2)}) %collective-permute-start) | collective-permute-done | bytes 524320 | tf_op jit(solution)/shard_map/ppermute | solution.py:30
  20.5 2.7 %collective-permute-start.5 = (bf16[768,256]{1,0:T(8,128)(2,1)}, bf16[768,256]{1,0:T(8,128)(2,1)S(1)}, u32[]{:S(2)}, u32[]{:S(2)}) collective-permute-start(bf16[768,256]{1,0:T(8,128)(2,1)} %get-tuple-element.115.refs_0_.refs_3_), channel_id=1, source_target_pairs={{0,4},{1,5},{2,6},{3,7},{4,0},{5,1},{6,2},{7,3},{8,12},{9,13},{10,... | collective-permute-start | bytes 1179656 | tf_op jit(solution)/shard_map/ppermute | solution.py:39
  23.5 11.3 %collective-permute-done.7.second = bf16[256,1024]{1,0:T(8,128)(2,1)S(1)} collective-permute-done((bf16[256,1024]{1,0:T(8,128)(2,1)}, bf16[256,1024]{1,0:T(8,128)(2,1)S(1)}, u32[]{:S(2)}, u32[]{:S(2)}) %collective-permute-start.7) | collective-permute-done | bytes 524320 | tf_op jit(solution)/shard_map/ppermute | solution.py:34
  34.8 6.8 %collective-permute-done.4.refs_1_ = bf16[768,256]{1,0:T(8,128)(2,1)S(1)} collective-permute-done((bf16[768,256]{1,0:T(8,128)(2,1)}, bf16[768,256]{1,0:T(8,128)(2,1)S(1)}, u32[]{:S(2)}, u32[]{:S(2)}) %collective-permute-start.4) | collective-permute-done | bytes 393248 | tf_op jit(solution)/shard_map/ppermute | solution.py:39
  41.7 3.1 %collective-permute-start.10 = (bf16[128,1024]{1,0:T(8,128)(2,1)S(1)}, bf16[128,1024]{1,0:T(8,128)(2,1)S(1)}, u32[]{:S(2)}, u32[]{:S(2)}) collective-permute-start(bf16[128,1024]{1,0:T(8,128)(2,1)S(1)} %get-tuple-element.119), channel_id=1, source_target_pairs={{0,16},{16,32},{32,48},{48,0},{64,80},{80,96},{96,112},{112,64},{1... | collective-permute-start | bytes 786440 | tf_op jit(solution)/shard_map/ppermute | solution.py:34
  44.7 3.1 %collective-permute-start.11 = (bf16[128,1024]{1,0:T(8,128)(2,1)S(1)}, bf16[128,1024]{1,0:T(8,128)(2,1)S(1)}, u32[]{:S(2)}, u32[]{:S(2)}) collective-permute-start(bf16[128,1024]{1,0:T(8,128)(2,1)S(1)} %get-tuple-element.120), channel_id=1, source_target_pairs={{0,48},{16,0},{32,16},{48,32},{64,112},{80,64},{96,80},{112,96},{1... | collective-permute-start | bytes 786440 | tf_op jit(solution)/shard_map/ppermute | solution.py:34
  49.7 5.9 %collective-permute-done.10.first = bf16[128,1024]{1,0:T(8,128)(2,1)S(1)} collective-permute-done((bf16[128,1024]{1,0:T(8,128)(2,1)S(1)}, bf16[128,1024]{1,0:T(8,128)(2,1)S(1)}, u32[]{:S(2)}, u32[]{:S(2)}) %collective-permute-start.10) | collective-permute-done | bytes 262176 | tf_op jit(solution)/shard_map/ppermute | solution.py:34
  55.6 5.3 %collective-permute-done.11.second = bf16[128,1024]{1,0:T(8,128)(2,1)S(1)} collective-permute-done((bf16[128,1024]{1,0:T(8,128)(2,1)S(1)}, bf16[128,1024]{1,0:T(8,128)(2,1)S(1)}, u32[]{:S(2)}, u32[]{:S(2)}) %collective-permute-start.11) | collective-permute-done | bytes 262176 | tf_op jit(solution)/shard_map/ppermute | solution.py:34
  60.9 11.0 %collective-permute-done.9.second.refs_1_ = bf16[2,256,1024]{2,1,0:T(8,128)(2,1)S(1)} collective-permute-done((bf16[2,256,1024]{2,1,0:T(8,128)(2,1)S(1)}, bf16[2,256,1024]{2,1,0:T(8,128)(2,1)S(1)}, u32[]{:S(2)}, u32[]{:S(2)}) %collective-permute-start.9) | collective-permute-done | bytes 1048608 | tf_op jit(solution)/shard_map/ppermute | solution.py:30
  77.8 8.1 %collective-permute-done.16.second.refs_1_ = bf16[256,1024]{1,0:T(8,128)(2,1)S(1)} collective-permute-done((bf16[256,1024]{1,0:T(8,128)(2,1)S(1)}, bf16[256,1024]{1,0:T(8,128)(2,1)S(1)}, u32[]{:S(2)}, u32[]{:S(2)}) %collective-permute-start.16) | collective-permute-done | bytes 524320 | tf_op jit(solution)/shard_map/ppermute | solution.py:30
  87.4 9.8 %collective-permute-done.12.refs_4_ = bf16[256,1024]{1,0:T(8,128)(2,1)S(1)} collective-permute-done((bf16[256,1024]{1,0:T(8,128)(2,1)S(1)}, bf16[256,1024]{1,0:T(8,128)(2,1)S(1)}, u32[]{:S(2)}, u32[]{:S(2)}) %collective-permute-start.12) | collective-permute-done | bytes 524320 | tf_op jit(solution)/shard_map/ppermute | solution.py:30
  98.8 3.3 %collective-permute-start.17 = (bf16[2,4,768,256]{3,2,1,0:T(8,128)(2,1)S(1)}, bf16[2,4,768,256]{3,2,1,0:T(8,128)(2,1)S(1)}, u32[]{:S(2)}, u32[]{:S(2)}) collective-permute-start(bf16[2,4,768,256]{3,2,1,0:T(8,128)(2,1)S(1)} %shard_map.150.own_ref), channel_id=1, source_target_pairs={{0,1},{1,0},{2,3},{3,2},{4,5},{5,4},{6,7},{7,6},{8,9},{9,8},{10,11... | collective-permute-start | bytes 9437192 | tf_op jit(solution)/shard_map/ppermute | solution.py:39
  107.3 3.6 %shard_map.151 = (bf16[16,256,256]{2,1,0:T(8,128)(2,1)S(1)}, bf16[16,256,256]{2,1,0:T(8,128)(2,1)S(1)}, bf16[16,256,256]{2,1,0:T(8,128)(2,1)S(1)}, f32[256,128]{1,0:T(8,128)S(1)}) custom-call(s32[1]{0:T(128)S(6)} %copy.19.len_ref.refs_0_, bf16[2,4,768,256]{3,2,1,0:T(8,128)(2,1)S(1)} %shard_map.150.own_ref, ...), custom_call_target="tpu_custom_call" | custom-call | bytes 12582912 | tf_op jit(solution)/shard_map/pallas_call | solution.py:65
  114.9 3.8 %shard_map.156 = bf16[2,4,784,256]{3,2,1,0:T(8,128)(2,1)S(1)} custom-call(bf16[256,256]{1,0:T(8,128)(2,1)S(1)} %get-tuple-element.143.q_t_ref.refs_0_, bf16[256,512]{1,0:T(8,128)(2,1)S(1)} %get-tuple-element.144.kv_ref, bf16[256,256]{1,0:T(8,128)(2,1)S(1)} %get-tuple-element.145.at_t_ref.refs_2_, bf16[16,256]{1,0:T(8,128)(2,1)S(1)} %get-tuple-element.146.stat_ref, ...), custom_call_target="tpu_custom_call" | custom-call | flops 4294967296 | bytes 14680064 | tf_op jit(solution)/shard_map/pallas_call | solution.py:65
  123.4 3.8 %shard_map.157.keep_ref = bf16[2,4,784,256]{3,2,1,0:T(8,128)(2,1)S(1)} custom-call(bf16[256,256]{1,0:T(8,128)(2,1)S(1)} %get-tuple-element.143.q_t_ref.refs_0_, bf16[256,512]{1,0:T(8,128)(2,1)S(1)} %get-tuple-element.144.kv_ref, bf16[256,256]{1,0:T(8,128)(2,1)S(1)} %get-tuple-element.145.at_t_ref.refs_2_, bf16[16,256]{1,0:T(8,128)(2,1)S(1)} %get-tuple-element.146.stat_ref, ...), custom_call_target="tpu_custom_call" | custom-call | flops 4294967296 | bytes 14680064 | tf_op jit(solution)/shard_map/pallas_call | solution.py:65
  137.6 8.3 %collective-permute-done.23.far1 = bf16[1024,256]{1,0:T(8,128)(2,1)S(1)} collective-permute-done((bf16[1024,256]{1,0:T(8,128)(2,1)S(1)}, bf16[1024,256]{1,0:T(8,128)(2,1)S(1)}, u32[]{:S(2)}, u32[]{:S(2)}) %collective-permute-start.23) | collective-permute-done | bytes 524320 | tf_op jit(solution)/shard_map/ppermute | solution.py:30
  145.9 11.2 %collective-permute-done.25.bf2 = bf16[1024,256]{1,0:T(8,128)(2,1)S(1)} collective-permute-done((bf16[1024,256]{1,0:T(8,128)(2,1)S(1)}, bf16[1024,256]{1,0:T(8,128)(2,1)S(1)}, u32[]{:S(2)}, u32[]{:S(2)}) %collective-permute-start.25) | collective-permute-done | bytes 524320 | tf_op jit(solution)/shard_map/ppermute | solution.py:30
  164.1 15.6 %collective-permute-done.27.low = bf16[512,256]{1,0:T(8,128)(2,1)S(1)} collective-permute-done((bf16[512,256]{1,0:T(8,128)(2,1)S(1)}, bf16[512,256]{1,0:T(8,128)(2,1)S(1)}, u32[]{:S(2)}, u32[]{:S(2)}) %collective-permute-start.27) | collective-permute-done | bytes 262176 | tf_op jit(solution)/shard_map/ppermute | solution.py:34
  188.7 5.6 %collective-permute-done.34.refs_1_ = bf16[1024,256]{1,0:T(8,128)(2,1)S(1)} collective-permute-done((bf16[1024,256]{1,0:T(8,128)(2,1)S(1)}, bf16[1024,256]{1,0:T(8,128)(2,1)S(1)}, u32[]{:S(2)}, u32[]{:S(2)}) %collective-permute-start.34) | collective-permute-done | bytes 524320 | tf_op jit(solution)/shard_map/ppermute | solution.py:30
  194.3 5.3 %collective-permute-done.30.second_ref = bf16[2,784,256]{2,1,0:T(8,128)(2,1)S(1)} collective-permute-done((bf16[2,784,256]{2,1,0:T(8,128)(2,1)S(1)}, bf16[2,784,256]{2,1,0:T(8,128)(2,1)S(1)}, u32[]{:S(2)}, u32[]{:S(2)}) %collective-permute-start.30) | collective-permute-done | bytes 802848 | tf_op jit(solution)/shard_map/ppermute | solution.py:44
  200.0 3.9 %collective-permute-done.37.refs_4_ = bf16[1024,256]{1,0:T(8,128)(2,1)S(1)} collective-permute-done((bf16[1024,256]{1,0:T(8,128)(2,1)S(1)}, bf16[1024,256]{1,0:T(8,128)(2,1)S(1)}, u32[]{:S(2)}, u32[]{:S(2)}) %collective-permute-start.37) | collective-permute-done | bytes 524320 | tf_op jit(solution)/shard_map/ppermute | solution.py:34
  203.8 8.0 %collective-permute-done.38.refs_5_ = bf16[1024,256]{1,0:T(8,128)(2,1)S(1)} collective-permute-done((bf16[1024,256]{1,0:T(8,128)(2,1)S(1)}, bf16[1024,256]{1,0:T(8,128)(2,1)S(1)}, u32[]{:S(2)}, u32[]{:S(2)}) %collective-permute-start.38) | collective-permute-done | bytes 524320 | tf_op jit(solution)/shard_map/ppermute | solution.py:34
  (84 shorter events, 59.8 us)
Async XLA Ops:
  2.9 14.5 %collective-permute-start.1 = (bf16[256,1024]{1,0:T(8,128)(2,1)}, bf16[256,1024]{1,0:T(8,128)(2,1)S(1)}, u32[]{:S(2)}, u32[]{:S(2)}) collective-permute-start(bf16[256,1024]{1,0:T(8,128)(2,1)} %get-tuple-element.114.refs_0_), channel_id=1, source_target_pairs={{0,192},{16,208},{32,224},{48,240},{64,0},{80,16},{96,32},{112,48}... | collective-permute-start | bytes 1572872 | tf_op jit(solution)/shard_map/ppermute | solution.py:30
  9.0 25.7 %collective-permute-start.7 = (bf16[256,1024]{1,0:T(8,128)(2,1)}, bf16[256,1024]{1,0:T(8,128)(2,1)S(1)}, u32[]{:S(2)}, u32[]{:S(2)}) collective-permute-start(bf16[256,1024]{1,0:T(8,128)(2,1)} %get-tuple-element.114.refs_0_), channel_id=1, source_target_pairs={{0,48},{16,0},{32,16},{48,32},{64,112},{80,64},{96,80},{112,96},{1... | collective-permute-start | bytes 1572872 | tf_op jit(solution)/shard_map/ppermute | solution.py:34
  15.1 19.7 %collective-permute-start.6 = (bf16[256,1024]{1,0:T(8,128)(2,1)}, bf16[256,1024]{1,0:T(8,128)(2,1)S(1)}, u32[]{:S(2)}, u32[]{:S(2)}) collective-permute-start(bf16[256,1024]{1,0:T(8,128)(2,1)} %get-tuple-element.114.refs_0_), channel_id=1, source_target_pairs={{0,16},{16,32},{32,48},{48,0},{64,80},{80,96},{96,112},{112,64},{1... | collective-permute-start | bytes 1572872 | tf_op jit(solution)/shard_map/ppermute | solution.py:34
  20.4 21.2 %collective-permute-start.3 = (bf16[256,1024]{1,0:T(8,128)(2,1)}, bf16[256,1024]{1,0:T(8,128)(2,1)S(1)}, u32[]{:S(2)}, u32[]{:S(2)}) collective-permute-start(bf16[256,1024]{1,0:T(8,128)(2,1)} %get-tuple-element.114.refs_0_), channel_id=1, source_target_pairs={{0,128},{16,144},{32,160},{48,176},{64,192},{80,208},{96,224},{112... | collective-permute-start | bytes 1572872 | tf_op jit(solution)/shard_map/ppermute | solution.py:30
  20.5 14.3 %collective-permute-start.5 = (bf16[768,256]{1,0:T(8,128)(2,1)}, bf16[768,256]{1,0:T(8,128)(2,1)S(1)}, u32[]{:S(2)}, u32[]{:S(2)}) collective-permute-start(bf16[768,256]{1,0:T(8,128)(2,1)} %get-tuple-element.115.refs_0_.refs_3_), channel_id=1, source_target_pairs={{0,4},{1,5},{2,6},{3,7},{4,0},{5,1},{6,2},{7,3},{8,12},{9,13},{10,... | collective-permute-start | bytes 1179656 | tf_op jit(solution)/shard_map/ppermute | solution.py:39
  23.2 18.4 %collective-permute-start.4 = (bf16[768,256]{1,0:T(8,128)(2,1)}, bf16[768,256]{1,0:T(8,128)(2,1)S(1)}, u32[]{:S(2)}, u32[]{:S(2)}) collective-permute-start(bf16[768,256]{1,0:T(8,128)(2,1)} %get-tuple-element.115.refs_0_.refs_3_), channel_id=1, source_target_pairs={{0,2},{1,3},{2,4},{3,5},{4,6},{5,7},{6,0},{7,1},{8,10},{9,11},{10,... | collective-permute-start | bytes 1179656 | tf_op jit(solution)/shard_map/ppermute | solution.py:39
  44.7 16.1 %collective-permute-start.11 = (bf16[128,1024]{1,0:T(8,128)(2,1)S(1)}, bf16[128,1024]{1,0:T(8,128)(2,1)S(1)}, u32[]{:S(2)}, u32[]{:S(2)}) collective-permute-start(bf16[128,1024]{1,0:T(8,128)(2,1)S(1)} %get-tuple-element.120), channel_id=1, source_target_pairs={{0,48},{16,0},{32,16},{48,32},{64,112},{80,64},{96,80},{112,96},{1... | collective-permute-start | bytes 786440 | tf_op jit(solution)/shard_map/ppermute | solution.py:34
  47.9 24.0 %collective-permute-start.9 = (bf16[2,256,1024]{2,1,0:T(8,128)(2,1)S(1)}, bf16[2,256,1024]{2,1,0:T(8,128)(2,1)S(1)}, u32[]{:S(2)}, u32[]{:S(2)}) collective-permute-start(bf16[2,256,1024]{2,1,0:T(8,128)(2,1)S(1)} %shard_map.145.refs_0_), channel_id=1, source_target_pairs={{0,192},{16,208},{32,224},{48,240},{64,0},{80,16},{96,32},{112,48}... | collective-permute-start | bytes 3145736 | tf_op jit(solution)/shard_map/ppermute | solution.py:30
  49.5 24.8 %collective-permute-start.8 = (bf16[2,256,1024]{2,1,0:T(8,128)(2,1)S(1)}, bf16[2,256,1024]{2,1,0:T(8,128)(2,1)S(1)}, u32[]{:S(2)}, u32[]{:S(2)}) collective-permute-start(bf16[2,256,1024]{2,1,0:T(8,128)(2,1)S(1)} %shard_map.145.refs_0_), channel_id=1, source_target_pairs={{0,64},{16,80},{32,96},{48,112},{64,128},{80,144},{96,160},{112,17... | collective-permute-start | bytes 3145736 | tf_op jit(solution)/shard_map/ppermute | solution.py:30
  60.9 37.7 %collective-permute-start.14 = (bf16[4,768,256]{2,1,0:T(8,128)(2,1)S(1)}, bf16[4,768,256]{2,1,0:T(8,128)(2,1)S(1)}, u32[]{:S(2)}, u32[]{:S(2)}) collective-permute-start(bf16[4,768,256]{2,1,0:T(8,128)(2,1)S(1)} %shard_map.148.first), channel_id=1, source_target_pairs={{0,8},{1,9},{2,10},{3,11},{4,12},{5,13},{6,14},{7,15},{8,0},{9,1},... | collective-permute-start | bytes 4718600 | tf_op jit(solution)/shard_map/ppermute | solution.py:39
  76.0 21.1 %collective-permute-start.12 = (bf16[256,1024]{1,0:T(8,128)(2,1)S(1)}, bf16[256,1024]{1,0:T(8,128)(2,1)S(1)}, u32[]{:S(2)}, u32[]{:S(2)}) collective-permute-start(bf16[256,1024]{1,0:T(8,128)(2,1)S(1)} %get-tuple-element.123), channel_id=1, source_target_pairs={{0,192},{16,208},{32,224},{48,240},{64,0},{80,16},{96,32},{112,48}... | collective-permute-start | bytes 1572872 | tf_op jit(solution)/shard_map/ppermute | solution.py:30
  77.8 20.8 %collective-permute-start.13 = (bf16[256,1024]{1,0:T(8,128)(2,1)S(1)}, bf16[256,1024]{1,0:T(8,128)(2,1)S(1)}, u32[]{:S(2)}, u32[]{:S(2)}) collective-permute-start(bf16[256,1024]{1,0:T(8,128)(2,1)S(1)} %get-tuple-element.124), channel_id=1, source_target_pairs={{0,64},{16,80},{32,96},{48,112},{64,128},{80,144},{96,160},{112,17... | collective-permute-start | bytes 1572872 | tf_op jit(solution)/shard_map/ppermute | solution.py:30
  131.2 48.5 %collective-permute-start.29 = (bf16[4,784,256]{2,1,0:T(8,128)(2,1)S(1)}, bf16[4,784,256]{2,1,0:T(8,128)(2,1)S(1)}, u32[]{:S(2)}, u32[]{:S(2)}) collective-permute-start(bf16[4,784,256]{2,1,0:T(8,128)(2,1)S(1)} %get-tuple-element.180), channel_id=1, source_target_pairs={{0,8},{1,9},{2,10},{3,11},{4,12},{5,13},{6,14},{7,15},{8,0},{9,1},... | collective-permute-start | bytes 4816904 | tf_op jit(solution)/shard_map/ppermute | solution.py:39
  134.9 22.2 %collective-permute-start.25 = (bf16[1024,256]{1,0:T(8,128)(2,1)S(1)}, bf16[1024,256]{1,0:T(8,128)(2,1)S(1)}, u32[]{:S(2)}, u32[]{:S(2)}) collective-permute-start(bf16[1024,256]{1,0:T(8,128)(2,1)S(1)} %get-tuple-element.168), channel_id=1, source_target_pairs={{0,64},{16,80},{32,96},{48,112},{64,128},{80,144},{96,160},{112,17... | collective-permute-start | bytes 1572872 | tf_op jit(solution)/shard_map/ppermute | solution.py:30
  134.9 22.2 %collective-permute-start.26 = (bf16[1024,256]{1,0:T(8,128)(2,1)S(1)}, bf16[1024,256]{1,0:T(8,128)(2,1)S(1)}, u32[]{:S(2)}, u32[]{:S(2)}) collective-permute-start(bf16[1024,256]{1,0:T(8,128)(2,1)S(1)} %get-tuple-element.169), channel_id=1, source_target_pairs={{0,192},{16,208},{32,224},{48,240},{64,0},{80,16},{96,32},{112,48}... | collective-permute-start | bytes 1572872 | tf_op jit(solution)/shard_map/ppermute | solution.py:30
  157.8 24.1 %collective-permute-start.32 = (bf16[2,1024,256]{2,1,0:T(8,128)(2,1)S(1)}, bf16[2,1024,256]{2,1,0:T(8,128)(2,1)S(1)}, u32[]{:S(2)}, u32[]{:S(2)}) collective-permute-start(bf16[2,1024,256]{2,1,0:T(8,128)(2,1)S(1)} %get-tuple-element.192), channel_id=1, source_target_pairs={{0,64},{16,80},{32,96},{48,112},{64,128},{80,144},{96,160},{112,17... | collective-permute-start | bytes 3145736 | tf_op jit(solution)/shard_map/ppermute | solution.py:30
  157.9 24.0 %collective-permute-start.33 = (bf16[2,1024,256]{2,1,0:T(8,128)(2,1)S(1)}, bf16[2,1024,256]{2,1,0:T(8,128)(2,1)S(1)}, u32[]{:S(2)}, u32[]{:S(2)}) collective-permute-start(bf16[2,1024,256]{2,1,0:T(8,128)(2,1)S(1)} %get-tuple-element.193), channel_id=1, source_target_pairs={{0,192},{16,208},{32,224},{48,240},{64,0},{80,16},{96,32},{112,48}... | collective-permute-start | bytes 3145736 | tf_op jit(solution)/shard_map/ppermute | solution.py:30
  160.5 19.1 %collective-permute-start.27 = (bf16[512,256]{1,0:T(8,128)(2,1)S(1)}, bf16[512,256]{1,0:T(8,128)(2,1)S(1)}, u32[]{:S(2)}, u32[]{:S(2)}) collective-permute-start(bf16[512,256]{1,0:T(8,128)(2,1)S(1)} %get-tuple-element.178), channel_id=1, source_target_pairs={{0,16},{16,32},{32,48},{48,0},{64,80},{80,96},{96,112},{112,64},{1... | collective-permute-start | bytes 786440 | tf_op jit(solution)/shard_map/ppermute | solution.py:34
  161.6 18.1 %collective-permute-start.28 = (bf16[512,256]{1,0:T(8,128)(2,1)S(1)}, bf16[512,256]{1,0:T(8,128)(2,1)S(1)}, u32[]{:S(2)}, u32[]{:S(2)}) collective-permute-start(bf16[512,256]{1,0:T(8,128)(2,1)S(1)} %get-tuple-element.179), channel_id=1, source_target_pairs={{0,48},{16,0},{32,16},{48,32},{64,112},{80,64},{96,80},{112,96},{1... | collective-permute-start | bytes 786440 | tf_op jit(solution)/shard_map/ppermute | solution.py:34
  180.2 19.4 %collective-permute-start.30 = (bf16[2,784,256]{2,1,0:T(8,128)(2,1)S(1)}, bf16[2,784,256]{2,1,0:T(8,128)(2,1)S(1)}, u32[]{:S(2)}, u32[]{:S(2)}) collective-permute-start(bf16[2,784,256]{2,1,0:T(8,128)(2,1)S(1)} %get-tuple-element.183), channel_id=1, source_target_pairs={{0,4},{1,5},{2,6},{3,7},{4,0},{5,1},{6,2},{7,3},{8,12},{9,13},{10,... | collective-permute-start | bytes 2408456 | tf_op jit(solution)/shard_map/ppermute | solution.py:44
  182.7 17.3 %collective-permute-start.36 = (bf16[1024,256]{1,0:T(8,128)(2,1)S(1)}, bf16[1024,256]{1,0:T(8,128)(2,1)S(1)}, u32[]{:S(2)}, u32[]{:S(2)}) collective-permute-start(bf16[1024,256]{1,0:T(8,128)(2,1)S(1)} %get-tuple-element.210), channel_id=1, source_target_pairs={{0,192},{16,208},{32,224},{48,240},{64,0},{80,16},{96,32},{112,48}... | collective-permute-start | bytes 1572872 | tf_op jit(solution)/shard_map/ppermute | solution.py:30
  185.1 18.7 %collective-permute-start.37 = (bf16[1024,256]{1,0:T(8,128)(2,1)S(1)}, bf16[1024,256]{1,0:T(8,128)(2,1)S(1)}, u32[]{:S(2)}, u32[]{:S(2)}) collective-permute-start(bf16[1024,256]{1,0:T(8,128)(2,1)S(1)} %get-tuple-element.211), channel_id=1, source_target_pairs={{0,16},{16,32},{32,48},{48,0},{64,80},{80,96},{96,112},{112,64},{1... | collective-permute-start | bytes 1572872 | tf_op jit(solution)/shard_map/ppermute | solution.py:34
  186.2 25.7 %collective-permute-start.38 = (bf16[1024,256]{1,0:T(8,128)(2,1)S(1)}, bf16[1024,256]{1,0:T(8,128)(2,1)S(1)}, u32[]{:S(2)}, u32[]{:S(2)}) collective-permute-start(bf16[1024,256]{1,0:T(8,128)(2,1)S(1)} %get-tuple-element.212), channel_id=1, source_target_pairs={{0,48},{16,0},{32,16},{48,32},{64,112},{80,64},{96,80},{112,96},{1... | collective-permute-start | bytes 1572872 | tf_op jit(solution)/shard_map/ppermute | solution.py:34
  194.3 17.6 %collective-permute-start.35 = (bf16[1024,256]{1,0:T(8,128)(2,1)S(1)}, bf16[1024,256]{1,0:T(8,128)(2,1)S(1)}, u32[]{:S(2)}, u32[]{:S(2)}) collective-permute-start(bf16[1024,256]{1,0:T(8,128)(2,1)S(1)} %get-tuple-element.209), channel_id=1, source_target_pairs={{0,128},{16,144},{32,160},{48,176},{64,192},{80,208},{96,224},{112... | collective-permute-start | bytes 1572872 | tf_op jit(solution)/shard_map/ppermute | solution.py:30
  (17 other events, 227.0 us)
